TPU v7x, 32 devices: a whole 2x2x4 slice. The times are simulated.
32 devices in a mesh: groups: 2 (over x), serve: 16 (over z, y, core), tensor: 1.
Axes of the slice: x: 2, y: 2, z: 4, core: 2. Of those that a mesh axis runs over, the one named last changes fastest.
Arguments:
- span_states: bfloat16 [32, 256, 12288], P(('groups', 'serve'), None, 'tensor'), parts along dimension 0, may hold values from -6 to 6
- recomp_states: bfloat16 [32, 240, 12288], P(('groups', 'serve'), None, 'tensor'), parts along dimension 0, may hold values from -24 to 24
- w_query: bfloat16 [12288, 6, 128], P('tensor', None, 'serve'), may hold values from -0.054126588 to 0.054126588
- w_kv: bfloat16 [12288, 2, 128], P('tensor', None, 'serve'), may hold values from -0.054126588 to 0.054126588
- w_out: bfloat16 [6, 128, 1, 12288], P('tensor', None, None, 'serve'), may hold values from -0.21875 to 0.21875
- span_map: int32 [32, 6], P(('groups', 'serve')), parts along dimension 0, may hold values from 0 to 15, all different within a row
- span_lengths: int32 [32], P(('groups', 'serve')), parts along dimension 0, may hold values from 128 to 256, as said below
- recompute_idx: int32 [32, 240], P(('groups', 'serve')), parts along dimension 0, may hold values from 0 to 1407, as said below
- block_table: int32 [512], P(('groups', 'serve')), parts along dimension 0, may hold values from 0 to 15, as said below
Outputs:
- kv_cache: bfloat16 [512, 16, 256], P(('groups', 'serve')), parts along dimension 0
- attn_out: bfloat16 [32, 240, 12288], P(('groups', 'serve'), None, 'tensor'), parts along dimension 0
There are 2 independent parts, one for each index of `groups`. A program takes and returns all parts, laid end to end along the dimension named above; an argument that names none is the same for every part. Nothing has to cross between parts.
Inputs may be any that keep to these rules, and one draw needn't show every extreme that they name: `span_lengths`: some span has exactly 256 live tokens and some exactly 128. `recompute_idx`: entries s * 40 to (s + 1) * 40 - 1 of a row are distinct positions s * 256 + o with o < 128. `block_table`: each span's 16 entries are a permutation of 0 to 15. `span_map`: A row names 6 different spans; every span is named by some row.
All inputs are finite; a program needn't handle non-finite values.
Results may differ from a plain program's by a relative error of at most 0.014.
Values may be sent and summed in bfloat16 or wider, within the bound.
No kernel may reach another device: no remote copies, remote signals or barrier semaphores. Data moves between devices by JAX's collectives and lax.ppermute only.
A program may use at most 128 MiB of HBM per device.

v0:
```python
from functools import partial
import math

import jax
import jax.numpy as jnp
from jax import lax
from jax.sharding import PartitionSpec as P

HD = 128
SPAN = 256
PAGE = 16
CPR = 6
PPC = 16


def merge_block(state, query, key_rows, value_rows, allowed, score_scale):
    old_max, old_sum, old_acc = state
    scores = (
        jnp.einsum("rhc,kc->rhk", query, key_rows, preferred_element_type=jnp.float32) * score_scale
    )
    block_max = jnp.max(jnp.where(allowed, scores, -jnp.inf), axis=2)
    new_max = jnp.maximum(old_max, block_max)
    weights_now = jnp.where(allowed, jnp.exp(scores - new_max[:, :, None]), 0.0)
    rescale = jnp.exp(old_max - new_max)
    new_acc = old_acc * rescale[:, :, None] + jnp.einsum(
        "rhk,kc->rhc", weights_now, value_rows.astype(jnp.float32)
    )
    return (new_max, old_sum * rescale + jnp.sum(weights_now, axis=2), new_acc)


def body(
    span_states,
    recomp_states,
    w_query,
    w_kv,
    w_out,
    span_map,
    span_lengths,
    recompute_idx,
    block_table,
):
    span_rows = span_states[0]
    req_rows = recomp_states[0]
    num_recomp = req_rows.shape[0]
    all_heads = w_query.shape[1]
    query_piece = lax.all_gather(w_query, "serve", axis=2, tiled=True)
    kv_piece = lax.all_gather(w_kv, "serve", axis=2, tiled=True)
    query_part = jnp.einsum(
        "rd,dhc->rhc", req_rows, query_piece, preferred_element_type=jnp.float32
    )
    new_part = jnp.einsum("rd,dhc->rhc", req_rows, kv_piece, preferred_element_type=jnp.float32)
    span_part = jnp.einsum("rd,dhc->rhc", span_rows, kv_piece, preferred_element_type=jnp.float32)
    query_full, new_full, span_full = lax.psum((query_part, new_part, span_part), "tensor")
    core_heads = all_heads // lax.axis_size("tensor")
    my_core = lax.axis_index("tensor")
    query = lax.dynamic_slice_in_dim(query_full, my_core * core_heads, core_heads, 1).astype(
        jnp.bfloat16
    )
    new_kv = new_full.astype(jnp.bfloat16)
    span_kv = span_full.astype(jnp.bfloat16)
    logical_pages = span_kv.reshape(PPC, PAGE, 2 * HD)
    inverse = jnp.argsort(block_table)
    physical = logical_pages[inverse]
    page_lens = jnp.repeat(span_lengths, PPC, total_repeat_length=PPC)
    positions = recompute_idx[0]
    my_spans = span_map[0]
    score_scale = HD ** (-0.5)
    slot_ids = jnp.arange(CPR, dtype=jnp.int32)
    token_ids = jnp.arange(PAGE, dtype=jnp.int32)
    local_allowed = (positions[None, :] <= positions[:, None])[:, None, :]
    empty_state = (
        jnp.full((num_recomp, core_heads), -jnp.inf, jnp.float32),
        jnp.zeros((num_recomp, core_heads), jnp.float32),
        jnp.zeros((num_recomp, core_heads, HD), jnp.float32),
    )
    state = merge_block(empty_state, query, new_kv[:, 0], new_kv[:, 1], local_allowed, score_scale)

    def block_update(skipping, totals, block):
        page_data, logical, lens_block, first_page = block
        width = page_data.shape[0]
        global_page = first_page + jnp.arange(width, dtype=jnp.int32)
        span_id = global_page // PPC
        matches = my_spans[None, :] == span_id[:, None]
        in_request = jnp.any(matches, axis=1)
        slot_num = jnp.sum(jnp.where(matches, slot_ids[None, :], 0), axis=1)
        offset = logical[:, None] * PAGE + token_ids[None, :]
        key_pos = (slot_num[:, None] * SPAN + offset).reshape(width * PAGE)
        usable = (in_request[:, None] & (offset < lens_block[:, None])).reshape(width * PAGE)
        redone = jnp.any(key_pos[:, None] == positions[None, :], axis=1)
        usable = usable & jnp.logical_not(redone)
        allowed = (usable[None, :] & (key_pos[None, :] <= positions[:, None]))[:, None, :]
        key_rows = page_data.reshape(width * PAGE, 2, HD)
        result = merge_block(totals, query, key_rows[:, 0], key_rows[:, 1], allowed, score_scale)
        return (result, None)

    page_data = lax.all_gather(physical, "serve", axis=0, tiled=True)
    logical = lax.all_gather(inverse, "serve", axis=0, tiled=True)
    lens_piece = lax.all_gather(page_lens, "serve", axis=0, tiled=True)
    count = page_data.shape[0]
    block = math.gcd(count, 64)
    steps_here = count // block
    blocks = (
        page_data.reshape(steps_here, block, PAGE, 2 * HD),
        logical.reshape(steps_here, block),
        lens_piece.reshape(steps_here, block),
        jnp.arange(steps_here, dtype=jnp.int32) * block,
    )
    result, unused_out = lax.scan(partial(block_update, False), state, blocks)
    state = result
    run_max, run_sum, run_acc = state
    attended = (run_acc / run_sum[:, :, None]).astype(jnp.bfloat16)
    partial_out = jnp.einsum(
        "rhc,hctd->rtd",
        attended,
        lax.all_gather(w_out, "serve", axis=3, tiled=True),
        preferred_element_type=jnp.float32,
    )
    reduced = lax.psum_scatter(
        partial_out.astype(jnp.bfloat16), "tensor", scatter_dimension=1, tiled=True
    )
    attn_out = reduced.reshape(1, reduced.shape[0], reduced.shape[2])
    return (physical, attn_out)


def solution(mesh):
    in_specs = (
        P(("groups", "serve"), None, "tensor"),
        P(("groups", "serve"), None, "tensor"),
        P("tensor", None, "serve"),
        P("tensor", None, "serve"),
        P("tensor", None, None, "serve"),
        P(("groups", "serve"), None),
        P(("groups", "serve")),
        P(("groups", "serve"), None),
        P(("groups", "serve")),
    )
    out_specs = (P(("groups", "serve"), None, None), P(("groups", "serve"), None, "tensor"))
    return jax.shard_map(body, mesh=mesh, in_specs=in_specs, out_specs=out_specs, check_vma=False)
```

profile of v0, /device:TPU:0, one launch (start us, length us, event | category | flops | bytes accessed | tf_op | source)
XLA Modules:
  0.0 334.6 jit_solution(7180798263031954354)
XLA Ops:
  7.2 0.7 all-gather.6.cloned.1.call-update
  7.9 0.7 all-gather.8.cloned.1.call-update
  8.7 1.9 sort.17
  10.6 64.3 %all-gather.6.cloned.1.call-done = bf16[12288,2,128]{0,2,1:T(8,128)(2,1)} async-done(((bf16[12288,2,8]{0,2,1:T(8,128)(2,1)}), bf16[12288,2,128]{0,2,1:T(8,128)(2,1)}) %all-gather.6.cloned.1.call-update) | async-done | bytes 6291472 | tf_op jit(solution)/shard_map/all_gather | solution.py:47
  75.0 6.4 %fusion.48 = bf16[256,2,128]{2,0,1:T(8,128)(2,1)S(1)} fusion(bf16[12288,2,128]{0,2,1:T(8,128)(2,1)} %all-gather.6.cloned.1.call-done, bf16[1,256,12288]{2,1,0:T(8,128)(2,1)} %param.15), kind=kOutput, calls=%fused_computation.60 | convolution fusion | flops 1610678272 | bytes 12713984 | tf_op jit(solution)/shard_map/rd,dhc->rhc/dot_general | solution.py:52
  81.4 0.1 copy.25
  81.6 1.2 gather_fusion
  82.9 0.5 all-gather.10.cloned.1.call-update
  84.1 0.6 dynamic-slice.12
  85.4 0.2 dynamic-update-slice.7
  85.6 10.1 %all-reduce.2 = (s32[256]{0:T(256)S(1)}, s32[256]{0:T(256)S(1)}) all-reduce(s32[256]{0:T(256)S(1)} %dynamic-update-slice.7, s32[256]{0:T(256)S(1)} %broadcast_dynamic-update-slice_fusion), channel_id=1, replica_groups=mesh['groups'=2,'serve'=16,'tensor'=1] {'serve'}, use_global_device_ids=true, to_apply=%add | all-reduce | flops 512 | bytes 4096
  96.0 0.1 broadcast_compare_fusion
  96.1 6.5 %fusion.51 = bf16[240,2,128]{2,0,1:T(8,128)(2,1)S(1)} fusion(bf16[12288,2,128]{0,2,1:T(8,128)(2,1)} %all-gather.6.cloned.1.call-done, bf16[1,240,12288]{2,1,0:T(8,128)(2,1)} %param.16), kind=kOutput, calls=%fused_computation.61 | convolution fusion | flops 1510010880 | bytes 12312576 | tf_op jit(solution)/shard_map/rd,dhc->rhc/dot_general | solution.py:51
  102.6 71.6 %all-gather.8.cloned.1.call-done = bf16[12288,6,128]{0,2,1:T(8,128)(2,1)} async-done(((bf16[12288,6,8]{0,2,1:T(8,128)(2,1)}), bf16[12288,6,128]{0,2,1:T(8,128)(2,1)}) %all-gather.8.cloned.1.call-update) | async-done | bytes 18874384 | tf_op jit(solution)/shard_map/all_gather | solution.py:46
  174.2 12.1 %fusion.44 = bf16[240,6,128]{2,0,1:T(8,128)(2,1)S(1)} fusion(bf16[12288,6,128]{0,2,1:T(8,128)(2,1)} %all-gather.8.cloned.1.call-done, bf16[1,240,12288]{2,1,0:T(8,128)(2,1)} %param.16), kind=kOutput, calls=%fused_computation.58 | convolution fusion | flops 4530032640 | bytes 25141248 | tf_op jit(solution)/shard_map/rd,dhc->rhc/dot_general | solution.py:48
  186.3 0.4 select_reduce_fusion
  186.8 0.3 fusion.47
  187.1 0.5 convolution_add_fusion
  187.6 30.8 %all-gather.12.cloned.1.call-done = bf16[256,16,256]{2,1,0:T(8,128)(2,1)} async-done(((bf16[16,16,256]{2,1,0:T(8,128)(2,1)}), bf16[256,16,256]{2,1,0:T(8,128)(2,1)}) %all-gather.12.cloned.1.call-update) | async-done | bytes 2097168 | tf_op jit(solution)/shard_map/all_gather | solution.py:96
  218.4 35.1 %while.19 = (s32[]{:T(128)}, f32[240,6]{0,1:T(8,128)S(1)}, f32[240,6]{0,1:T(8,128)S(1)}, f32[240,6,128]{2,0,1:T(8,128)S(1)}, s32[1,6]{1,0:T(1,128)S(1)}, /*index...) while((s32[]{:T(128)}, f32[240,6]{0,1:T(8,128)S(1)}, ...), condition=%wide.region_9.10_spmd.clone, body=%wide.region_3.9_spmd.clone.sunk | while | flops 771083968 | bytes 24317628 | solution.py:108
  218.4 0.6 dynamic_slice.46
  219.0 0.6 and_select_fusion.2
  219.7 0.1 fusion.81
  220.2 0.2 compare_reduce_fusion.5
  220.4 0.2 compare_and_fusion.2
  220.7 1.1 constant_dynamic-slice_fusion.4
  221.7 0.1 reshape.354
  221.9 0.7 fusion.82
  222.6 1.2 fusion.83
  223.8 1.7 fusion.84
  225.6 1.6 fusion.85
  227.2 0.6 dynamic_slice.46
  227.8 0.6 and_select_fusion.2
  229.0 0.2 compare_reduce_fusion.5
  229.2 0.2 compare_and_fusion.2
  229.4 1.1 constant_dynamic-slice_fusion.4
  230.5 0.1 reshape.354
  230.7 0.7 fusion.82
  231.4 1.2 fusion.83
  232.6 1.7 fusion.84
  234.4 1.6 fusion.85
  236.0 0.6 dynamic_slice.46
  236.6 0.6 and_select_fusion.2
  237.3 0.1 fusion.81
  237.8 0.2 compare_reduce_fusion.5
  238.0 0.2 compare_and_fusion.2
  238.2 1.1 constant_dynamic-slice_fusion.4
  239.3 0.1 reshape.354
  239.5 0.7 fusion.82
  240.2 1.2 fusion.83
  241.4 1.7 fusion.84
  243.1 1.6 fusion.85
  244.8 0.6 dynamic_slice.46
  245.4 0.6 and_select_fusion.2
  246.6 0.2 compare_reduce_fusion.5
  246.8 0.2 compare_and_fusion.2
  247.0 1.1 constant_dynamic-slice_fusion.4
  248.1 0.1 reshape.354
  248.3 0.7 fusion.82
  249.0 1.2 fusion.83
  250.2 1.7 fusion.84
  251.9 1.6 fusion.85
  253.6 64.0 %all-gather.10.cloned.1.call-done = bf16[6,128,1,12288]{3,1,0,2:T(8,128)(2,1)} async-done(((bf16[6,128,1,768]{3,1,0,2:T(8,128)(2,1)}), bf16[6,128,1,12288]{3,1,0,2:T(8,128)(2,1)}) %all-gather.10.cloned.1.call-update) | async-done | bytes 18874384 | tf_op jit(solution)/shard_map/all_gather | solution.py:115
  317.5 10.5 %fusion.35 = bf16[1,240,12288]{2,1,0:T(8,128)(2,1)} fusion(bf16[6,128,1,12288]{3,1,0,2:T(8,128)(2,1)} %all-gather.10.cloned.1.call-done, f32[240,6,128]{2,0,1:T(8,128)S(1)} %get-tuple-element.191, f32[240,6]{0,1:T(8,128)S(1)} %get-tuple-element.192), kind=kOutput, calls=%fused_computation.47 | convolution fusion | flops 4533166080 | bytes 25515648 | tf_op jit(solution)/shard_map/rhc,hctd->rtd/dot_general | solution.py:112
  (68 shorter events, 2.5 us)
Async XLA Ops:
  7.2 67.8 %all-gather.6.cloned.1.call-start = ((), (), s32[]{:S(2)}) async-start(), calls=%async_computation | async-start | bytes 6684672 | tf_op jit(solution)/shard_map/all_gather | solution.py:47
  7.9 166.3 %all-gather.8.cloned.1.call-start = ((), (), s32[]{:S(2)}) async-start(), calls=%async_computation.1 | async-start | bytes 20054016 | tf_op jit(solution)/shard_map/all_gather | solution.py:46
  8.6 209.8 %all-gather.12.cloned.1.call-start = ((), (), s32[]{:S(2)}) async-start(), calls=%async_computation.3 | async-start | bytes 2228224 | tf_op jit(solution)/shard_map/all_gather | solution.py:96
  10.6 73.5 %copy-start.2 = (u32[32]{0:T(128)S(1)}, u32[32]{0:T(128)}, u32[]{:S(2)}) copy-start(u32[32]{0:T(128)} %constant.192) | copy-start | bytes 388
  10.6 85.3 %copy-start = (s32[1,240]{1,0:T(1,128)S(1)}, s32[1,240]{1,0:T(1,128)}, u32[]{:S(2)}) copy-start(s32[1,240]{1,0:T(1,128)} %param.22) | copy-start | bytes 2884
  82.9 234.7 %all-gather.10.cloned.1.call-start = ((), (), s32[]{:S(2)}) async-start(), calls=%async_computation.2 | async-start | bytes 20054016 | tf_op jit(solution)/shard_map/all_gather | solution.py:115
  186.3 32.1 %copy-start.1 = (s32[1,6]{1,0:T(1,128)S(1)}, s32[1,6]{1,0:T(1,128)}, u32[]{:S(2)}) copy-start(s32[1,6]{1,0:T(1,128)} %param.20) | copy-start | bytes 76
Sparse Core Ops, SparseCore 0:
  10.3 64.6 all-gather.5
  76.5 97.6 all-gather.7
  177.0 41.3 all-gather.11
  219.8 97.6 all-gather.9
where the time goes:
time: 335 us
  waiting for transfers between devices  233 us (70%)
  matrix products  47.7 us (14%)
  between operations  15.2 us (5%)
  other arithmetic  15 us (4%)
  local copies, waits for them, and re-layouts  13.4 us (4%)
  blocking collectives  10.1 us (3%)
    all_gather x1, waiting for transfers between devices, body(): query_piece = lax.all_gather(w_query, 'serve', axis=2, tiled=True)  71.6 us
    all_gather x1, waiting for transfers between devices, body(): kv_piece = lax.all_gather(w_kv, 'serve', axis=2, tiled=True)  64.3 us
    all_gather x1, waiting for transfers between devices, body(): lax.all_gather(w_out, 'serve', axis=3, tiled=True)  64 us
    all_gather x1, waiting for transfers between devices, body(): page_data = lax.all_gather(physical, 'serve', axis=0, tiled=True)  30.8 us
    dot_general x1, matrix products, body(): jnp.einsum('rd,dhc->rhc', req_rows, query_piece, preferred_element_type=j...  12.1 us
    dot_general x1, matrix products, body(): jnp.einsum('rhc,hctd->rtd', attended, lax.all_gather(w_out, 'serve', axis...  10.5 us
    unnamed x1, blocking collectives  10.1 us
    reduce_sum x5, other arithmetic, merge_block(): return (new_max, old_sum * rescale + jnp.sum(weights_now, axis=2), new_acc)  7.17 us
  transfers between devices with their start and end apart: 4, of which 4 were waited for; matrix products, arithmetic and copies ran while one was open for 20% of the time, Pallas kernels for 0%

commit v1 on v0

--- a/solution.py
+++ b/solution.py
@@ -3,7 +3,10 @@
 
 import jax
 import jax.numpy as jnp
+import numpy as np
 from jax import lax
+from jax.experimental import pallas as pl
+from jax.experimental.pallas import tpu as pltpu
 from jax.sharding import PartitionSpec as P
 
 HD = 128
@@ -28,7 +31,7 @@
     return (new_max, old_sum * rescale + jnp.sum(weights_now, axis=2), new_acc)
 
 
-def body(
+def general_body(
     span_states,
     recomp_states,
     w_query,
@@ -122,6 +125,439 @@
     return (physical, attn_out)
 
 
+CHIPS = 8
+CORES = 2
+RING = ((0, 0), (1, 0), (2, 0), (3, 0), (3, 1), (2, 1), (1, 1), (0, 1))
+CHIP_AT = tuple((z * 2 + y) * CORES for z, y in RING)
+NT = (((1,), (1,)), ((), ()))
+
+
+def ring_fits(mesh):
+    return tuple(mesh.shape[name] for name in ("groups", "serve", "tensor")) == (2, CHIPS * CORES, 1)
+
+
+def ring_pairs(step):
+    return [
+        (CHIP_AT[i] + c, CHIP_AT[(i + step) % CHIPS] + c) for i in range(CHIPS) for c in range(CORES)
+    ]
+
+
+AHEAD, BACK = ring_pairs(1), ring_pairs(-1)
+SIBLING = [(i, i ^ 1) for i in range(CHIPS * CORES)]
+ACROSS = [(0, 1), (1, 0)]
+
+
+def slot_table():
+    table = np.zeros((CHIPS * CORES, CHIPS * CORES), np.int32)
+    for i in range(CHIPS):
+        for c in range(CORES):
+            for slot, step in enumerate((0, -1, 1, -2, 2, -3, 3, 4)):
+                chip = CHIP_AT[(i + step) % CHIPS]
+                table[CHIP_AT[i] + c, slot] = chip + c
+                table[CHIP_AT[i] + c, CHIPS + slot] = chip + 1 - c
+    return table
+
+
+def move(block, pairs):
+    return lax.ppermute(block, "serve", pairs)
+
+
+def across(block):
+    return lax.ppermute(block, "groups", ACROSS)
+
+
+def column_order(order_ref, slots, planes):
+    rows, width = planes * 8, planes * HD
+    row = lax.broadcasted_iota(jnp.int32, (rows, width), 0)
+    col = lax.broadcasted_iota(jnp.int32, (rows, width), 1)
+    place = (row // 8) * HD + row % 8
+    parts = [(col == place + order_ref[p] * 8).astype(jnp.float32) for p in range(slots)]
+    return jnp.concatenate(parts, axis=0).astype(jnp.bfloat16)
+
+
+def kv_kernel(order_ref, table_ref, len_ref, span_ref, req_ref, *refs):
+    slots = CHIPS * CORES
+    w_refs = refs[:slots]
+    pay_ref, new_ref, cache_ref, span_acc, req_acc = refs[slots:]
+    step = pl.program_id(0)
+    w = jnp.concatenate([ref[...] for ref in w_refs], axis=0)
+    span_now = lax.dot_general(span_ref[0], w, NT, preferred_element_type=jnp.float32)
+    req_now = lax.dot_general(req_ref[0], w, NT, preferred_element_type=jnp.float32)
+
+    @pl.when(step == 0)
+    def _():
+        span_acc[...] = span_now
+        req_acc[...] = req_now
+
+    @pl.when(step > 0)
+    def _():
+        span_acc[...] += span_now
+        req_acc[...] += req_now
+
+    @pl.when(step == pl.num_programs(0) - 1)
+    def _():
+        order = column_order(order_ref, slots, 2)
+        span_kv = jnp.dot(
+            span_acc[...].astype(jnp.bfloat16), order, preferred_element_type=jnp.float32
+        ).astype(jnp.bfloat16)
+        new_ref[...] = jnp.dot(
+            req_acc[...].astype(jnp.bfloat16), order, preferred_element_type=jnp.float32
+        ).astype(jnp.bfloat16)
+        tokens = span_kv.shape[0]
+        pay_ref[0:tokens] = span_kv
+        length = jnp.full((PAGE, 2 * HD), len_ref[0], jnp.int32)
+        pay_ref[tokens:] = length.astype(jnp.float32).astype(jnp.bfloat16)
+        for p in range(tokens // PAGE):
+            cache_ref[table_ref[p]] = span_kv[p * PAGE : (p + 1) * PAGE]
+
+
+def project_kv(order, block_table, span_lengths, span_states, recomp_states, w_blocks, last_block):
+    tokens, width = span_states.shape[1:]
+    rows = recomp_states.shape[1]
+    chunk = width // 4
+    per_half = width // 2 // chunk
+    rows_at = w_blocks[0].shape[0] // 16 - 2
+
+    def piece(first):
+        return pl.BlockSpec((16, chunk), lambda k, *_: (first + k // per_half, k % per_half))
+
+    half_slots = [piece(rows_at)] * (CHIPS - 1) + [piece(0)]
+    blocks = w_blocks[: CHIPS - 1] + last_block[:1] + w_blocks[CHIPS - 1 :] + last_block[1:]
+    return pl.pallas_call(
+        kv_kernel,
+        grid_spec=pltpu.PrefetchScalarGridSpec(
+            num_scalar_prefetch=3,
+            grid=(width // chunk,),
+            in_specs=[
+                pl.BlockSpec((1, tokens, chunk), lambda k, *_: (0, 0, k)),
+                pl.BlockSpec((1, rows, chunk), lambda k, *_: (0, 0, k)),
+                *half_slots,
+                *half_slots,
+            ],
+            out_specs=[
+                pl.BlockSpec((tokens + PAGE, 2 * HD), lambda k, *_: (0, 0)),
+                pl.BlockSpec((rows, 2 * HD), lambda k, *_: (0, 0)),
+                pl.BlockSpec((tokens // PAGE, PAGE, 2 * HD), lambda k, *_: (0, 0, 0)),
+            ],
+            scratch_shapes=[
+                pltpu.VMEM((tokens, 2 * HD), jnp.float32),
+                pltpu.VMEM((rows, 2 * HD), jnp.float32),
+            ],
+        ),
+        out_shape=[
+            jax.ShapeDtypeStruct((tokens + PAGE, 2 * HD), jnp.bfloat16),
+            jax.ShapeDtypeStruct((rows, 2 * HD), jnp.bfloat16),
+            jax.ShapeDtypeStruct((tokens // PAGE, PAGE, 2 * HD), jnp.bfloat16),
+        ],
+        cost_estimate=pl.CostEstimate(
+            flops=2 * (tokens + rows) * width * 2 * HD,
+            bytes_accessed=2 * (tokens + rows + 2 * HD) * width,
+            transcendentals=0,
+        ),
+        compiler_params=pltpu.CompilerParams(vmem_limit_bytes=40 * 2**20),
+        name="project_kv",
+    )(order, block_table, span_lengths, span_states, recomp_states, *blocks)
+
+
+def query_kernel(half_ref, mine_ref, other_ref, *refs):
+    slots = CHIPS * CORES
+    w_refs = refs[:slots]
+    mine_out, other_out, mine_acc, other_acc = refs[slots:]
+    step = pl.program_id(0)
+    w = jnp.concatenate([ref[...] for ref in w_refs], axis=0)
+    mine_now = lax.dot_general(mine_ref[0], w, NT, preferred_element_type=jnp.float32)
+    other_now = lax.dot_general(other_ref[...], w, NT, preferred_element_type=jnp.float32)
+
+    @pl.when(step == 0)
+    def _():
+        mine_acc[...] = mine_now
+        other_acc[...] = other_now
+
+    @pl.when(step > 0)
+    def _():
+        mine_acc[...] += mine_now
+        other_acc[...] += other_now
+
+    @pl.when(step == pl.num_programs(0) - 1)
+    def _():
+        mine_out[...] = mine_acc[...]
+        other_out[...] = other_acc[...].astype(other_out.dtype)
+
+
+def project_query(half, recomp_states, other_rows, w_blocks, last_block, columns):
+    rows, depth = other_rows.shape
+    chunk = depth // 6
+    steps = depth // chunk
+    part = columns // (CHIPS * CORES)
+    blocks = w_blocks[: CHIPS - 1] + last_block[:1] + w_blocks[CHIPS - 1 :] + last_block[1:]
+    return pl.pallas_call(
+        query_kernel,
+        grid_spec=pltpu.PrefetchScalarGridSpec(
+            num_scalar_prefetch=1,
+            grid=(steps,),
+            in_specs=[
+                pl.BlockSpec((1, rows, chunk), lambda k, half_ref: (0, 0, half_ref[0] * steps + k)),
+                pl.BlockSpec((rows, chunk), lambda k, *_: (0, k)),
+                *([pl.BlockSpec((part, chunk), lambda k, *_: (0, k))] * (CHIPS * CORES)),
+            ],
+            out_specs=[
+                pl.BlockSpec((rows, columns), lambda k, *_: (0, 0)),
+                pl.BlockSpec((rows, columns), lambda k, *_: (0, 0)),
+            ],
+            scratch_shapes=[
+                pltpu.VMEM((rows, columns), jnp.float32),
+                pltpu.VMEM((rows, columns), jnp.float32),
+            ],
+        ),
+        out_shape=[
+            jax.ShapeDtypeStruct((rows, columns), jnp.float32),
+            jax.ShapeDtypeStruct((rows, columns), jnp.bfloat16),
+        ],
+        cost_estimate=pl.CostEstimate(
+            flops=4 * rows * depth * columns,
+            bytes_accessed=2 * (2 * rows + columns) * depth,
+            transcendentals=0,
+        ),
+        compiler_params=pltpu.CompilerParams(vmem_limit_bytes=40 * 2**20),
+        name="project_query",
+    )(half, recomp_states, other_rows, *blocks)
+
+
+def attend_kernel(map_ref, order_ref, mine_ref, other_ref, new_ref, col_ref, row_ref, *refs):
+    span_refs = refs[:CPR]
+    out_ref, keys, values, bias = refs[CPR:]
+    rows = new_ref.shape[0]
+    cached = CPR * SPAN
+    padded = keys.shape[0]
+    for s in range(CPR):
+        keys[s * SPAN : (s + 1) * SPAN] = span_refs[s][0, 0:SPAN, 0:HD]
+        values[s * SPAN : (s + 1) * SPAN] = span_refs[s][0, 0:SPAN, HD : 2 * HD]
+    keys[cached : cached + rows] = new_ref[:, 0:HD]
+    values[cached : cached + rows] = new_ref[:, HD : 2 * HD]
+    keys[cached + rows :] = jnp.zeros((padded - cached - rows, HD), jnp.bfloat16)
+    values[cached + rows :] = jnp.zeros((padded - cached - rows, HD), jnp.bfloat16)
+    mine_at = jnp.broadcast_to(col_ref[...], (rows, SPAN))
+    lane = lax.broadcasted_iota(jnp.int32, (rows, SPAN), 1)
+    blocked = jnp.float32(-jnp.inf)
+    for s in range(CPR):
+        key_pos = lane + s * SPAN
+        redone = jnp.max(jnp.where(mine_at == key_pos, 1.0, 0.0), axis=0, keepdims=True)
+        length = span_refs[s][0, SPAN : SPAN + PAGE, :].astype(jnp.float32)[0:1]
+        offset = lax.broadcasted_iota(jnp.int32, (1, SPAN), 1).astype(jnp.float32)
+        usable = jnp.where(offset < length, 1.0 - redone, 0.0)
+        allowed = (jnp.broadcast_to(usable, (rows, SPAN)) > 0.5) & (key_pos <= mine_at)
+        bias[:, s * SPAN : (s + 1) * SPAN] = jnp.where(allowed, 0.0, blocked)
+    key_pos = jnp.broadcast_to(row_ref[...], (rows, padded - cached))
+    bias[:, cached:] = jnp.where(key_pos <= mine_at, 0.0, blocked)
+
+    query = (mine_ref[...] + other_ref[...].astype(jnp.float32)).astype(jnp.bfloat16)
+    heads = query.shape[1] // HD
+    order = column_order(order_ref, CHIPS * CORES, heads)
+    query = jnp.dot(query, order, preferred_element_type=jnp.float32).astype(jnp.bfloat16)
+    for h in range(heads):
+        scores = lax.dot_general(
+            query[:, h * HD : (h + 1) * HD], keys[...], NT, preferred_element_type=jnp.float32
+        )
+        scores = scores * (HD ** (-0.5)) + bias[...]
+        top = jnp.max(scores, axis=1, keepdims=True)
+        weights = jnp.exp(scores - top)
+        total = jnp.sum(weights, axis=1, keepdims=True)
+        mixed = jnp.dot(weights.astype(jnp.bfloat16), values[...], preferred_element_type=jnp.float32)
+        out_ref[:, h * HD : (h + 1) * HD] = (mixed / total).astype(jnp.bfloat16)
+
+
+def attend(span_map, order, mine, other, new_kv, positions, payload):
+    rows, columns = mine.shape
+    cached = CPR * SPAN
+    padded = cached + SPAN
+    row_pos = jnp.pad(positions, (0, SPAN - rows), constant_values=2 * cached)[None, :]
+    whole = lambda *shape: pl.BlockSpec(shape, lambda i, *_: (0,) * len(shape))
+    slot = lambda s: pl.BlockSpec((1,) + payload.shape[1:], lambda i, map_ref, *_: (map_ref[s], 0, 0))
+    return pl.pallas_call(
+        attend_kernel,
+        grid_spec=pltpu.PrefetchScalarGridSpec(
+            num_scalar_prefetch=2,
+            grid=(1,),
+            in_specs=[
+                whole(rows, columns),
+                whole(rows, columns),
+                whole(rows, 2 * HD),
+                whole(rows, 1),
+                whole(1, SPAN),
+                *[slot(s) for s in range(CPR)],
+            ],
+            out_specs=whole(rows, columns),
+            scratch_shapes=[
+                pltpu.VMEM((padded, HD), jnp.bfloat16),
+                pltpu.VMEM((padded, HD), jnp.bfloat16),
+                pltpu.VMEM((rows, padded), jnp.float32),
+            ],
+        ),
+        out_shape=jax.ShapeDtypeStruct((rows, columns), jnp.bfloat16),
+        cost_estimate=pl.CostEstimate(
+            flops=4 * rows * columns * padded,
+            bytes_accessed=2 * padded * 2 * HD + 8 * rows * columns,
+            transcendentals=rows * (columns // HD) * padded,
+        ),
+        compiler_params=pltpu.CompilerParams(vmem_limit_bytes=40 * 2**20),
+        name="attend",
+    )(span_map, order, mine, other, new_kv, positions[:, None], row_pos, *([payload] * CPR))
+
+
+def output_kernel(plan, order_ref, half_ref, att_ref, *refs):
+    count = 1 + max(copy[0] for copies in plan for copy in copies)
+    sources = refs[:count]
+    out_ref, w_buf, o_buf, in_sem, out_sem = refs[count:]
+    slots = len(plan)
+    third = w_buf.shape[3]
+    loads = []
+    for p, copies in enumerate(plan):
+        group = []
+        for n, (src, index, part, first, size) in enumerate(copies):
+            view = sources[src] if index is None else sources[src].at[index]
+            copy = pltpu.make_async_copy(
+                view, w_buf.at[p, part, pl.ds(first, size)], in_sem.at[p, n]
+            )
+            copy.start()
+            group.append(copy)
+        loads.append(group)
+    stores = []
+    half = half_ref[0]
+    for p in range(slots):
+        for copy in loads[p]:
+            copy.wait()
+        own = p % CHIPS == 0
+        for part in range(3):
+            o_buf[p, part] = jnp.dot(
+                att_ref[...], w_buf[p, part], preferred_element_type=jnp.float32
+            ).astype(jnp.bfloat16)
+            lot = (half, 2, 1 - half)[part] if not own else part
+            start = pl.multiple_of(order_ref[p] * (3 * third) + lot * third, third)
+            copy = pltpu.make_async_copy(
+                o_buf.at[p, part], out_ref.at[0, :, pl.ds(start, third)], out_sem.at[p, part]
+            )
+            copy.start()
+            stores.append(copy)
+    for copy in stores:
+        copy.wait()
+
+
+def project_output(order, half, attended, plan, sources, depth, third):
+    rows = attended.shape[0]
+    slots = len(plan)
+    most = max(len(copies) for copies in plan)
+    width = slots * 3 * third
+    return pl.pallas_call(
+        partial(output_kernel, plan),
+        grid_spec=pltpu.PrefetchScalarGridSpec(
+            num_scalar_prefetch=2,
+            grid=(1,),
+            in_specs=[pl.BlockSpec((rows, depth), lambda i, *_: (0, 0))]
+            + [pl.BlockSpec(memory_space=pl.ANY)] * len(sources),
+            out_specs=pl.BlockSpec(memory_space=pl.ANY),
+            scratch_shapes=[
+                pltpu.VMEM((slots, 3, depth, third), jnp.bfloat16),
+                pltpu.VMEM((slots, 3, rows, third), jnp.bfloat16),
+                pltpu.SemaphoreType.DMA((slots, most)),
+                pltpu.SemaphoreType.DMA((slots, 3)),
+            ],
+        ),
+        out_shape=jax.ShapeDtypeStruct((1, rows, width), jnp.bfloat16),
+        cost_estimate=pl.CostEstimate(
+            flops=2 * rows * depth * width,
+            bytes_accessed=2 * width * (rows + depth),
+            transcendentals=0,
+        ),
+        compiler_params=pltpu.CompilerParams(vmem_limit_bytes=44 * 2**20),
+        name="project_output",
+    )(order, half, attended, *sources)
+
+
+def gather_ring(block, split):
+    ahead = back = block
+    held = [block]
+    for _ in range(CHIPS // 2 - 1):
+        ahead, back = move(ahead, AHEAD), move(back, BACK)
+        held += [ahead, back]
+    first, second = split(ahead, back)
+    return held, (move(first, AHEAD), move(second, BACK))
+
+
+def ring_body(
+    span_states,
+    recomp_states,
+    w_query,
+    w_kv,
+    w_out,
+    span_map,
+    span_lengths,
+    recompute_idx,
+    block_table,
+):
+    group = lax.axis_index("groups")
+    width, heads, part = w_query.shape
+    half = width // 2
+    depth = heads * HD
+    columns = w_out.shape[3]
+    third = columns // 3
+    slots = CHIPS * CORES
+    order = jnp.asarray(slot_table())[lax.axis_index("serve")]
+    group_arr = group.astype(jnp.int32)[None]
+
+    theirs = lax.dynamic_slice_in_dim(recomp_states[0], (1 - group) * half, half, 1)
+    other_rows = across(theirs)
+    query_rows = w_query.transpose(1, 2, 0).reshape(heads * part, width)
+    query_rows = lax.dynamic_slice_in_dim(query_rows, group * half, half, 1)
+    kv_rows = w_kv.transpose(1, 2, 0).reshape(2 * part, width)
+    block = jnp.concatenate([query_rows, kv_rows[:, :half], kv_rows[:, half:]], axis=0)
+    cut = heads * part
+    held, (far_query, far_kv) = gather_ring(block, lambda a, b: (a[:cut], b[cut:]))
+    both = held + [move(b, SIBLING) for b in held]
+    far_query = [far_query, move(far_query, SIBLING)]
+    far_kv = [far_kv, move(far_kv, SIBLING)]
+
+    payload, new_kv, cache = project_kv(
+        order, block_table, span_lengths, span_states, recomp_states, both, far_kv
+    )
+    payloads = lax.all_gather(payload, "serve", axis=0)
+    mine, theirs_part = project_query(group_arr, recomp_states, other_rows, both, far_query, depth)
+    other = across(theirs_part)
+
+    own_out = w_out.reshape(depth, columns)
+    shared = lax.dynamic_slice_in_dim(own_out, group * third, third, 1)
+    out_block = jnp.stack([shared, own_out[:, 2 * third :]])
+    cut = depth // 2
+    out_held, out_far = gather_ring(out_block, lambda a, b: (a[:, :cut], b[:, cut:]))
+    ring_blocks = out_held[1:] + list(out_far)
+    side_blocks = [across(b[0]) for b in ring_blocks]
+    sources = [own_out, *ring_blocks, *side_blocks]
+    sources += [move(b, SIBLING) for b in sources]
+    step = len(sources) // CORES
+    plan = []
+    for c in range(CORES):
+        at = c * step
+        columns_of = lambda t: (slice(None), pl.ds(t * third, third))
+        plan.append([(at, columns_of(t), t, 0, depth) for t in range(3)])
+        for n in range(CHIPS - 2):
+            ring_at, side_at = at + 1 + n, at + 1 + CHIPS + n
+            plan.append(
+                [(ring_at, 0, 0, 0, depth), (ring_at, 1, 1, 0, depth), (side_at, None, 2, 0, depth)]
+            )
+        far = []
+        for n in range(2):
+            ring_at, side_at = at + CHIPS - 1 + n, at + 2 * CHIPS - 1 + n
+            far += [
+                (ring_at, 0, 0, n * cut, cut),
+                (ring_at, 1, 1, n * cut, cut),
+                (side_at, None, 2, n * cut, cut),
+            ]
+        plan.append(far)
+
+    attended = attend(span_map[0], order, mine, other, new_kv, recompute_idx[0], payloads)
+    attn_out = project_output(order, group_arr, attended, plan, sources, depth, third)
+    return (cache, attn_out)
+
+
 def solution(mesh):
     in_specs = (
         P(("groups", "serve"), None, "tensor"),
@@ -135,4 +571,5 @@
         P(("groups", "serve")),
     )
     out_specs = (P(("groups", "serve"), None, None), P(("groups", "serve"), None, "tensor"))
+    body = ring_body if ring_fits(mesh) else general_body
     return jax.shard_map(body, mesh=mesh, in_specs=in_specs, out_specs=out_specs, check_vma=False)

time: 335 us -> 309 us (0.922)
  matrix products: 47.7 us -> 0 us
  waiting for transfers between devices: 233 us -> 188 us
  Pallas kernels: 0 us -> 40.1 us
  starting transfers between devices: 0.16 us -> 34.9 us
  local copies, waits for them, and re-layouts: 13.4 us -> 29.4 us
  other arithmetic: 15 us -> 0.15 us
  blocking collectives: 10.1 us -> 0 us
    all_gather x4 -> x1, waiting for transfers between devices: 231 us -> 0.02 us  [ring_body(): payloads = lax.all_gather(payload, 'serve', axis=0)]
    ppermute x0 -> x52, waiting for transfers between devices: none -> 188 us  [the longest x42 99.8 us: move(): return lax.ppermute(block, 'serve', pairs)]
    dot_general x14 -> x0, matrix products: 47.7 us -> none  [the longest x1 12.1 us: body(): jnp.einsum('rd,dhc->rhc', req_rows, query_piece, preferred_element_type=j...]
    pallas_call x0 -> x4, Pallas kernels: none -> 40.1 us  [the longest x1 16.2 us: project_output(): pl.pallas_call(partial(output_kernel, plan), grid_spec=pltpu.PrefetchScal...]
    ppermute x0 -> x52, starting transfers between devices: none -> 34.9 us  [the longest x42 23.7 us: move(): return lax.ppermute(block, 'serve', pairs)]
    unnamed x11 -> x102, local copies, waits for them, and re-layouts: 0.89 us -> 17.1 us
    unnamed x1 -> x0, blocking collectives: 10.1 us -> none
    reduce_sum x9 -> x0, other arithmetic: 7.51 us -> none  [the longest x5 7.17 us: merge_block(): return (new_max, old_sum * rescale + jnp.sum(weights_now, axis=2), new_acc)]
  transfers between devices with their start and end apart: 4 -> 53, of which waited for: 4 -> 14; matrix products, arithmetic and copies ran while one was open for 20% -> 4% of each run, Pallas kernels for 0% -> 8%
where the time goes in v1:
time: 309 us; the launch traced here: 308 us
  waiting for transfers between devices  188 us (61%)
  Pallas kernels  40.1 us (13%)
  starting transfers between devices  34.9 us (11%)
  local copies, waits for them, and re-layouts  29.4 us (10%)
  between operations  15.4 us (5%)
    ppermute x42, waiting for transfers between devices, move(): return lax.ppermute(block, 'serve', pairs)  99.8 us
    ppermute x10, waiting for transfers between devices, across(): return lax.ppermute(block, 'groups', ACROSS)  88.5 us
    ppermute x42, starting transfers between devices, move(): return lax.ppermute(block, 'serve', pairs)  23.7 us
    unnamed x102, local copies, waits for them, and re-layouts  17.1 us
    pallas_call x1, Pallas kernels, project_output(): pl.pallas_call(partial(output_kernel, plan), grid_spec=pltpu.PrefetchScal...  16.2 us
    ppermute x10, starting transfers between devices, across(): return lax.ppermute(block, 'groups', ACROSS)  11.2 us
    pallas_call x1, Pallas kernels, project_query(): pl.pallas_call(query_kernel, grid_spec=pltpu.PrefetchScalarGridSpec(num_s...  9.13 us
    pallas_call x1, Pallas kernels, project_kv(): pl.pallas_call(kv_kernel, grid_spec=pltpu.PrefetchScalarGridSpec(num_scal...  9.07 us
  transfers between devices with their start and end apart: 53, of which 14 were waited for; matrix products, arithmetic and copies ran while one was open for 4% of the time, Pallas kernels for 8%

profile of v1, /device:TPU:0, one launch (start us, length us, event | category | flops | bytes accessed | tf_op | source)
XLA Modules:
  0.0 308.2 jit_solution(9162828441830468879)
XLA Ops:
  7.2 1.1 fusion.1
  8.8 3.1 collective-permute-start
  11.8 1.2 dynamic-slice_bitcast_fusion.1
  13.1 2.1 collective-permute-start.19
  15.2 19.3 %collective-permute-done.refs_1_ = bf16[80,6144]{1,0:T(8,128)(2,1)} collective-permute-done((bf16[80,6144]{1,0:T(8,128)(2,1)S(1)}, bf16[80,6144]{1,0:T(8,128)(2,1)}, u32[]{:S(2)}, u32[]{:S(2)}) %collective-permute-start) | collective-permute-done | bytes 983072 | tf_op jit(solution)/shard_map/ppermute | solution.py:162
  34.5 2.1 collective-permute-start.2
  36.6 2.0 collective-permute-start.20
  38.6 12.8 %collective-permute-done.19.refs_1_ = bf16[2,768,256]{2,1,0:T(8,128)(2,1)} collective-permute-done((bf16[2,768,256]{2,1,0:T(8,128)(2,1)S(1)}, bf16[2,768,256]{2,1,0:T(8,128)(2,1)}, u32[]{:S(2)}, u32[]{:S(2)}) %collective-permute-start.19) | collective-permute-done | bytes 786464 | tf_op jit(solution)/shard_map/ppermute | solution.py:162
  51.3 20.2 %collective-permute-done.2.refs_3_ = bf16[80,6144]{1,0:T(8,128)(2,1)} collective-permute-done((bf16[80,6144]{1,0:T(8,128)(2,1)}, bf16[80,6144]{1,0:T(8,128)(2,1)}, u32[]{:S(2)}, u32[]{:S(2)}) %collective-permute-start.2) | collective-permute-done | bytes 983072 | tf_op jit(solution)/shard_map/ppermute | solution.py:162
  71.6 1.8 collective-permute-start.4
  73.6 1.0 collective-permute-done.20.refs_2_
  74.7 1.0 copy-done.6
  76.2 1.0 copy-done.9
  77.2 17.5 %collective-permute-done.4.refs_5_ = bf16[80,6144]{1,0:T(8,128)(2,1)S(1)} collective-permute-done((bf16[80,6144]{1,0:T(8,128)(2,1)}, bf16[80,6144]{1,0:T(8,128)(2,1)S(1)}, u32[]{:S(2)}, u32[]{:S(2)}) %collective-permute-start.4) | collective-permute-done | bytes 983072 | tf_op jit(solution)/shard_map/ppermute | solution.py:162
  94.7 1.2 collective-permute-done.5.refs_6_
  96.0 1.0 copy-done.12
  96.9 0.7 collective-permute-start.6
  98.3 0.8 fusion.order_ref
  99.1 9.5 %collective-permute-done.6.refs_7_ = bf16[32,6144]{1,0:T(8,128)(2,1)} collective-permute-done((bf16[32,6144]{1,0:T(8,128)(2,1)S(1)}, bf16[32,6144]{1,0:T(8,128)(2,1)}, u32[]{:S(2)}, u32[]{:S(2)}) %collective-permute-start.6) | collective-permute-done | bytes 393248 | tf_op jit(solution)/shard_map/ppermute | solution.py:162
  108.6 1.8 slice_bitcast_fusion.5
  110.8 1.5 collective-permute-start.27
  112.3 1.8 slice_bitcast_fusion.4
  114.1 0.5 collective-permute-start.28
  114.6 1.6 collective-permute-start.21
  116.7 1.2 copy-done.7
  117.9 1.2 copy-done.10
  119.1 1.2 copy-done.13
  120.3 9.1 %project_kv.1 = (bf16[272,256]{1,0:T(8,128)(2,1)}, bf16[240,256]{1,0:T(8,128)(2,1)S(1)}, bf16[16,16,256]{2,1,0:T(8,128)(2,1)}) custom-call(s32[16]{0:T(128)S(1)} %fusion.order_ref, s32[16]{0:T(128)S(1)} %copy-done.40, s32[1]{0:T(128)S(6)} %copy.13.len_ref, bf16[1,256,12288]{2,1,0:T(8,128)(2,1)} %span_ref.1, bf16[1,240,12288]{2,1,0:T(8,128)(2,1)} %mine_ref.1, ...), custom_call_target="tpu_custom_call" | custom-call | flops 3120562176 | bytes 18481152 | tf_op jit(solution)/shard_map/project_kv/pallas_call | solution.py:226
  129.4 0.6 copy-done.38
  130.1 2.3 dynamic-slice_bitcast_fusion
  132.5 1.5 collective-permute-start.15
  134.5 1.0 slice_bitcast_fusion.3
  135.7 1.3 collective-permute-start.29
  137.0 1.0 slice_bitcast_fusion.2
  138.1 0.8 collective-permute-start.30
  138.9 0.7 copy-done.22
  139.6 1.6 collective-permute-start.23
  141.2 0.8 copy-done.24
  142.4 65.2 %collective-permute-done.29.refs_11_ = bf16[768,256]{1,0:T(8,128)(2,1)S(1)} collective-permute-done((bf16[768,256]{1,0:T(8,128)(2,1)S(1)}, bf16[768,256]{1,0:T(8,128)(2,1)S(1)}, u32[]{:S(2)}, u32[]{:S(2)}) %collective-permute-start.29) | collective-permute-done | bytes 393248 | tf_op jit(solution)/shard_map/ppermute | solution.py:166
  207.7 7.8 %collective-permute-done.30.refs_12_ = bf16[768,256]{1,0:T(8,128)(2,1)S(1)} collective-permute-done((bf16[768,256]{1,0:T(8,128)(2,1)S(1)}, bf16[768,256]{1,0:T(8,128)(2,1)S(1)}, u32[]{:S(2)}, u32[]{:S(2)}) %collective-permute-start.30) | collective-permute-done | bytes 393248 | tf_op jit(solution)/shard_map/ppermute | solution.py:166
  215.6 1.6 collective-permute-start.16
  218.0 1.6 collective-permute-start.25
  219.6 0.7 collective-permute-start.26
  220.3 1.5 collective-permute-start.31
  221.8 10.0 %collective-permute-done.16.refs_7_ = bf16[48,6144]{1,0:T(8,128)(2,1)S(1)} collective-permute-done((bf16[48,6144]{1,0:T(8,128)(2,1)S(1)}, bf16[48,6144]{1,0:T(8,128)(2,1)S(1)}, u32[]{:S(2)}, u32[]{:S(2)}) %collective-permute-start.16) | collective-permute-done | bytes 589856 | tf_op jit(solution)/shard_map/ppermute | solution.py:162
  231.8 8.0 %collective-permute-done.25.refs_7_ = bf16[2,384,256]{2,1,0:T(8,128)(2,1)S(1)} collective-permute-done((bf16[2,384,256]{2,1,0:T(8,128)(2,1)S(1)}, bf16[2,384,256]{2,1,0:T(8,128)(2,1)S(1)}, u32[]{:S(2)}, u32[]{:S(2)}) %collective-permute-start.25) | collective-permute-done | bytes 393248 | tf_op jit(solution)/shard_map/ppermute | solution.py:162
  239.8 1.5 collective-permute-start.32
  241.9 0.9 slice_bitcast_fusion.7
  242.9 7.8 %collective-permute-done.32.refs_14_ = bf16[768,256]{1,0:T(8,128)(2,1)} collective-permute-done((bf16[768,256]{1,0:T(8,128)(2,1)S(1)}, bf16[768,256]{1,0:T(8,128)(2,1)}, u32[]{:S(2)}, u32[]{:S(2)}) %collective-permute-start.32) | collective-permute-done | bytes 393248 | tf_op jit(solution)/shard_map/ppermute | solution.py:166
  250.7 1.5 collective-permute-start.33
  252.1 0.6 collective-permute-start.34
  252.7 1.0 copy-done.44
  253.8 9.1 %project_query.1 = (f32[240,768]{1,0:T(8,128)S(1)}, bf16[240,768]{1,0:T(8,128)(2,1)S(1)}) custom-call(s32[1]{0:T(128)} %bitcast.6.half_ref, bf16[1,240,12288]{2,1,0:T(8,128)(2,1)} %mine_ref.1, bf16[240,6144]{1,0:T(8,128)(2,1)} %copy-done.44, bf16[80,6144]{1,0:T(8,128)(2,1)S(1)} %pad_maximum_fusion.refs_0_, bf16[80,6144]{1,0:T(8,128)(2,1)} %collective-permute-done.refs_1_, ...), custom_call_target="tpu_custom_call" | custom-call | flops 4529848320 | bytes 15335424 | tf_op jit(solution)/shard_map/project_query/pallas_call | solution.py:293
  262.9 0.9 copy-done.18
  263.8 0.6 collective-permute-start.18
  265.0 0.9 copy-done.34
  266.2 7.6 %collective-permute-done.18.other_ref = bf16[240,768]{1,0:T(8,128)(2,1)S(1)} collective-permute-done((bf16[240,768]{1,0:T(8,128)(2,1)S(1)}, bf16[240,768]{1,0:T(8,128)(2,1)S(1)}, u32[]{:S(2)}, u32[]{:S(2)}) %collective-permute-start.18) | collective-permute-done | bytes 368672 | tf_op jit(solution)/shard_map/ppermute | solution.py:166
  274.0 1.6 copy-done.2
  275.6 1.1 copy-done.19
  276.8 0.9 copy-done.39
  277.7 5.7 %attend.1.att_ref = bf16[240,768]{1,0:T(8,128)(2,1)S(1)} custom-call(s32[6]{0:T(128)S(1)} %bitcast.45, s32[16]{0:T(128)S(1)} %fusion.order_ref, f32[240,768]{1,0:T(8,128)S(1)} %copy-done.19, bf16[240,768]{1,0:T(8,128)(2,1)S(1)} %collective-permute-done.18.other_ref, bf16[240,256]{1,0:T(8,128)(2,1)S(1)} %copy-done.39, s32[240,1]{1,0:T(8,128)S(1)} %copy.12.col_ref, ...), custom_call_target="tpu_custom_call" | custom-call | flops 1321205760 | bytes 2392064 | tf_op jit(solution)/shard_map/attend/pallas_call | solution.py:376
  283.5 0.7 copy-done.36
  284.3 0.9 copy-done.37
  285.2 16.2 %project_output.1 = bf16[1,240,12288]{2,1,0:T(8,128)(2,1)} custom-call(s32[16]{0:T(128)S(1)} %fusion.order_ref, s32[1]{0:T(128)} %bitcast.6.half_ref, bf16[240,768]{1,0:T(8,128)(2,1)S(1)} %attend.1.att_ref, bf16[768,768]{1,0:T(8,128)(2,1)} %bitcast.48, bf16[2,768,256]{2,1,0:T(8,128)(2,1)} %collective-permute-done.19.refs_1_, ...), custom_call_target="tpu_custom_call" | custom-call | flops 4529848320 | bytes 24772608 | tf_op jit(solution)/shard_map/project_output/pallas_call | solution.py:450
  (170 shorter events, 6.2 us)
Async XLA Ops:
  7.2 266.8 %all-gather.3.cloned.1.call-start = ((), (), s32[]{:S(2)}) async-start(), calls=%async_computation | async-start | bytes 2367488 | tf_op jit(solution)/shard_map/all_gather | solution.py:522
  8.8 25.7 %collective-permute-start = (bf16[80,6144]{1,0:T(8,128)(2,1)S(1)}, bf16[80,6144]{1,0:T(8,128)(2,1)}, u32[]{:S(2)}, u32[]{:S(2)}) collective-permute-start(bf16[80,6144]{1,0:T(8,128)(2,1)S(1)} %pad_maximum_fusion.refs_0_), channel_id=1, source_target_pairs={{0,4},{1,5},{4,8},{5,9},{8,12},{9,13},{12,14},{13,15},{14,10},{15,... | collective-permute-start | bytes 2949128 | tf_op jit(solution)/shard_map/ppermute | solution.py:162
  11.8 24.7 %collective-permute-start.1 = (bf16[80,6144]{1,0:T(8,128)(2,1)S(1)}, bf16[80,6144]{1,0:T(8,128)(2,1)S(1)}, u32[]{:S(2)}, u32[]{:S(2)}) collective-permute-start(bf16[80,6144]{1,0:T(8,128)(2,1)S(1)} %pad_maximum_fusion.refs_0_), channel_id=1, source_target_pairs={{0,2},{1,3},{4,0},{5,1},{8,4},{9,5},{12,8},{13,9},{14,12},{15,13},... | collective-permute-start | bytes 2949128 | tf_op jit(solution)/shard_map/ppermute | solution.py:162
  13.0 103.7 %copy-start.40 = (s32[16]{0:T(128)S(1)}, s32[16]{0:T(128)}, u32[]{:S(2)}) copy-start(s32[16]{0:T(128)} %table_ref.1) | copy-start | bytes 196
  13.1 38.2 %collective-permute-start.19 = (bf16[2,768,256]{2,1,0:T(8,128)(2,1)S(1)}, bf16[2,768,256]{2,1,0:T(8,128)(2,1)}, u32[]{:S(2)}, u32[]{:S(2)}) collective-permute-start(bf16[2,768,256]{2,1,0:T(8,128)(2,1)S(1)} %pad_maximum_fusion.1), channel_id=1, source_target_pairs={{0,4},{1,5},{4,8},{5,9},{8,12},{9,13},{12,14},{13,15},{14,10},{15,... | collective-permute-start | bytes 2359304 | tf_op jit(solution)/shard_map/ppermute | solution.py:162
  34.5 37.1 %collective-permute-start.2 = (bf16[80,6144]{1,0:T(8,128)(2,1)}, bf16[80,6144]{1,0:T(8,128)(2,1)}, u32[]{:S(2)}, u32[]{:S(2)}) collective-permute-start(bf16[80,6144]{1,0:T(8,128)(2,1)} %collective-permute-done.refs_1_), channel_id=1, source_target_pairs={{0,4},{1,5},{4,8},{5,9},{8,12},{9,13},{12,14},{13,15},{14,10},{15,... | collective-permute-start | bytes 2949128 | tf_op jit(solution)/shard_map/ppermute | solution.py:162
  36.6 36.8 %copy-start.3 = (bf16[80,6144]{1,0:T(8,128)(2,1)}, bf16[80,6144]{1,0:T(8,128)(2,1)S(1)}, u32[]{:S(2)}) copy-start(bf16[80,6144]{1,0:T(8,128)(2,1)S(1)} %collective-permute-done.1.refs_2_) | copy-start | bytes 2949124
  36.6 36.8 %collective-permute-start.3 = (bf16[80,6144]{1,0:T(8,128)(2,1)S(1)}, bf16[80,6144]{1,0:T(8,128)(2,1)}, u32[]{:S(2)}, u32[]{:S(2)}) collective-permute-start(bf16[80,6144]{1,0:T(8,128)(2,1)S(1)} %collective-permute-done.1.refs_2_), channel_id=1, source_target_pairs={{0,2},{1,3},{4,0},{5,1},{8,4},{9,5},{12,8},{13,9},{14,12},{15,13},... | collective-permute-start | bytes 2949128 | tf_op jit(solution)/shard_map/ppermute | solution.py:162
  36.6 38.0 %collective-permute-start.20 = (bf16[2,768,256]{2,1,0:T(8,128)(2,1)S(1)}, bf16[2,768,256]{2,1,0:T(8,128)(2,1)S(1)}, u32[]{:S(2)}, u32[]{:S(2)}) collective-permute-start(bf16[2,768,256]{2,1,0:T(8,128)(2,1)S(1)} %pad_maximum_fusion.1), channel_id=1, source_target_pairs={{0,2},{1,3},{4,0},{5,1},{8,4},{9,5},{12,8},{13,9},{14,12},{15,13},... | collective-permute-start | bytes 2359304 | tf_op jit(solution)/shard_map/ppermute | solution.py:162
  38.6 36.1 %collective-permute-start.7 = (bf16[80,6144]{1,0:T(8,128)(2,1)S(1)}, bf16[80,6144]{1,0:T(8,128)(2,1)S(1)}, u32[]{:S(2)}, u32[]{:S(2)}) collective-permute-start(bf16[80,6144]{1,0:T(8,128)(2,1)S(1)} %pad_maximum_fusion.refs_0_), channel_id=1, source_target_pairs={{0,1},{1,0},{2,3},{3,2},{4,5},{5,4},{6,7},{7,6},{8,9},{9,8},{10,11... | collective-permute-start | bytes 2949128 | tf_op jit(solution)/shard_map/ppermute | solution.py:162
  51.3 24.9 %collective-permute-start.8 = (bf16[80,6144]{1,0:T(8,128)(2,1)}, bf16[80,6144]{1,0:T(8,128)(2,1)S(1)}, u32[]{:S(2)}, u32[]{:S(2)}) collective-permute-start(bf16[80,6144]{1,0:T(8,128)(2,1)} %collective-permute-done.refs_1_), channel_id=1, source_target_pairs={{0,1},{1,0},{2,3},{3,2},{4,5},{5,4},{6,7},{7,6},{8,9},{9,8},{10,11... | collective-permute-start | bytes 2949128 | tf_op jit(solution)/shard_map/ppermute | solution.py:162
  71.6 23.2 %collective-permute-start.4 = (bf16[80,6144]{1,0:T(8,128)(2,1)}, bf16[80,6144]{1,0:T(8,128)(2,1)S(1)}, u32[]{:S(2)}, u32[]{:S(2)}) collective-permute-start(bf16[80,6144]{1,0:T(8,128)(2,1)} %collective-permute-done.2.refs_3_), channel_id=1, source_target_pairs={{0,4},{1,5},{4,8},{5,9},{8,12},{9,13},{12,14},{13,15},{14,10},{15,... | collective-permute-start | bytes 2949128 | tf_op jit(solution)/shard_map/ppermute | solution.py:162
  73.4 22.6 %collective-permute-start.5 = (bf16[80,6144]{1,0:T(8,128)(2,1)}, bf16[80,6144]{1,0:T(8,128)(2,1)S(1)}, u32[]{:S(2)}, u32[]{:S(2)}) collective-permute-start(bf16[80,6144]{1,0:T(8,128)(2,1)} %collective-permute-done.3.refs_4_), channel_id=1, source_target_pairs={{0,2},{1,3},{4,0},{5,1},{8,4},{9,5},{12,8},{13,9},{14,12},{15,13},... | collective-permute-start | bytes 2949128 | tf_op jit(solution)/shard_map/ppermute | solution.py:162
  74.6 21.3 %collective-permute-start.9 = (bf16[80,6144]{1,0:T(8,128)(2,1)}, bf16[80,6144]{1,0:T(8,128)(2,1)S(1)}, u32[]{:S(2)}, u32[]{:S(2)}) collective-permute-start(bf16[80,6144]{1,0:T(8,128)(2,1)} %copy-done.3), channel_id=1, source_target_pairs={{0,1},{1,0},{2,3},{3,2},{4,5},{5,4},{6,7},{7,6},{8,9},{9,8},{10,11... | collective-permute-start | bytes 2949128 | tf_op jit(solution)/shard_map/ppermute | solution.py:162
  75.7 34.6 %collective-permute-start.10 = (bf16[80,6144]{1,0:T(8,128)(2,1)}, bf16[80,6144]{1,0:T(8,128)(2,1)}, u32[]{:S(2)}, u32[]{:S(2)}) collective-permute-start(bf16[80,6144]{1,0:T(8,128)(2,1)} %collective-permute-done.2.refs_3_), channel_id=1, source_target_pairs={{0,1},{1,0},{2,3},{3,2},{4,5},{5,4},{6,7},{7,6},{8,9},{9,8},{10,11... | collective-permute-start | bytes 2949128 | tf_op jit(solution)/shard_map/ppermute | solution.py:162
  77.1 33.7 %collective-permute-start.11 = (bf16[80,6144]{1,0:T(8,128)(2,1)}, bf16[80,6144]{1,0:T(8,128)(2,1)}, u32[]{:S(2)}, u32[]{:S(2)}) collective-permute-start(bf16[80,6144]{1,0:T(8,128)(2,1)} %collective-permute-done.3.refs_4_), channel_id=1, source_target_pairs={{0,1},{1,0},{2,3},{3,2},{4,5},{5,4},{6,7},{7,6},{8,9},{9,8},{10,11... | collective-permute-start | bytes 2949128 | tf_op jit(solution)/shard_map/ppermute | solution.py:162
  94.7 19.9 %collective-permute-start.12 = (bf16[80,6144]{1,0:T(8,128)(2,1)S(1)}, bf16[80,6144]{1,0:T(8,128)(2,1)}, u32[]{:S(2)}, u32[]{:S(2)}) collective-permute-start(bf16[80,6144]{1,0:T(8,128)(2,1)S(1)} %collective-permute-done.4.refs_5_), channel_id=1, source_target_pairs={{0,1},{1,0},{2,3},{3,2},{4,5},{5,4},{6,7},{7,6},{8,9},{9,8},{10,11... | collective-permute-start | bytes 2949128 | tf_op jit(solution)/shard_map/ppermute | solution.py:162
  95.9 20.3 %collective-permute-start.13 = (bf16[80,6144]{1,0:T(8,128)(2,1)S(1)}, bf16[80,6144]{1,0:T(8,128)(2,1)}, u32[]{:S(2)}, u32[]{:S(2)}) collective-permute-start(bf16[80,6144]{1,0:T(8,128)(2,1)S(1)} %collective-permute-done.5.refs_6_), channel_id=1, source_target_pairs={{0,1},{1,0},{2,3},{3,2},{4,5},{5,4},{6,7},{7,6},{8,9},{9,8},{10,11... | collective-permute-start | bytes 2949128 | tf_op jit(solution)/shard_map/ppermute | solution.py:162
  96.9 11.6 %collective-permute-start.6 = (bf16[32,6144]{1,0:T(8,128)(2,1)S(1)}, bf16[32,6144]{1,0:T(8,128)(2,1)}, u32[]{:S(2)}, u32[]{:S(2)}) collective-permute-start(bf16[32,6144]{1,0:T(8,128)(2,1)S(1)} %slice.62), channel_id=1, source_target_pairs={{0,2},{1,3},{4,0},{5,1},{8,4},{9,5},{12,8},{13,9},{14,12},{15,13},... | collective-permute-start | bytes 1179656 | tf_op jit(solution)/shard_map/ppermute | solution.py:162
  108.6 5.5 %collective-permute-start.14 = (bf16[32,6144]{1,0:T(8,128)(2,1)}, bf16[32,6144]{1,0:T(8,128)(2,1)S(1)}, u32[]{:S(2)}, u32[]{:S(2)}) collective-permute-start(bf16[32,6144]{1,0:T(8,128)(2,1)} %collective-permute-done.6.refs_7_), channel_id=1, source_target_pairs={{0,1},{1,0},{2,3},{3,2},{4,5},{5,4},{6,7},{7,6},{8,9},{9,8},{10,11... | collective-permute-start | bytes 1179656 | tf_op jit(solution)/shard_map/ppermute | solution.py:162
  110.3 23.7 %collective-permute-start.35 = (bf16[768,768]{1,0:T(8,128)(2,1)}, bf16[768,768]{1,0:T(8,128)(2,1)}, u32[]{:S(2)}, u32[]{:S(2)}) collective-permute-start(bf16[768,768]{1,0:T(8,128)(2,1)} %bitcast.47), channel_id=1, source_target_pairs={{0,1},{1,0},{2,3},{3,2},{4,5},{5,4},{6,7},{7,6},{8,9},{9,8},{10,11... | collective-permute-start | bytes 3538952 | tf_op jit(solution)/shard_map/ppermute | solution.py:162
  110.8 19.2 %collective-permute-start.27 = (bf16[768,256]{1,0:T(8,128)(2,1)}, bf16[768,256]{1,0:T(8,128)(2,1)S(1)}, u32[]{:S(2)}, u32[]{:S(2)}) collective-permute-start(bf16[768,256]{1,0:T(8,128)(2,1)} %slice_bitcast_fusion.5), channel_id=1, source_target_pairs={{0,16},{16,0},{1,17},{17,1},{2,18},{18,2},{3,19},{19,3},{4,20},{20... | collective-permute-start | bytes 1179656 | tf_op jit(solution)/shard_map/ppermute | solution.py:166
  114.1 18.4 %collective-permute-start.28 = (bf16[768,256]{1,0:T(8,128)(2,1)}, bf16[768,256]{1,0:T(8,128)(2,1)}, u32[]{:S(2)}, u32[]{:S(2)}) collective-permute-start(bf16[768,256]{1,0:T(8,128)(2,1)} %slice_bitcast_fusion.4), channel_id=1, source_target_pairs={{0,16},{16,0},{1,17},{17,1},{2,18},{18,2},{3,19},{19,3},{4,20},{20... | collective-permute-start | bytes 1179656 | tf_op jit(solution)/shard_map/ppermute | solution.py:166
  114.6 19.4 %collective-permute-start.21 = (bf16[2,768,256]{2,1,0:T(8,128)(2,1)}, bf16[2,768,256]{2,1,0:T(8,128)(2,1)}, u32[]{:S(2)}, u32[]{:S(2)}) collective-permute-start(bf16[2,768,256]{2,1,0:T(8,128)(2,1)} %collective-permute-done.19.refs_1_), channel_id=1, source_target_pairs={{0,4},{1,5},{4,8},{5,9},{8,12},{9,13},{12,14},{13,15},{14,10},{15,... | collective-permute-start | bytes 2359304 | tf_op jit(solution)/shard_map/ppermute | solution.py:162
  116.2 19.4 %collective-permute-start.22 = (bf16[2,768,256]{2,1,0:T(8,128)(2,1)}, bf16[2,768,256]{2,1,0:T(8,128)(2,1)}, u32[]{:S(2)}, u32[]{:S(2)}) collective-permute-start(bf16[2,768,256]{2,1,0:T(8,128)(2,1)} %copy-done.15), channel_id=1, source_target_pairs={{0,2},{1,3},{4,0},{5,1},{8,4},{9,5},{12,8},{13,9},{14,12},{15,13},... | collective-permute-start | bytes 2359304 | tf_op jit(solution)/shard_map/ppermute | solution.py:162
  130.1 5.7 %collective-permute-start.36 = (bf16[2,768,256]{2,1,0:T(8,128)(2,1)}, bf16[2,768,256]{2,1,0:T(8,128)(2,1)S(1)}, u32[]{:S(2)}, u32[]{:S(2)}) collective-permute-start(bf16[2,768,256]{2,1,0:T(8,128)(2,1)} %collective-permute-done.19.refs_1_), channel_id=1, source_target_pairs={{0,1},{1,0},{2,3},{3,2},{4,5},{5,4},{6,7},{7,6},{8,9},{9,8},{10,11... | collective-permute-start | bytes 2359304 | tf_op jit(solution)/shard_map/ppermute | solution.py:162
  132.5 119.7 %collective-permute-start.15 = (bf16[240,6144]{1,0:T(8,128)(2,1)S(1)}, bf16[240,6144]{1,0:T(8,128)(2,1)S(1)}, u32[]{:S(2)}, u32[]{:S(2)}) collective-permute-start(bf16[240,6144]{1,0:T(8,128)(2,1)S(1)} %dynamic-slice_bitcast_fusion), channel_id=1, source_target_pairs={{0,16},{16,0},{1,17},{17,1},{2,18},{18,2},{3,19},{19,3},{4,20},{20... | collective-permute-start | bytes 8847368 | tf_op jit(solution)/shard_map/ppermute | solution.py:166
  134.0 4.0 %collective-permute-start.37 = (bf16[2,768,256]{2,1,0:T(8,128)(2,1)S(1)}, bf16[2,768,256]{2,1,0:T(8,128)(2,1)S(1)}, u32[]{:S(2)}, u32[]{:S(2)}) collective-permute-start(bf16[2,768,256]{2,1,0:T(8,128)(2,1)S(1)} %copy-done.16), channel_id=1, source_target_pairs={{0,1},{1,0},{2,3},{3,2},{4,5},{5,4},{6,7},{7,6},{8,9},{9,8},{10,11... | collective-permute-start | bytes 2359304 | tf_op jit(solution)/shard_map/ppermute | solution.py:162
  134.1 4.8 %collective-permute-start.44 = (bf16[768,256]{1,0:T(8,128)(2,1)S(1)}, bf16[768,256]{1,0:T(8,128)(2,1)S(1)}, u32[]{:S(2)}, u32[]{:S(2)}) collective-permute-start(bf16[768,256]{1,0:T(8,128)(2,1)S(1)} %collective-permute-done.27.refs_9_), channel_id=1, source_target_pairs={{0,1},{1,0},{2,3},{3,2},{4,5},{5,4},{6,7},{7,6},{8,9},{9,8},{10,11... | collective-permute-start | bytes 1179656 | tf_op jit(solution)/shard_map/ppermute | solution.py:162
  135.6 5.6 %collective-permute-start.45 = (bf16[768,256]{1,0:T(8,128)(2,1)}, bf16[768,256]{1,0:T(8,128)(2,1)S(1)}, u32[]{:S(2)}, u32[]{:S(2)}) collective-permute-start(bf16[768,256]{1,0:T(8,128)(2,1)} %collective-permute-done.28.refs_10_), channel_id=1, source_target_pairs={{0,1},{1,0},{2,3},{3,2},{4,5},{5,4},{6,7},{7,6},{8,9},{9,8},{10,11... | collective-permute-start | bytes 1179656 | tf_op jit(solution)/shard_map/ppermute | solution.py:162
  135.7 83.9 %copy-start.45 = (bf16[2,768,256]{2,1,0:T(8,128)(2,1)}, bf16[2,768,256]{2,1,0:T(8,128)(2,1)S(1)}, u32[]{:S(2)}) copy-start(bf16[2,768,256]{2,1,0:T(8,128)(2,1)S(1)} %collective-permute-done.36.refs_18_) | copy-start | bytes 2359300
  135.7 72.0 %collective-permute-start.29 = (bf16[768,256]{1,0:T(8,128)(2,1)S(1)}, bf16[768,256]{1,0:T(8,128)(2,1)S(1)}, u32[]{:S(2)}, u32[]{:S(2)}) collective-permute-start(bf16[768,256]{1,0:T(8,128)(2,1)S(1)} %slice_bitcast_fusion.3), channel_id=1, source_target_pairs={{0,16},{16,0},{1,17},{17,1},{2,18},{18,2},{3,19},{19,3},{4,20},{20... | collective-permute-start | bytes 1179656 | tf_op jit(solution)/shard_map/ppermute | solution.py:166
  138.1 114.6 %copy-start.46 = (bf16[2,768,256]{2,1,0:T(8,128)(2,1)}, bf16[2,768,256]{2,1,0:T(8,128)(2,1)S(1)}, u32[]{:S(2)}) copy-start(bf16[2,768,256]{2,1,0:T(8,128)(2,1)S(1)} %collective-permute-done.37.refs_19_) | copy-start | bytes 2359300
  138.1 77.4 %collective-permute-start.30 = (bf16[768,256]{1,0:T(8,128)(2,1)S(1)}, bf16[768,256]{1,0:T(8,128)(2,1)S(1)}, u32[]{:S(2)}, u32[]{:S(2)}) collective-permute-start(bf16[768,256]{1,0:T(8,128)(2,1)S(1)} %slice_bitcast_fusion.2), channel_id=1, source_target_pairs={{0,16},{16,0},{1,17},{17,1},{2,18},{18,2},{3,19},{19,3},{4,20},{20... | collective-permute-start | bytes 1179656 | tf_op jit(solution)/shard_map/ppermute | solution.py:166
  139.6 75.9 %collective-permute-start.23 = (bf16[2,768,256]{2,1,0:T(8,128)(2,1)}, bf16[2,768,256]{2,1,0:T(8,128)(2,1)S(1)}, u32[]{:S(2)}, u32[]{:S(2)}) collective-permute-start(bf16[2,768,256]{2,1,0:T(8,128)(2,1)} %collective-permute-done.21.refs_3_), channel_id=1, source_target_pairs={{0,4},{1,5},{4,8},{5,9},{8,12},{9,13},{12,14},{13,15},{14,10},{15,... | collective-permute-start | bytes 2359304 | tf_op jit(solution)/shard_map/ppermute | solution.py:162
  142.0 75.2 %collective-permute-start.24 = (bf16[2,768,256]{2,1,0:T(8,128)(2,1)}, bf16[2,768,256]{2,1,0:T(8,128)(2,1)S(1)}, u32[]{:S(2)}, u32[]{:S(2)}) collective-permute-start(bf16[2,768,256]{2,1,0:T(8,128)(2,1)} %collective-permute-done.22.refs_4_), channel_id=1, source_target_pairs={{0,2},{1,3},{4,0},{5,1},{8,4},{9,5},{12,8},{13,9},{14,12},{15,13},... | collective-permute-start | bytes 2359304 | tf_op jit(solution)/shard_map/ppermute | solution.py:162
  207.7 9.8 %collective-permute-start.38 = (bf16[2,768,256]{2,1,0:T(8,128)(2,1)}, bf16[2,768,256]{2,1,0:T(8,128)(2,1)}, u32[]{:S(2)}, u32[]{:S(2)}) collective-permute-start(bf16[2,768,256]{2,1,0:T(8,128)(2,1)} %collective-permute-done.21.refs_3_), channel_id=1, source_target_pairs={{0,1},{1,0},{2,3},{3,2},{4,5},{5,4},{6,7},{7,6},{8,9},{9,8},{10,11... | collective-permute-start | bytes 2359304 | tf_op jit(solution)/shard_map/ppermute | solution.py:162
  215.5 2.5 collective-permute-start.39
  215.5 38.2 %copy-start.5 = (bf16[80,6144]{1,0:T(8,128)(2,1)S(1)}, bf16[80,6144]{1,0:T(8,128)(2,1)}, u32[]{:S(2)}) copy-start(bf16[80,6144]{1,0:T(8,128)(2,1)} %copy-done.3) | copy-start | bytes 2949124
  215.5 38.2 %copy-start.8 = (bf16[80,6144]{1,0:T(8,128)(2,1)S(1)}, bf16[80,6144]{1,0:T(8,128)(2,1)}, u32[]{:S(2)}) copy-start(bf16[80,6144]{1,0:T(8,128)(2,1)} %copy-done.6) | copy-start | bytes 2949124
  215.6 38.2 %copy-start.11 = (bf16[80,6144]{1,0:T(8,128)(2,1)S(1)}, bf16[80,6144]{1,0:T(8,128)(2,1)}, u32[]{:S(2)}) copy-start(bf16[80,6144]{1,0:T(8,128)(2,1)} %copy-done.9) | copy-start | bytes 2949124
  215.6 38.2 %copy-start.14 = (bf16[80,6144]{1,0:T(8,128)(2,1)S(1)}, bf16[80,6144]{1,0:T(8,128)(2,1)}, u32[]{:S(2)}) copy-start(bf16[80,6144]{1,0:T(8,128)(2,1)} %copy-done.12) | copy-start | bytes 2949124
  215.6 16.2 %collective-permute-start.16 = (bf16[48,6144]{1,0:T(8,128)(2,1)S(1)}, bf16[48,6144]{1,0:T(8,128)(2,1)S(1)}, u32[]{:S(2)}, u32[]{:S(2)}) collective-permute-start(bf16[48,6144]{1,0:T(8,128)(2,1)S(1)} %slice.63), channel_id=1, source_target_pairs={{0,4},{1,5},{4,8},{5,9},{8,12},{9,13},{12,14},{13,15},{14,10},{15,... | collective-permute-start | bytes 1769480 | tf_op jit(solution)/shard_map/ppermute | solution.py:162
  217.2 2.4 collective-permute-start.46
  217.5 2.9 collective-permute-start.47
  218.0 44.9 %copy-start.47 = (bf16[2,768,256]{2,1,0:T(8,128)(2,1)}, bf16[2,768,256]{2,1,0:T(8,128)(2,1)S(1)}, u32[]{:S(2)}) copy-start(bf16[2,768,256]{2,1,0:T(8,128)(2,1)S(1)} %collective-permute-done.39.refs_21_) | copy-start | bytes 2359300
  218.0 21.8 %collective-permute-start.25 = (bf16[2,384,256]{2,1,0:T(8,128)(2,1)S(1)}, bf16[2,384,256]{2,1,0:T(8,128)(2,1)S(1)}, u32[]{:S(2)}, u32[]{:S(2)}) collective-permute-start(bf16[2,384,256]{2,1,0:T(8,128)(2,1)S(1)} %slice.65), channel_id=1, source_target_pairs={{0,4},{1,5},{4,8},{5,9},{8,12},{9,13},{12,14},{13,15},{14,10},{15,... | collective-permute-start | bytes 1179656 | tf_op jit(solution)/shard_map/ppermute | solution.py:162
  219.6 33.1 %copy-start.30 = (bf16[768,256]{1,0:T(8,128)(2,1)}, bf16[768,256]{1,0:T(8,128)(2,1)S(1)}, u32[]{:S(2)}) copy-start(bf16[768,256]{1,0:T(8,128)(2,1)S(1)} %collective-permute-done.46.refs_28_) | copy-start | bytes 1179652
  219.6 21.7 %collective-permute-start.26 = (bf16[2,384,256]{2,1,0:T(8,128)(2,1)S(1)}, bf16[2,384,256]{2,1,0:T(8,128)(2,1)}, u32[]{:S(2)}, u32[]{:S(2)}) collective-permute-start(bf16[2,384,256]{2,1,0:T(8,128)(2,1)S(1)} %slice.66), channel_id=1, source_target_pairs={{0,2},{1,3},{4,0},{5,1},{8,4},{9,5},{12,8},{13,9},{14,12},{15,13},... | collective-permute-start | bytes 1179656 | tf_op jit(solution)/shard_map/ppermute | solution.py:162
  220.3 32.4 %copy-start.32 = (bf16[768,256]{1,0:T(8,128)(2,1)}, bf16[768,256]{1,0:T(8,128)(2,1)S(1)}, u32[]{:S(2)}) copy-start(bf16[768,256]{1,0:T(8,128)(2,1)S(1)} %collective-permute-done.47.refs_29_) | copy-start | bytes 1179652
  220.3 21.1 %collective-permute-start.31 = (bf16[768,256]{1,0:T(8,128)(2,1)S(1)}, bf16[768,256]{1,0:T(8,128)(2,1)}, u32[]{:S(2)}, u32[]{:S(2)}) collective-permute-start(bf16[768,256]{1,0:T(8,128)(2,1)S(1)} %slice_bitcast_fusion.1), channel_id=1, source_target_pairs={{0,16},{16,0},{1,17},{17,1},{2,18},{18,2},{3,19},{19,3},{4,20},{20... | collective-permute-start | bytes 1179656 | tf_op jit(solution)/shard_map/ppermute | solution.py:166
  231.8 20.9 %collective-permute-start.17 = (bf16[48,6144]{1,0:T(8,128)(2,1)S(1)}, bf16[48,6144]{1,0:T(8,128)(2,1)S(1)}, u32[]{:S(2)}, u32[]{:S(2)}) collective-permute-start(bf16[48,6144]{1,0:T(8,128)(2,1)S(1)} %collective-permute-done.16.refs_7_), channel_id=1, source_target_pairs={{0,1},{1,0},{2,3},{3,2},{4,5},{5,4},{6,7},{7,6},{8,9},{9,8},{10,11... | collective-permute-start | bytes 1769480 | tf_op jit(solution)/shard_map/ppermute | solution.py:162
  239.8 10.9 %collective-permute-start.32 = (bf16[768,256]{1,0:T(8,128)(2,1)S(1)}, bf16[768,256]{1,0:T(8,128)(2,1)}, u32[]{:S(2)}, u32[]{:S(2)}) collective-permute-start(bf16[768,256]{1,0:T(8,128)(2,1)S(1)} %slice_bitcast_fusion), channel_id=1, source_target_pairs={{0,16},{16,0},{1,17},{17,1},{2,18},{18,2},{3,19},{19,3},{4,20},{20... | collective-permute-start | bytes 1179656 | tf_op jit(solution)/shard_map/ppermute | solution.py:166
  241.3 23.2 %collective-permute-start.40 = (bf16[2,768,256]{2,1,0:T(8,128)(2,1)S(1)}, bf16[2,768,256]{2,1,0:T(8,128)(2,1)S(1)}, u32[]{:S(2)}, u32[]{:S(2)}) collective-permute-start(bf16[2,768,256]{2,1,0:T(8,128)(2,1)S(1)} %collective-permute-done.23.refs_5_), channel_id=1, source_target_pairs={{0,1},{1,0},{2,3},{3,2},{4,5},{5,4},{6,7},{7,6},{8,9},{9,8},{10,11... | collective-permute-start | bytes 2359304 | tf_op jit(solution)/shard_map/ppermute | solution.py:162
  241.4 23.5 %collective-permute-start.41 = (bf16[2,768,256]{2,1,0:T(8,128)(2,1)S(1)}, bf16[2,768,256]{2,1,0:T(8,128)(2,1)S(1)}, u32[]{:S(2)}, u32[]{:S(2)}) collective-permute-start(bf16[2,768,256]{2,1,0:T(8,128)(2,1)S(1)} %collective-permute-done.24.refs_6_), channel_id=1, source_target_pairs={{0,1},{1,0},{2,3},{3,2},{4,5},{5,4},{6,7},{7,6},{8,9},{9,8},{10,11... | collective-permute-start | bytes 2359304 | tf_op jit(solution)/shard_map/ppermute | solution.py:162
  250.7 13.1 %collective-permute-start.33 = (bf16[384,256]{1,0:T(8,128)(2,1)S(1)}, bf16[384,256]{1,0:T(8,128)(2,1)}, u32[]{:S(2)}, u32[]{:S(2)}) collective-permute-start(bf16[384,256]{1,0:T(8,128)(2,1)S(1)} %slice_bitcast_fusion.8), channel_id=1, source_target_pairs={{0,16},{16,0},{1,17},{17,1},{2,18},{18,2},{3,19},{19,3},{4,20},{20... | collective-permute-start | bytes 589832 | tf_op jit(solution)/shard_map/ppermute | solution.py:166
  252.1 12.2 %collective-permute-start.34 = (bf16[384,256]{1,0:T(8,128)(2,1)S(1)}, bf16[384,256]{1,0:T(8,128)(2,1)}, u32[]{:S(2)}, u32[]{:S(2)}) collective-permute-start(bf16[384,256]{1,0:T(8,128)(2,1)S(1)} %slice_bitcast_fusion.7), channel_id=1, source_target_pairs={{0,16},{16,0},{1,17},{17,1},{2,18},{18,2},{3,19},{19,3},{4,20},{20... | collective-permute-start | bytes 589832 | tf_op jit(solution)/shard_map/ppermute | solution.py:166
  252.7 12.3 %collective-permute-start.42 = (bf16[2,384,256]{2,1,0:T(8,128)(2,1)S(1)}, bf16[2,384,256]{2,1,0:T(8,128)(2,1)S(1)}, u32[]{:S(2)}, u32[]{:S(2)}) collective-permute-start(bf16[2,384,256]{2,1,0:T(8,128)(2,1)S(1)} %collective-permute-done.25.refs_7_), channel_id=1, source_target_pairs={{0,1},{1,0},{2,3},{3,2},{4,5},{5,4},{6,7},{7,6},{8,9},{9,8},{10,11... | collective-permute-start | bytes 1179656 | tf_op jit(solution)/shard_map/ppermute | solution.py:162
  263.8 10.0 %collective-permute-start.18 = (bf16[240,768]{1,0:T(8,128)(2,1)S(1)}, bf16[240,768]{1,0:T(8,128)(2,1)S(1)}, u32[]{:S(2)}, u32[]{:S(2)}) collective-permute-start(bf16[240,768]{1,0:T(8,128)(2,1)S(1)} %get-tuple-element.9), channel_id=1, source_target_pairs={{0,16},{16,0},{1,17},{17,1},{2,18},{18,2},{3,19},{19,3},{4,20},{20... | collective-permute-start | bytes 1105928 | tf_op jit(solution)/shard_map/ppermute | solution.py:166
  264.4 19.1 %collective-permute-start.43 = (bf16[2,384,256]{2,1,0:T(8,128)(2,1)}, bf16[2,384,256]{2,1,0:T(8,128)(2,1)S(1)}, u32[]{:S(2)}, u32[]{:S(2)}) collective-permute-start(bf16[2,384,256]{2,1,0:T(8,128)(2,1)} %collective-permute-done.26.refs_8_), channel_id=1, source_target_pairs={{0,1},{1,0},{2,3},{3,2},{4,5},{5,4},{6,7},{7,6},{8,9},{9,8},{10,11... | collective-permute-start | bytes 1179656 | tf_op jit(solution)/shard_map/ppermute | solution.py:162
  264.5 18.9 %collective-permute-start.48 = (bf16[768,256]{1,0:T(8,128)(2,1)}, bf16[768,256]{1,0:T(8,128)(2,1)S(1)}, u32[]{:S(2)}, u32[]{:S(2)}) collective-permute-start(bf16[768,256]{1,0:T(8,128)(2,1)} %collective-permute-done.31.refs_13_), channel_id=1, source_target_pairs={{0,1},{1,0},{2,3},{3,2},{4,5},{5,4},{6,7},{7,6},{8,9},{9,8},{10,11... | collective-permute-start | bytes 1179656 | tf_op jit(solution)/shard_map/ppermute | solution.py:162
  264.9 18.6 %collective-permute-start.49 = (bf16[768,256]{1,0:T(8,128)(2,1)}, bf16[768,256]{1,0:T(8,128)(2,1)S(1)}, u32[]{:S(2)}, u32[]{:S(2)}) collective-permute-start(bf16[768,256]{1,0:T(8,128)(2,1)} %collective-permute-done.32.refs_14_), channel_id=1, source_target_pairs={{0,1},{1,0},{2,3},{3,2},{4,5},{5,4},{6,7},{7,6},{8,9},{9,8},{10,11... | collective-permute-start | bytes 1179656 | tf_op jit(solution)/shard_map/ppermute | solution.py:162
  265.9 17.6 %collective-permute-start.50 = (bf16[384,256]{1,0:T(8,128)(2,1)}, bf16[384,256]{1,0:T(8,128)(2,1)S(1)}, u32[]{:S(2)}, u32[]{:S(2)}) collective-permute-start(bf16[384,256]{1,0:T(8,128)(2,1)} %collective-permute-done.33.refs_15_), channel_id=1, source_target_pairs={{0,1},{1,0},{2,3},{3,2},{4,5},{5,4},{6,7},{7,6},{8,9},{9,8},{10,11... | collective-permute-start | bytes 589832 | tf_op jit(solution)/shard_map/ppermute | solution.py:162
  273.8 9.7 %collective-permute-start.51 = (bf16[384,256]{1,0:T(8,128)(2,1)}, bf16[384,256]{1,0:T(8,128)(2,1)S(1)}, u32[]{:S(2)}, u32[]{:S(2)}) collective-permute-start(bf16[384,256]{1,0:T(8,128)(2,1)} %collective-permute-done.34.refs_16_), channel_id=1, source_target_pairs={{0,1},{1,0},{2,3},{3,2},{4,5},{5,4},{6,7},{7,6},{8,9},{9,8},{10,11... | collective-permute-start | bytes 589832 | tf_op jit(solution)/shard_map/ppermute | solution.py:162
  (40 other events, 293.3 us)
Sparse Core Ops, SparseCore 0:
  130.1 46.0 all-gather.2

commit v2 on v1

--- a/solution.py
+++ b/solution.py
@@ -158,6 +158,78 @@
     return table
 
 
+def in_hbm(blocks):
+    return [pltpu.with_memory_space_constraint(block, pltpu.HBM) for block in blocks]
+
+
+def in_vmem(blocks):
+    return [pltpu.with_memory_space_constraint(block, pltpu.VMEM) for block in blocks]
+
+
+def hold_kernel(packs, *refs):
+    for pack, out_ref in zip(packs, refs[len(refs) - len(packs) :]):
+        at = 0
+        for n, first, size in pack:
+            out_ref[at : at + size] = refs[n][first : first + size]
+            at += size
+
+
+def together(*blocks, packs=()):
+    read = [n for pack in packs for n, first, size in pack]
+    packed = [
+        (sum(size for n, first, size in pack),) + blocks[pack[0][0]].shape[1:] for pack in packs
+    ]
+    return pl.pallas_call(
+        partial(hold_kernel, packs),
+        in_specs=[
+            pl.BlockSpec(memory_space=pltpu.VMEM if n in read else pl.ANY) for n in range(len(blocks))
+        ],
+        out_specs=[pl.BlockSpec(memory_space=pl.ANY)] * len(blocks)
+        + [pl.BlockSpec(memory_space=pltpu.VMEM)] * len(packs),
+        out_shape=[pltpu.VMEM(block.shape, block.dtype) for block in blocks]
+        + [pltpu.VMEM(shape, jnp.bfloat16) for shape in packed],
+        input_output_aliases={n: n for n in range(len(blocks))},
+        compiler_params=pltpu.CompilerParams(vmem_limit_bytes=2**20),
+        name="together",
+    )(*in_vmem(blocks))
+
+
+def copy_kernel(plan, facts, *refs):
+    sem = refs[-1]
+    group = facts[GROUP]
+    copies = []
+    for n, (source, out, row, first, flip, shape) in enumerate(plan):
+        side = 1 - group if flip else group
+        width = shape[-1]
+        start = first if flip is None else pl.multiple_of(side * width, width)
+        view = refs[source].at[pl.ds(row[0], shape[0]), pl.ds(start, width)]
+        copies.append(
+            pltpu.make_async_copy(view, refs[out].at[pl.ds(row[1], shape[0])], sem.at[n])
+        )
+    for copy in copies:
+        copy.start()
+    for copy in copies:
+        copy.wait()
+
+
+def take_parts(facts, sources, outs, plan):
+    count = len(sources)
+    plan = [(s, count + o, *rest) for s, o, *rest in plan]
+    return pl.pallas_call(
+        partial(copy_kernel, plan),
+        grid_spec=pltpu.PrefetchScalarGridSpec(
+            num_scalar_prefetch=1,
+            grid=(),
+            in_specs=[pl.BlockSpec(memory_space=pl.ANY)] * count,
+            out_specs=[pl.BlockSpec(memory_space=pltpu.VMEM)] * len(outs),
+            scratch_shapes=[pltpu.SemaphoreType.DMA((len(plan),))],
+        ),
+        out_shape=[pltpu.VMEM(shape, jnp.bfloat16) for shape in outs],
+        compiler_params=pltpu.CompilerParams(vmem_limit_bytes=2**20),
+        name="take_parts",
+    )(facts, *in_hbm(sources))
+
+
 def move(block, pairs):
     return lax.ppermute(block, "serve", pairs)
 
@@ -166,21 +238,33 @@
     return lax.ppermute(block, "groups", ACROSS)
 
 
-def column_order(order_ref, slots, planes):
+GROUP, LENGTH, ORDER, TABLE = 0, 1, 2, 2 + CHIPS * CORES
+
+
+def column_order(facts, slots, planes):
     rows, width = planes * 8, planes * HD
     row = lax.broadcasted_iota(jnp.int32, (rows, width), 0)
     col = lax.broadcasted_iota(jnp.int32, (rows, width), 1)
     place = (row // 8) * HD + row % 8
-    parts = [(col == place + order_ref[p] * 8).astype(jnp.float32) for p in range(slots)]
+    parts = [(col == place + facts[ORDER + p] * 8).astype(jnp.float32) for p in range(slots)]
     return jnp.concatenate(parts, axis=0).astype(jnp.bfloat16)
 
 
-def kv_kernel(order_ref, table_ref, len_ref, span_ref, req_ref, *refs):
+def kv_kernel(facts, span_ref, req_ref, *refs):
     slots = CHIPS * CORES
     w_refs = refs[:slots]
     pay_ref, new_ref, cache_ref, span_acc, req_acc = refs[slots:]
     step = pl.program_id(0)
-    w = jnp.concatenate([ref[...] for ref in w_refs], axis=0)
+    chunk = span_ref.shape[2]
+    per_half = w_refs[0].shape[1] // chunk
+    columns = pl.ds(pl.multiple_of(step % per_half * chunk, chunk), chunk)
+    w = jnp.concatenate(
+        [
+            ref[pl.ds(pl.multiple_of(ref.shape[0] - 32 + step // per_half * 16, 16), 16), columns]
+            for ref in w_refs
+        ],
+        axis=0,
+    )
     span_now = lax.dot_general(span_ref[0], w, NT, preferred_element_type=jnp.float32)
     req_now = lax.dot_general(req_ref[0], w, NT, preferred_element_type=jnp.float32)
 
@@ -196,7 +280,7 @@
 
     @pl.when(step == pl.num_programs(0) - 1)
     def _():
-        order = column_order(order_ref, slots, 2)
+        order = column_order(facts, slots, 2)
         span_kv = jnp.dot(
             span_acc[...].astype(jnp.bfloat16), order, preferred_element_type=jnp.float32
         ).astype(jnp.bfloat16)
@@ -205,34 +289,26 @@
         ).astype(jnp.bfloat16)
         tokens = span_kv.shape[0]
         pay_ref[0:tokens] = span_kv
-        length = jnp.full((PAGE, 2 * HD), len_ref[0], jnp.int32)
+        length = jnp.full((PAGE, 2 * HD), facts[LENGTH], jnp.int32)
         pay_ref[tokens:] = length.astype(jnp.float32).astype(jnp.bfloat16)
         for p in range(tokens // PAGE):
-            cache_ref[table_ref[p]] = span_kv[p * PAGE : (p + 1) * PAGE]
-
-
-def project_kv(order, block_table, span_lengths, span_states, recomp_states, w_blocks, last_block):
+            cache_ref[facts[TABLE + p]] = span_kv[p * PAGE : (p + 1) * PAGE]
+
+
+def project_kv(facts, span_states, recomp_states, w_blocks, last_block):
     tokens, width = span_states.shape[1:]
     rows = recomp_states.shape[1]
     chunk = width // 4
-    per_half = width // 2 // chunk
-    rows_at = w_blocks[0].shape[0] // 16 - 2
-
-    def piece(first):
-        return pl.BlockSpec((16, chunk), lambda k, *_: (first + k // per_half, k % per_half))
-
-    half_slots = [piece(rows_at)] * (CHIPS - 1) + [piece(0)]
     blocks = w_blocks[: CHIPS - 1] + last_block[:1] + w_blocks[CHIPS - 1 :] + last_block[1:]
     return pl.pallas_call(
         kv_kernel,
         grid_spec=pltpu.PrefetchScalarGridSpec(
-            num_scalar_prefetch=3,
+            num_scalar_prefetch=1,
             grid=(width // chunk,),
             in_specs=[
                 pl.BlockSpec((1, tokens, chunk), lambda k, *_: (0, 0, k)),
                 pl.BlockSpec((1, rows, chunk), lambda k, *_: (0, 0, k)),
-                *half_slots,
-                *half_slots,
+                *([pl.BlockSpec(memory_space=pltpu.VMEM)] * len(blocks)),
             ],
             out_specs=[
                 pl.BlockSpec((tokens + PAGE, 2 * HD), lambda k, *_: (0, 0)),
@@ -254,19 +330,24 @@
             bytes_accessed=2 * (tokens + rows + 2 * HD) * width,
             transcendentals=0,
         ),
-        compiler_params=pltpu.CompilerParams(vmem_limit_bytes=40 * 2**20),
+        compiler_params=pltpu.CompilerParams(vmem_limit_bytes=16 * 2**20),
         name="project_kv",
-    )(order, block_table, span_lengths, span_states, recomp_states, *blocks)
-
-
-def query_kernel(half_ref, mine_ref, other_ref, *refs):
+    )(facts, *in_hbm([span_states, recomp_states]), *blocks)
+
+
+def query_kernel(facts, mine_ref, *refs):
     slots = CHIPS * CORES
     w_refs = refs[:slots]
-    mine_out, other_out, mine_acc, other_acc = refs[slots:]
+    other_refs = refs[slots:-4]
+    mine_out, other_out, mine_acc, other_acc = refs[-4:]
     step = pl.program_id(0)
-    w = jnp.concatenate([ref[...] for ref in w_refs], axis=0)
+    chunk = mine_ref.shape[2]
+    part = mine_out.shape[1] // slots
+    columns = pl.ds(pl.multiple_of(step * chunk, chunk), chunk)
+    w = jnp.concatenate([ref[0:part, columns] for ref in w_refs], axis=0)
     mine_now = lax.dot_general(mine_ref[0], w, NT, preferred_element_type=jnp.float32)
-    other_now = lax.dot_general(other_ref[...], w, NT, preferred_element_type=jnp.float32)
+    other = jnp.concatenate([ref[:, columns] for ref in other_refs], axis=0)
+    other_now = lax.dot_general(other, w, NT, preferred_element_type=jnp.float32)
 
     @pl.when(step == 0)
     def _():
@@ -284,11 +365,11 @@
         other_out[...] = other_acc[...].astype(other_out.dtype)
 
 
-def project_query(half, recomp_states, other_rows, w_blocks, last_block, columns):
-    rows, depth = other_rows.shape
+def project_query(facts, recomp_states, other_rows, w_blocks, last_block, columns):
+    rows = recomp_states.shape[1]
+    depth = other_rows[0].shape[1]
     chunk = depth // 6
     steps = depth // chunk
-    part = columns // (CHIPS * CORES)
     blocks = w_blocks[: CHIPS - 1] + last_block[:1] + w_blocks[CHIPS - 1 :] + last_block[1:]
     return pl.pallas_call(
         query_kernel,
@@ -296,9 +377,8 @@
             num_scalar_prefetch=1,
             grid=(steps,),
             in_specs=[
-                pl.BlockSpec((1, rows, chunk), lambda k, half_ref: (0, 0, half_ref[0] * steps + k)),
-                pl.BlockSpec((rows, chunk), lambda k, *_: (0, k)),
-                *([pl.BlockSpec((part, chunk), lambda k, *_: (0, k))] * (CHIPS * CORES)),
+                pl.BlockSpec((1, rows, chunk), lambda k, facts: (0, 0, facts[GROUP] * steps + k)),
+                *([pl.BlockSpec(memory_space=pltpu.VMEM)] * (len(blocks) + len(other_rows))),
             ],
             out_specs=[
                 pl.BlockSpec((rows, columns), lambda k, *_: (0, 0)),
@@ -318,12 +398,12 @@
             bytes_accessed=2 * (2 * rows + columns) * depth,
             transcendentals=0,
         ),
-        compiler_params=pltpu.CompilerParams(vmem_limit_bytes=40 * 2**20),
+        compiler_params=pltpu.CompilerParams(vmem_limit_bytes=16 * 2**20),
         name="project_query",
-    )(half, recomp_states, other_rows, *blocks)
-
-
-def attend_kernel(map_ref, order_ref, mine_ref, other_ref, new_ref, col_ref, row_ref, *refs):
+    )(facts, *in_hbm([recomp_states]), *blocks, *other_rows)
+
+
+def attend_kernel(map_ref, facts, mine_ref, other_ref, new_ref, row_ref, *refs):
     span_refs = refs[:CPR]
     out_ref, keys, values, bias = refs[CPR:]
     rows = new_ref.shape[0]
@@ -336,7 +416,13 @@
     values[cached : cached + rows] = new_ref[:, HD : 2 * HD]
     keys[cached + rows :] = jnp.zeros((padded - cached - rows, HD), jnp.bfloat16)
     values[cached + rows :] = jnp.zeros((padded - cached - rows, HD), jnp.bfloat16)
-    mine_at = jnp.broadcast_to(col_ref[...], (rows, SPAN))
+    new_pos = jnp.broadcast_to(row_ref[...], (rows, rows))
+    diagonal = lax.broadcasted_iota(jnp.int32, (rows, rows), 0) == lax.broadcasted_iota(
+        jnp.int32, (rows, rows), 1
+    )
+    mine_at = jnp.sum(jnp.where(diagonal, new_pos, 0), axis=1, keepdims=True)
+    new_allowed = new_pos <= jnp.broadcast_to(mine_at, (rows, rows))
+    mine_at = jnp.broadcast_to(mine_at, (rows, SPAN))
     lane = lax.broadcasted_iota(jnp.int32, (rows, SPAN), 1)
     blocked = jnp.float32(-jnp.inf)
     for s in range(CPR):
@@ -347,12 +433,12 @@
         usable = jnp.where(offset < length, 1.0 - redone, 0.0)
         allowed = (jnp.broadcast_to(usable, (rows, SPAN)) > 0.5) & (key_pos <= mine_at)
         bias[:, s * SPAN : (s + 1) * SPAN] = jnp.where(allowed, 0.0, blocked)
-    key_pos = jnp.broadcast_to(row_ref[...], (rows, padded - cached))
-    bias[:, cached:] = jnp.where(key_pos <= mine_at, 0.0, blocked)
+    bias[:, cached:] = jnp.full((rows, padded - cached), blocked, jnp.float32)
+    bias[:, cached : cached + rows] = jnp.where(new_allowed, 0.0, blocked)
 
     query = (mine_ref[...] + other_ref[...].astype(jnp.float32)).astype(jnp.bfloat16)
     heads = query.shape[1] // HD
-    order = column_order(order_ref, CHIPS * CORES, heads)
+    order = column_order(facts, CHIPS * CORES, heads)
     query = jnp.dot(query, order, preferred_element_type=jnp.float32).astype(jnp.bfloat16)
     for h in range(heads):
         scores = lax.dot_general(
@@ -366,11 +452,10 @@
         out_ref[:, h * HD : (h + 1) * HD] = (mixed / total).astype(jnp.bfloat16)
 
 
-def attend(span_map, order, mine, other, new_kv, positions, payload):
+def attend(span_map, facts, mine, other, new_kv, positions, payload):
     rows, columns = mine.shape
     cached = CPR * SPAN
     padded = cached + SPAN
-    row_pos = jnp.pad(positions, (0, SPAN - rows), constant_values=2 * cached)[None, :]
     whole = lambda *shape: pl.BlockSpec(shape, lambda i, *_: (0,) * len(shape))
     slot = lambda s: pl.BlockSpec((1,) + payload.shape[1:], lambda i, map_ref, *_: (map_ref[s], 0, 0))
     return pl.pallas_call(
@@ -382,8 +467,7 @@
                 whole(rows, columns),
                 whole(rows, columns),
                 whole(rows, 2 * HD),
-                whole(rows, 1),
-                whole(1, SPAN),
+                whole(1, rows),
                 *[slot(s) for s in range(CPR)],
             ],
             out_specs=whole(rows, columns),
@@ -399,42 +483,44 @@
             bytes_accessed=2 * padded * 2 * HD + 8 * rows * columns,
             transcendentals=rows * (columns // HD) * padded,
         ),
-        compiler_params=pltpu.CompilerParams(vmem_limit_bytes=40 * 2**20),
+        compiler_params=pltpu.CompilerParams(vmem_limit_bytes=20 * 2**20),
         name="attend",
-    )(span_map, order, mine, other, new_kv, positions[:, None], row_pos, *([payload] * CPR))
-
-
-def output_kernel(plan, order_ref, half_ref, att_ref, *refs):
-    count = 1 + max(copy[0] for copies in plan for copy in copies)
-    sources = refs[:count]
-    out_ref, w_buf, o_buf, in_sem, out_sem = refs[count:]
-    slots = len(plan)
-    third = w_buf.shape[3]
+    )(span_map, facts, mine, other, new_kv, positions, *in_hbm([payload] * CPR))
+
+
+def output_kernel(plan, arrived, facts, att_ref, att2_ref, *refs):
+    out_ref, sent_ref, w_buf, o_buf, in_sem, out_sem, late_sem = refs[-7:]
+    third = o_buf.shape[3]
+    rows = o_buf.shape[2]
     loads = []
-    for p, copies in enumerate(plan):
-        group = []
-        for n, (src, index, part, first, size) in enumerate(copies):
-            view = sources[src] if index is None else sources[src].at[index]
-            copy = pltpu.make_async_copy(
-                view, w_buf.at[p, part, pl.ds(first, size)], in_sem.at[p, n]
-            )
+    for p, (slot, lots) in enumerate(plan):
+        copies = []
+        for lot, parts in enumerate(lots):
+            for n, (source, row, column, first, size) in enumerate(parts):
+                view = refs[source].at[pl.ds(row, size), pl.ds(column, third)]
+                copies.append(
+                    pltpu.make_async_copy(
+                        view, w_buf.at[p, lot, pl.ds(first, size)], in_sem.at[p, lot, n]
+                    )
+                )
+        for copy in copies:
             copy.start()
-            group.append(copy)
-        loads.append(group)
-    stores = []
-    half = half_ref[0]
-    for p in range(slots):
+        loads.append(copies)
+    stores = place(facts, [(refs[source], slots) for source, slots in arrived], out_ref, late_sem)
+    attended = jnp.concatenate([att_ref[...], att2_ref[...]], axis=0)
+    for p, (slot, lots) in enumerate(plan):
         for copy in loads[p]:
             copy.wait()
-        own = p % CHIPS == 0
-        for part in range(3):
-            o_buf[p, part] = jnp.dot(
-                att_ref[...], w_buf[p, part], preferred_element_type=jnp.float32
+        for lot in range(len(lots)):
+            both = jnp.dot(
+                attended, w_buf[p, lot], preferred_element_type=jnp.float32
             ).astype(jnp.bfloat16)
-            lot = (half, 2, 1 - half)[part] if not own else part
-            start = pl.multiple_of(order_ref[p] * (3 * third) + lot * third, third)
+            o_buf[p, lot] = both[:rows]
+            sent_ref[p, lot] = both[rows:]
             copy = pltpu.make_async_copy(
-                o_buf.at[p, part], out_ref.at[0, :, pl.ds(start, third)], out_sem.at[p, part]
+                o_buf.at[p, lot],
+                out_ref.at[0, :, pl.ds(place_of(facts, slot, lot, third), third)],
+                out_sem.at[p, lot],
             )
             copy.start()
             stores.append(copy)
@@ -442,45 +528,98 @@
         copy.wait()
 
 
-def project_output(order, half, attended, plan, sources, depth, third):
-    rows = attended.shape[0]
-    slots = len(plan)
-    most = max(len(copies) for copies in plan)
-    width = slots * 3 * third
+def place_of(facts, slot, lot, third):
+    group = facts[GROUP]
+    kind = lot if slot % CHIPS == 0 else (group, 2, 1 - group)[lot]
+    return pl.multiple_of(facts[ORDER + slot] * (3 * third) + kind * third, third)
+
+
+def place(facts, arrived, out_ref, sem):
+    copies = []
+    for ref, slots in arrived:
+        third = ref.shape[3]
+        for p, slot in enumerate(slots):
+            for lot in range(3):
+                start = place_of(facts, slot + CHIPS, lot, third)
+                copy = pltpu.make_async_copy(
+                    ref.at[p, lot], out_ref.at[0, :, pl.ds(start, third)], sem.at[len(copies)]
+                )
+                copy.start()
+                copies.append(copy)
+    return copies
+
+
+def place_kernel(slots, facts, *refs):
+    before_ref, out_ref, sem = refs[-3:]
+    for copy in place(facts, list(zip(refs, slots)), out_ref, sem):
+        copy.wait()
+
+
+def place_output(facts, arrived, before):
+    blocks = [block for block, _ in arrived]
+    slots = [slots for _, slots in arrived]
     return pl.pallas_call(
-        partial(output_kernel, plan),
+        partial(place_kernel, slots),
         grid_spec=pltpu.PrefetchScalarGridSpec(
-            num_scalar_prefetch=2,
-            grid=(1,),
-            in_specs=[pl.BlockSpec((rows, depth), lambda i, *_: (0, 0))]
-            + [pl.BlockSpec(memory_space=pl.ANY)] * len(sources),
+            num_scalar_prefetch=1,
+            grid=(),
+            in_specs=[pl.BlockSpec(memory_space=pl.ANY)] * (len(blocks) + 1),
             out_specs=pl.BlockSpec(memory_space=pl.ANY),
+            scratch_shapes=[pltpu.SemaphoreType.DMA((3 * sum(map(len, slots)),))],
+        ),
+        out_shape=pltpu.HBM(before.shape, jnp.bfloat16),
+        input_output_aliases={1 + len(blocks): 0},
+        compiler_params=pltpu.CompilerParams(vmem_limit_bytes=2**20),
+        name="place_output",
+    )(facts, *blocks, *in_hbm([before]))
+
+
+def project_output(facts, attended, before, work, arrived, width):
+    rows, depth = attended[0].shape
+    sources = []
+
+    def index_of(block):
+        if not any(block is held for held in sources):
+            sources.append(block)
+        return [block is held for held in sources].index(True)
+
+    plan = [
+        (slot, [[(index_of(block), *where) for block, *where in lot] for lot in lots])
+        for slot, lots in work
+    ]
+    arrived = [(index_of(block), slots) for block, slots in arrived]
+    placed = 3 * sum(len(slots) for _, slots in arrived)
+    third = width // (CHIPS * CORES * 3)
+    filled = [] if before is None else [before]
+    return pl.pallas_call(
+        partial(output_kernel, plan, arrived),
+        grid_spec=pltpu.PrefetchScalarGridSpec(
+            num_scalar_prefetch=1,
+            grid=(),
+            in_specs=[pl.BlockSpec(memory_space=pltpu.VMEM)] * CORES
+            + [pl.BlockSpec(memory_space=pl.ANY)] * (len(sources) + len(filled)),
+            out_specs=[pl.BlockSpec(memory_space=pl.ANY), pl.BlockSpec(memory_space=pltpu.VMEM)],
             scratch_shapes=[
-                pltpu.VMEM((slots, 3, depth, third), jnp.bfloat16),
-                pltpu.VMEM((slots, 3, rows, third), jnp.bfloat16),
-                pltpu.SemaphoreType.DMA((slots, most)),
-                pltpu.SemaphoreType.DMA((slots, 3)),
-            ],
-        ),
-        out_shape=jax.ShapeDtypeStruct((1, rows, width), jnp.bfloat16),
+                pltpu.VMEM((len(plan), 3, depth, third), jnp.bfloat16),
+                pltpu.VMEM((len(plan), 3, rows, third), jnp.bfloat16),
+                pltpu.SemaphoreType.DMA((len(plan), 3, 2)),
+                pltpu.SemaphoreType.DMA((len(plan), 3)),
+                pltpu.SemaphoreType.DMA((max(placed, 1),)),
+            ],
+        ),
+        out_shape=[
+            pltpu.HBM((1, rows, width), jnp.bfloat16),
+            pltpu.VMEM((len(plan), 3, rows, third), jnp.bfloat16),
+        ],
+        input_output_aliases={1 + CORES + len(sources): 0} if filled else {},
         cost_estimate=pl.CostEstimate(
-            flops=2 * rows * depth * width,
-            bytes_accessed=2 * width * (rows + depth),
+            flops=2 * rows * CORES * depth * 3 * third * len(plan),
+            bytes_accessed=2 * 3 * third * len(plan) * (rows + depth),
             transcendentals=0,
         ),
-        compiler_params=pltpu.CompilerParams(vmem_limit_bytes=44 * 2**20),
+        compiler_params=pltpu.CompilerParams(vmem_limit_bytes=(len(plan) * 3 + 6) * 2**20),
         name="project_output",
-    )(order, half, attended, *sources)
-
-
-def gather_ring(block, split):
-    ahead = back = block
-    held = [block]
-    for _ in range(CHIPS // 2 - 1):
-        ahead, back = move(ahead, AHEAD), move(back, BACK)
-        held += [ahead, back]
-    first, second = split(ahead, back)
-    return held, (move(first, AHEAD), move(second, BACK))
+    )(facts, *attended, *sources, *in_hbm(filled))
 
 
 def ring_body(
@@ -494,68 +633,123 @@
     recompute_idx,
     block_table,
 ):
+    swap = lambda *blocks: tuple(move(block, SIBLING) for block in blocks)
     group = lax.axis_index("groups")
     width, heads, part = w_query.shape
+    rows = recomp_states.shape[1]
     half = width // 2
     depth = heads * HD
     columns = w_out.shape[3]
     third = columns // 3
-    slots = CHIPS * CORES
     order = jnp.asarray(slot_table())[lax.axis_index("serve")]
-    group_arr = group.astype(jnp.int32)[None]
-
-    theirs = lax.dynamic_slice_in_dim(recomp_states[0], (1 - group) * half, half, 1)
-    other_rows = across(theirs)
+    facts = jnp.concatenate([group[None].astype(jnp.int32), span_lengths, order, block_table])
+
     query_rows = w_query.transpose(1, 2, 0).reshape(heads * part, width)
-    query_rows = lax.dynamic_slice_in_dim(query_rows, group * half, half, 1)
     kv_rows = w_kv.transpose(1, 2, 0).reshape(2 * part, width)
-    block = jnp.concatenate([query_rows, kv_rows[:, :half], kv_rows[:, half:]], axis=0)
+    own_out = w_out.reshape(depth, columns)
+    lot = rows // 3
     cut = heads * part
-    held, (far_query, far_kv) = gather_ring(block, lambda a, b: (a[:cut], b[cut:]))
-    both = held + [move(b, SIBLING) for b in held]
-    far_query = [far_query, move(far_query, SIBLING)]
-    far_kv = [far_kv, move(far_kv, SIBLING)]
-
+    (block,) = take_parts(
+        facts,
+        [query_rows, kv_rows],
+        [(cut + 4 * part, half)],
+        [
+            (0, 0, (0, 0), 0, False, (cut, half)),
+            (1, 0, (0, cut), 0, None, (2 * part, half)),
+            (1, 0, (0, cut + 2 * part), half, None, (2 * part, half)),
+        ],
+    )
+    *theirs, out_block = take_parts(
+        facts,
+        [recomp_states[0], own_out, block],
+        [(lot, half)] * 3 + [(2 * depth, third)],
+        [(0, n, (n * lot, 0), 0, True, (lot, half)) for n in range(3)]
+        + [
+            (1, 3, (0, 0), 0, False, (depth, third)),
+            (1, 3, (0, depth), 2 * third, None, (depth, third)),
+        ],
+    )
+    out = (move(block, AHEAD), move(block, BACK), across(theirs[0]), *swap(block))
+    ahead1, back1, rows1, block2 = together(*out)
+    out = (move(ahead1, AHEAD), move(back1, BACK), across(theirs[1]), *swap(ahead1, back1))
+    ahead2, back2, rows2, *swapped1 = together(*out)
+    out = (move(ahead2, AHEAD), move(back2, BACK), across(theirs[2]), *swap(ahead2, back2))
+    ahead3, back3, rows3, *swapped2, to_ahead, to_back = together(
+        *out, packs=([(0, 0, cut)], [(1, cut, 4 * part)])
+    )
+    far_query, far_kv, out_block, *swapped3 = together(
+        move(to_ahead, AHEAD), move(to_back, BACK), out_block, *swap(ahead3, back3)
+    )
+    far_query2, far_kv2 = swap(far_query, far_kv)
+    both = [block, ahead1, back1, ahead2, back2, ahead3, back3, block2, *swapped1, *swapped2, *swapped3]
+
+    shared = lambda n: (n, 0, depth)
     payload, new_kv, cache = project_kv(
-        order, block_table, span_lengths, span_states, recomp_states, both, far_kv
-    )
+        facts, span_states, recomp_states, both, [far_kv, far_kv2]
+    )
+    mine, theirs_part = project_query(
+        facts, recomp_states, (rows1, rows2, rows3), both, [far_query, far_query2], depth
+    )
+    a1, b1, payload, theirs_part = lax.optimization_barrier(
+        (move(out_block, AHEAD), move(out_block, BACK), payload, theirs_part)
+    )
+    a1, b1, send1 = together(a1, b1, packs=([shared(0), shared(1)],))
     payloads = lax.all_gather(payload, "serve", axis=0)
-    mine, theirs_part = project_query(group_arr, recomp_states, other_rows, both, far_query, depth)
-    other = across(theirs_part)
-
-    own_out = w_out.reshape(depth, columns)
-    shared = lax.dynamic_slice_in_dim(own_out, group * third, third, 1)
-    out_block = jnp.stack([shared, own_out[:, 2 * third :]])
+    a2, b2, x1, send2 = together(
+        move(a1, AHEAD), move(b1, BACK), across(send1), packs=([shared(0), shared(1)],)
+    )
     cut = depth // 2
-    out_held, out_far = gather_ring(out_block, lambda a, b: (a[:, :cut], b[:, cut:]))
-    ring_blocks = out_held[1:] + list(out_far)
-    side_blocks = [across(b[0]) for b in ring_blocks]
-    sources = [own_out, *ring_blocks, *side_blocks]
-    sources += [move(b, SIBLING) for b in sources]
-    step = len(sources) // CORES
-    plan = []
-    for c in range(CORES):
-        at = c * step
-        columns_of = lambda t: (slice(None), pl.ds(t * third, third))
-        plan.append([(at, columns_of(t), t, 0, depth) for t in range(3)])
-        for n in range(CHIPS - 2):
-            ring_at, side_at = at + 1 + n, at + 1 + CHIPS + n
-            plan.append(
-                [(ring_at, 0, 0, 0, depth), (ring_at, 1, 1, 0, depth), (side_at, None, 2, 0, depth)]
-            )
-        far = []
-        for n in range(2):
-            ring_at, side_at = at + CHIPS - 1 + n, at + 2 * CHIPS - 1 + n
-            far += [
-                (ring_at, 0, 0, n * cut, cut),
-                (ring_at, 1, 1, n * cut, cut),
-                (side_at, None, 2, n * cut, cut),
-            ]
-        plan.append(far)
-
-    attended = attend(span_map[0], order, mine, other, new_kv, recompute_idx[0], payloads)
-    attn_out = project_output(order, group_arr, attended, plan, sources, depth, third)
-    return (cache, attn_out)
+    a3, b3, x2, other, send3, to_ahead, to_back = together(
+        move(a2, AHEAD),
+        move(b2, BACK),
+        across(send2),
+        across(theirs_part),
+        packs=(
+            [shared(0), shared(1)],
+            [(0, 0, cut), (0, depth, cut)],
+            [(1, cut, cut), (1, depth + cut, cut)],
+        ),
+    )
+    attended = attend(span_map[0], facts, mine, other, new_kv, recompute_idx, payloads)
+    attended = (attended, *swap(attended))
+
+    def near(slot, block, side, first):
+        return slot, [
+            [(block, 0, 0, 0, depth)],
+            [(block, depth, 0, 0, depth)],
+            [(side, first * depth, 0, 0, depth)],
+        ]
+
+    early = [
+        (0, [[(own_out, 0, n * third, 0, depth)] for n in range(3)]),
+        near(1, a1, x1, 0),
+        near(2, b1, x1, 1),
+        near(3, a2, x2, 0),
+        near(4, b2, x2, 1),
+    ]
+    width_out = CHIPS * CORES * columns
+    result, sent1 = project_output(facts, attended, None, early, [], width_out)
+    a4, b4, x3, sent1 = lax.optimization_barrier(
+        (move(to_ahead, AHEAD), move(to_back, BACK), across(send3), sent1)
+    )
+    a4, b4, x3, send4 = together(a4, b4, x3, packs=([(0, 0, cut), (1, 0, cut)],))
+    late = [near(5, a3, x3, 0), near(6, b3, x3, 1)]
+    result, sent2 = project_output(facts, attended, result, late, [], width_out)
+    x4, arrived1, sent2 = lax.optimization_barrier((across(send4), *swap(sent1), sent2))
+    last = [
+        (
+            7,
+            [
+                [(a4, 0, 0, 0, cut), (b4, 0, 0, cut, cut)],
+                [(a4, cut, 0, 0, cut), (b4, cut, 0, cut, cut)],
+                [(x4, 0, 0, 0, depth)],
+            ],
+        )
+    ]
+    arrived = [(arrived1, (0, 1, 2, 3, 4))]
+    result, sent3 = project_output(facts, attended, result, last, arrived, width_out)
+    arrived = [(swap(sent2)[0], (5, 6)), (swap(sent3)[0], (7,))]
+    return (cache, place_output(facts, arrived, result))
 
 
 def solution(mesh):

time: 309 us -> 238 us (0.77)
  waiting for transfers between devices: 188 us -> 136 us
  local copies, waits for them, and re-layouts: 29.4 us -> 8.64 us
  Pallas kernels: 40.1 us -> 47.8 us
  starting transfers between devices: 34.9 us -> 29.3 us
    ppermute x42 -> x29, waiting for transfers between devices: 99.8 us -> 57.5 us  [move(): return lax.ppermute(block, 'serve', pairs)]
    ppermute x10 -> x8, waiting for transfers between devices: 88.5 us -> 78.6 us  [across(): return lax.ppermute(block, 'groups', ACROSS)]
    unnamed x102 -> x48, local copies, waits for them, and re-layouts: 17.1 us -> 7.94 us
    pallas_call x1 -> x14, Pallas kernels: 16.2 us -> 23.1 us  [the longest x3 16 us: project_output(): pl.pallas_call(partial(output_kernel, plan, arrived), grid_spec=pltpu.Pre...]
    squeeze x8 -> x0, local copies, waits for them, and re-layouts: 6.57 us -> none  [ring_body(): side_blocks = [across(b[0]) for b in ring_blocks]]
    ppermute x42 -> x29, starting transfers between devices: 23.7 us -> 19.9 us  [move(): return lax.ppermute(block, 'serve', pairs)]
    ppermute x10 -> x8, starting transfers between devices: 11.2 us -> 9.42 us  [across(): return lax.ppermute(block, 'groups', ACROSS)]
  transfers between devices with their start and end apart: 53 -> 38, of which waited for: 14 -> 20; matrix products, arithmetic and copies ran while one was open for 4% -> 0% of each run, Pallas kernels for 8% -> 19%
where the time goes in v2:
time: 238 us
  waiting for transfers between devices  136 us (57%)
  Pallas kernels  47.8 us (20%)
  starting transfers between devices  29.3 us (12%)
  between operations  15 us (6%)
  local copies, waits for them, and re-layouts  8.64 us (4%)
    ppermute x8, waiting for transfers between devices, across(): return lax.ppermute(block, 'groups', ACROSS)  78.6 us
    ppermute x29, waiting for transfers between devices, move(): return lax.ppermute(block, 'serve', pairs)  57.5 us
    ppermute x29, starting transfers between devices, move(): return lax.ppermute(block, 'serve', pairs)  19.9 us
    pallas_call x3, Pallas kernels, project_output(): pl.pallas_call(partial(output_kernel, plan, arrived), grid_spec=pltpu.Pre...  16 us
    ppermute x8, starting transfers between devices, across(): return lax.ppermute(block, 'groups', ACROSS)  9.42 us
    pallas_call x1, Pallas kernels, project_query(): pl.pallas_call(query_kernel, grid_spec=pltpu.PrefetchScalarGridSpec(num_s...  8.83 us
    pallas_call x1, Pallas kernels, project_kv(): pl.pallas_call(kv_kernel, grid_spec=pltpu.PrefetchScalarGridSpec(num_scal...  8.59 us
    unnamed x48, local copies, waits for them, and re-layouts  7.94 us
  transfers between devices with their start and end apart: 38, of which 20 were waited for; matrix products, arithmetic and copies ran while one was open for 0% of the time, Pallas kernels for 19%

profile of v2, /device:TPU:0, one launch (start us, length us, event | category | flops | bytes accessed | tf_op | source)
XLA Modules:
  0.0 237.7 jit_solution(9371849331611398479)
XLA Ops:
  7.9 0.7 dynamic-slice_bitcast_fusion
  8.6 0.7 pad_add_fusion.facts
  9.3 1.7 take_parts.2.refs_2_.refs_0_
  11.0 0.5 collective-permute-start.3
  11.6 2.6 %collective-permute-start.1 = (bf16[80,6144]{1,0:T(8,128)(2,1)S(1)}, bf16[80,6144]{1,0:T(8,128)(2,1)S(1)}, u32[]{:S(2)}, u32[]{:S(2)}) collective-permute-start(bf16[80,6144]{1,0:T(8,128)(2,1)S(1)} %take_parts.2.refs_2_.refs_0_), channel_id=1, source_target_pairs={{0,2},{1,3},{4,0},{5,1},{8,4},{9,5},{12,8},{13,9},{14,12},{15,13},... | collective-permute-start | bytes 2949128 | tf_op jit(solution)/shard_map/ppermute | solution.py:234
  14.3 2.6 %take_parts.3 = (bf16[80,6144]{1,0:T(8,128)(2,1)S(1)}, bf16[80,6144]{1,0:T(8,128)(2,1)S(1)}, bf16[80,6144]{1,0:T(8,128)(2,1)S(1)}, bf16[1536,256]{1,0:T(8,128)(2,1)S(1)}) custom-call(s32[34]{0:T(128)S(1)} %pad_add_fusion.facts, bf16[240,12288]{1,0:T(8,128)(2,1)} %bitcast.22, bf16[768,768]{1,0:T(8,128)(2,1)} %bitcast.13, bf16[80,6144]{1,0:T(8,128)(2,1)} %copy-done), custom_call_target="tpu_custom_call" | custom-call | tf_op jit(solution)/shard_map/take_parts/pallas_call | solution.py:218
  16.9 1.9 collective-permute-start.2
  19.0 17.6 %collective-permute-done.1.refs_1_ = bf16[80,6144]{1,0:T(8,128)(2,1)S(1)} collective-permute-done((bf16[80,6144]{1,0:T(8,128)(2,1)S(1)}, bf16[80,6144]{1,0:T(8,128)(2,1)S(1)}, u32[]{:S(2)}, u32[]{:S(2)}) %collective-permute-start.1) | collective-permute-done | bytes 983072 | tf_op jit(solution)/shard_map/ppermute | solution.py:234
  36.6 1.4 collective-permute-done.refs_0_
  38.0 3.6 %collective-permute-done.2.refs_2_ = bf16[80,6144]{1,0:T(8,128)(2,1)S(1)} collective-permute-done((bf16[80,6144]{1,0:T(8,128)(2,1)S(1)}, bf16[80,6144]{1,0:T(8,128)(2,1)S(1)}, u32[]{:S(2)}, u32[]{:S(2)}) %collective-permute-start.2) | collective-permute-done | bytes 983072 | tf_op jit(solution)/shard_map/ppermute | solution.py:238
  41.6 2.0 collective-permute-start.4
  44.0 17.8 %collective-permute-done.6.refs_2_ = bf16[80,6144]{1,0:T(8,128)(2,1)S(1)} collective-permute-done((bf16[80,6144]{1,0:T(8,128)(2,1)S(1)}, bf16[80,6144]{1,0:T(8,128)(2,1)S(1)}, u32[]{:S(2)}, u32[]{:S(2)}) %collective-permute-start.6) | collective-permute-done | bytes 983072 | tf_op jit(solution)/shard_map/ppermute | solution.py:238
  61.8 1.7 collective-permute-start.11
  63.4 2.5 %collective-permute-done.4.refs_0_ = bf16[80,6144]{1,0:T(8,128)(2,1)S(1)} collective-permute-done((bf16[80,6144]{1,0:T(8,128)(2,1)S(1)}, bf16[80,6144]{1,0:T(8,128)(2,1)S(1)}, u32[]{:S(2)}, u32[]{:S(2)}) %collective-permute-start.4) | collective-permute-done | bytes 983072 | tf_op jit(solution)/shard_map/ppermute | solution.py:234
  65.9 1.8 collective-permute-done.5.refs_1_
  67.7 1.6 collective-permute-start.9
  70.0 14.7 %collective-permute-done.11.refs_2_ = bf16[80,6144]{1,0:T(8,128)(2,1)S(1)} collective-permute-done((bf16[80,6144]{1,0:T(8,128)(2,1)S(1)}, bf16[80,6144]{1,0:T(8,128)(2,1)S(1)}, u32[]{:S(2)}, u32[]{:S(2)}) %collective-permute-start.11) | collective-permute-done | bytes 983072 | tf_op jit(solution)/shard_map/ppermute | solution.py:238
  84.7 7.2 %collective-permute-done.9.refs_0_ = bf16[80,6144]{1,0:T(8,128)(2,1)S(1)} collective-permute-done((bf16[80,6144]{1,0:T(8,128)(2,1)S(1)}, bf16[80,6144]{1,0:T(8,128)(2,1)S(1)}, u32[]{:S(2)}, u32[]{:S(2)}) %collective-permute-start.9) | collective-permute-done | bytes 983072 | tf_op jit(solution)/shard_map/ppermute | solution.py:234
  91.9 1.6 collective-permute-done.10.refs_1_
  93.6 0.5 collective-permute-start.17
  94.1 1.6 collective-permute-start.14
  95.7 0.4 collective-permute-start.15
  96.1 10.4 %collective-permute-done.15.refs_1_ = bf16[32,6144]{1,0:T(8,128)(2,1)S(1)} collective-permute-done((bf16[32,6144]{1,0:T(8,128)(2,1)S(1)}, bf16[32,6144]{1,0:T(8,128)(2,1)S(1)}, u32[]{:S(2)}, u32[]{:S(2)}) %collective-permute-start.15) | collective-permute-done | bytes 393248 | tf_op jit(solution)/shard_map/ppermute | solution.py:234
  106.5 2.9 %collective-permute-done.14.refs_0_ = bf16[48,6144]{1,0:T(8,128)(2,1)S(1)} collective-permute-done((bf16[48,6144]{1,0:T(8,128)(2,1)S(1)}, bf16[48,6144]{1,0:T(8,128)(2,1)S(1)}, u32[]{:S(2)}, u32[]{:S(2)}) %collective-permute-start.14) | collective-permute-done | bytes 589856 | tf_op jit(solution)/shard_map/ppermute | solution.py:234
  109.5 0.5 collective-permute-start.21
  110.4 1.6 collective-permute-start.19
  112.0 8.6 %project_kv.1 = (bf16[272,256]{1,0:T(8,128)(2,1)}, bf16[240,256]{1,0:T(8,128)(2,1)S(1)}, bf16[16,16,256]{2,1,0:T(8,128)(2,1)}) custom-call(s32[34]{0:T(128)S(1)} %pad_add_fusion.facts, bf16[1,256,12288]{2,1,0:T(8,128)(2,1)} %span_ref.1, bf16[1,240,12288]{2,1,0:T(8,128)(2,1)} %mine_ref.1, bf16[80,6144]{1,0:T(8,128)(2,1)S(1)} %copy-done.1, ...), custom_call_target="tpu_custom_call" | custom-call | flops 3120562176 | bytes 18481152 | tf_op jit(solution)/shard_map/project_kv/pallas_call | solution.py:303
  120.6 8.8 %project_query.1 = (f32[240,768]{1,0:T(8,128)S(1)}, bf16[240,768]{1,0:T(8,128)(2,1)S(1)}) custom-call(s32[34]{0:T(128)S(1)} %pad_add_fusion.facts, bf16[1,240,12288]{2,1,0:T(8,128)(2,1)} %mine_ref.1, bf16[80,6144]{1,0:T(8,128)(2,1)S(1)} %copy-done.1, bf16[80,6144]{1,0:T(8,128)(2,1)S(1)} %get-tuple-element.68.refs_1_, ...), custom_call_target="tpu_custom_call" | custom-call | flops 4529848320 | bytes 15335424 | tf_op jit(solution)/shard_map/project_query/pallas_call | solution.py:374
  129.5 0.9 copy-done.13
  130.4 0.7 copy-done.23
  131.2 1.6 collective-permute-start.24
  132.7 1.6 collective-permute-start.22
  134.3 0.5 collective-permute-start.23
  134.8 15.4 %collective-permute-done.24.refs_2_ = bf16[1536,256]{1,0:T(8,128)(2,1)S(1)} collective-permute-done((bf16[1536,256]{1,0:T(8,128)(2,1)S(1)}, bf16[1536,256]{1,0:T(8,128)(2,1)S(1)}, u32[]{:S(2)}, u32[]{:S(2)}) %collective-permute-start.24) | collective-permute-done | bytes 786464 | tf_op jit(solution)/shard_map/ppermute | solution.py:238
  150.2 4.8 %collective-permute-done.22.refs_0_ = bf16[1536,256]{1,0:T(8,128)(2,1)S(1)} collective-permute-done((bf16[1536,256]{1,0:T(8,128)(2,1)S(1)}, bf16[1536,256]{1,0:T(8,128)(2,1)S(1)}, u32[]{:S(2)}, u32[]{:S(2)}) %collective-permute-start.22) | collective-permute-done | bytes 786464 | tf_op jit(solution)/shard_map/ppermute | solution.py:234
  155.0 2.2 collective-permute-done.23.refs_1_
  157.3 0.9 copy-done.7
  158.2 0.5 collective-permute-start.27
  158.7 1.5 collective-permute-start.25
  160.2 0.5 collective-permute-start.26
  160.7 0.9 copy-done.11
  161.6 1.5 collective-permute-start.28
  163.1 20.4 %collective-permute-done.28.refs_3_ = bf16[240,768]{1,0:T(8,128)(2,1)S(1)} collective-permute-done((bf16[240,768]{1,0:T(8,128)(2,1)}, bf16[240,768]{1,0:T(8,128)(2,1)S(1)}, u32[]{:S(2)}, u32[]{:S(2)}) %collective-permute-start.28) | collective-permute-done | bytes 368672 | tf_op jit(solution)/shard_map/ppermute | solution.py:238
  183.5 1.9 collective-permute-done.26.refs_1_
  185.5 1.0 together.14
  186.4 0.9 copy-done.5
  187.4 0.8 copy-done.19
  188.2 0.8 copy-done.21
  189.0 1.5 collective-permute-start.31
  190.4 1.1 copy-done.14
  191.6 0.9 copy-done.16
  192.5 7.3 %attend.1.att_ref = bf16[240,768]{1,0:T(8,128)(2,1)S(1)} custom-call(s32[6]{0:T(128)S(1)} %bitcast.15, s32[34]{0:T(128)S(1)} %pad_add_fusion.facts, f32[240,768]{1,0:T(8,128)S(1)} %copy-done.14, bf16[240,768]{1,0:T(8,128)(2,1)S(1)} %get-tuple-element.108.other_ref, bf16[240,256]{1,0:T(8,128)(2,1)S(1)} %copy-done.16, s32[1,240]{1,0:T(1,128)S(1)} %copy-done.17, ...), custom_call_target="tpu_custom_call" | custom-call | flops 1321205760 | bytes 2392064 | tf_op jit(solution)/shard_map/attend/pallas_call | solution.py:461
  199.9 1.3 collective-permute-start.29
  201.1 0.8 collective-permute-start.30
  202.0 8.3 %project_output.3 = (bf16[1,240,12288]{2,1,0:T(8,128)(2,1)}, bf16[5,3,240,256]{3,2,1,0:T(8,128)(2,1)S(1)}) custom-call(s32[34]{0:T(128)S(1)} %pad_add_fusion.facts, bf16[240,768]{1,0:T(8,128)(2,1)S(1)} %attend.1.att_ref, bf16[240,768]{1,0:T(8,128)(2,1)S(1)} %collective-permute-done.32.att2_ref, bf16[768,768]{1,0:T(8,128)(2,1)S(1)} %bitcast.14, ...), custom_call_target="tpu_custom_call" | custom-call | flops 2831155200 | bytes 7741440 | tf_op jit(solution)/shard_map/project_output/pallas_call | solution.py:594
  210.3 1.0 collective-permute-done.29.refs_0_
  211.4 0.9 collective-permute-done.30.refs_1_
  212.3 0.6 collective-permute-start.33
  213.0 4.3 %project_output.4 = (bf16[1,240,12288]{2,1,0:T(8,128)(2,1)}, bf16[2,3,240,256]{3,2,1,0:T(8,128)(2,1)S(1)}) custom-call(s32[34]{0:T(128)S(1)} %pad_add_fusion.facts, bf16[240,768]{1,0:T(8,128)(2,1)S(1)} %attend.1.att_ref, bf16[240,768]{1,0:T(8,128)(2,1)S(1)} %collective-permute-done.32.att2_ref, ...), custom_call_target="tpu_custom_call", output_to_operand_aliasing={{0}: (6, {})} | custom-call | flops 1132462080 | bytes 3096576 | tf_op jit(solution)/shard_map/project_output/pallas_call | solution.py:594
  217.3 6.7 %collective-permute-done.33.refs_2_ = bf16[768,256]{1,0:T(8,128)(2,1)S(1)} collective-permute-done((bf16[768,256]{1,0:T(8,128)(2,1)S(1)}, bf16[768,256]{1,0:T(8,128)(2,1)S(1)}, u32[]{:S(2)}, u32[]{:S(2)}) %collective-permute-start.33) | collective-permute-done | bytes 393248 | tf_op jit(solution)/shard_map/ppermute | solution.py:238
  223.9 3.4 %project_output.5 = (bf16[1,240,12288]{2,1,0:T(8,128)(2,1)}, bf16[1,3,240,256]{3,2,1,0:T(8,128)(2,1)S(1)}) custom-call(s32[34]{0:T(128)S(1)} %pad_add_fusion.facts, bf16[240,768]{1,0:T(8,128)(2,1)S(1)} %attend.1.att_ref, bf16[240,768]{1,0:T(8,128)(2,1)S(1)} %collective-permute-done.32.att2_ref, ...), custom_call_target="tpu_custom_call", output_to_operand_aliasing={{0}: (7, {})} | custom-call | flops 566231040 | bytes 1548288 | tf_op jit(solution)/shard_map/project_output/pallas_call | solution.py:594
  227.3 0.6 collective-permute-start.36
  227.9 1.3 collective-permute-done.36.refs_1_
  229.2 1.6 place_output.1
  (80 shorter events, 2.5 us)
Async XLA Ops:
  7.2 183.3 %all-gather.3.cloned.1.call-start = ((), (), s32[]{:S(2)}) async-start(), calls=%async_computation | async-start | bytes 2367488 | tf_op jit(solution)/shard_map/all_gather | solution.py:697
  11.0 3.3 %copy-start = (bf16[80,6144]{1,0:T(8,128)(2,1)}, bf16[80,6144]{1,0:T(8,128)(2,1)S(1)}, u32[]{:S(2)}) copy-start(bf16[80,6144]{1,0:T(8,128)(2,1)S(1)} %take_parts.2.refs_2_.refs_0_) | copy-start | bytes 2949124
  11.0 7.9 %collective-permute-start.3 = (bf16[80,6144]{1,0:T(8,128)(2,1)S(1)}, bf16[80,6144]{1,0:T(8,128)(2,1)S(1)}, u32[]{:S(2)}, u32[]{:S(2)}) collective-permute-start(bf16[80,6144]{1,0:T(8,128)(2,1)S(1)} %take_parts.2.refs_2_.refs_0_), channel_id=1, source_target_pairs={{0,1},{1,0},{2,3},{3,2},{4,5},{5,4},{6,7},{7,6},{8,9},{9,8},{10,11... | collective-permute-start | bytes 2949128 | tf_op jit(solution)/shard_map/ppermute | solution.py:234
  11.6 25.0 %collective-permute-start.1 = (bf16[80,6144]{1,0:T(8,128)(2,1)S(1)}, bf16[80,6144]{1,0:T(8,128)(2,1)S(1)}, u32[]{:S(2)}, u32[]{:S(2)}) collective-permute-start(bf16[80,6144]{1,0:T(8,128)(2,1)S(1)} %take_parts.2.refs_2_.refs_0_), channel_id=1, source_target_pairs={{0,2},{1,3},{4,0},{5,1},{8,4},{9,5},{12,8},{13,9},{14,12},{15,13},... | collective-permute-start | bytes 2949128 | tf_op jit(solution)/shard_map/ppermute | solution.py:234
  14.1 23.8 %collective-permute-start = (bf16[80,6144]{1,0:T(8,128)(2,1)S(1)}, bf16[80,6144]{1,0:T(8,128)(2,1)S(1)}, u32[]{:S(2)}, u32[]{:S(2)}) collective-permute-start(bf16[80,6144]{1,0:T(8,128)(2,1)S(1)} %take_parts.2.refs_2_.refs_0_), channel_id=1, source_target_pairs={{0,4},{1,5},{4,8},{5,9},{8,12},{9,13},{12,14},{13,15},{14,10},{15,... | collective-permute-start | bytes 2949128 | tf_op jit(solution)/shard_map/ppermute | solution.py:234
  16.9 24.7 %collective-permute-start.2 = (bf16[80,6144]{1,0:T(8,128)(2,1)S(1)}, bf16[80,6144]{1,0:T(8,128)(2,1)S(1)}, u32[]{:S(2)}, u32[]{:S(2)}) collective-permute-start(bf16[80,6144]{1,0:T(8,128)(2,1)S(1)} %get-tuple-element.67), channel_id=1, source_target_pairs={{0,16},{16,0},{1,17},{17,1},{2,18},{18,2},{3,19},{19,3},{4,20},{20... | collective-permute-start | bytes 2949128 | tf_op jit(solution)/shard_map/ppermute | solution.py:238
  18.8 43.0 %collective-permute-start.6 = (bf16[80,6144]{1,0:T(8,128)(2,1)S(1)}, bf16[80,6144]{1,0:T(8,128)(2,1)S(1)}, u32[]{:S(2)}, u32[]{:S(2)}) collective-permute-start(bf16[80,6144]{1,0:T(8,128)(2,1)S(1)} %get-tuple-element.70), channel_id=1, source_target_pairs={{0,16},{16,0},{1,17},{17,1},{2,18},{18,2},{3,19},{19,3},{4,20},{20... | collective-permute-start | bytes 2949128 | tf_op jit(solution)/shard_map/ppermute | solution.py:238
  41.6 21.9 %collective-permute-start.7 = (bf16[80,6144]{1,0:T(8,128)(2,1)S(1)}, bf16[80,6144]{1,0:T(8,128)(2,1)S(1)}, u32[]{:S(2)}, u32[]{:S(2)}) collective-permute-start(bf16[80,6144]{1,0:T(8,128)(2,1)S(1)} %get-tuple-element.68.refs_1_), channel_id=1, source_target_pairs={{0,1},{1,0},{2,3},{3,2},{4,5},{5,4},{6,7},{7,6},{8,9},{9,8},{10,11... | collective-permute-start | bytes 2949128 | tf_op jit(solution)/shard_map/ppermute | solution.py:234
  41.6 24.3 %collective-permute-start.4 = (bf16[80,6144]{1,0:T(8,128)(2,1)S(1)}, bf16[80,6144]{1,0:T(8,128)(2,1)S(1)}, u32[]{:S(2)}, u32[]{:S(2)}) collective-permute-start(bf16[80,6144]{1,0:T(8,128)(2,1)S(1)} %get-tuple-element.68.refs_1_), channel_id=1, source_target_pairs={{0,4},{1,5},{4,8},{5,9},{8,12},{9,13},{12,14},{13,15},{14,10},{15,... | collective-permute-start | bytes 2949128 | tf_op jit(solution)/shard_map/ppermute | solution.py:234
  43.5 22.4 %collective-permute-start.8 = (bf16[80,6144]{1,0:T(8,128)(2,1)S(1)}, bf16[80,6144]{1,0:T(8,128)(2,1)S(1)}, u32[]{:S(2)}, u32[]{:S(2)}) collective-permute-start(bf16[80,6144]{1,0:T(8,128)(2,1)S(1)} %get-tuple-element.69.refs_2_), channel_id=1, source_target_pairs={{0,1},{1,0},{2,3},{3,2},{4,5},{5,4},{6,7},{7,6},{8,9},{9,8},{10,11... | collective-permute-start | bytes 2949128 | tf_op jit(solution)/shard_map/ppermute | solution.py:234
  43.8 23.9 %collective-permute-start.5 = (bf16[80,6144]{1,0:T(8,128)(2,1)S(1)}, bf16[80,6144]{1,0:T(8,128)(2,1)S(1)}, u32[]{:S(2)}, u32[]{:S(2)}) collective-permute-start(bf16[80,6144]{1,0:T(8,128)(2,1)S(1)} %get-tuple-element.69.refs_2_), channel_id=1, source_target_pairs={{0,2},{1,3},{4,0},{5,1},{8,4},{9,5},{12,8},{13,9},{14,12},{15,13},... | collective-permute-start | bytes 2949128 | tf_op jit(solution)/shard_map/ppermute | solution.py:234
  61.8 50.3 %copy-start.1 = (bf16[80,6144]{1,0:T(8,128)(2,1)S(1)}, bf16[80,6144]{1,0:T(8,128)(2,1)}, u32[]{:S(2)}) copy-start(bf16[80,6144]{1,0:T(8,128)(2,1)} %copy-done) | copy-start | bytes 2949124
  61.8 22.9 %collective-permute-start.11 = (bf16[80,6144]{1,0:T(8,128)(2,1)S(1)}, bf16[80,6144]{1,0:T(8,128)(2,1)S(1)}, u32[]{:S(2)}, u32[]{:S(2)}) collective-permute-start(bf16[80,6144]{1,0:T(8,128)(2,1)S(1)} %get-tuple-element.73), channel_id=1, source_target_pairs={{0,16},{16,0},{1,17},{17,1},{2,18},{18,2},{3,19},{19,3},{4,20},{20... | collective-permute-start | bytes 2949128 | tf_op jit(solution)/shard_map/ppermute | solution.py:238
  67.7 17.0 %collective-permute-start.12 = (bf16[80,6144]{1,0:T(8,128)(2,1)S(1)}, bf16[80,6144]{1,0:T(8,128)(2,1)S(1)}, u32[]{:S(2)}, u32[]{:S(2)}) collective-permute-start(bf16[80,6144]{1,0:T(8,128)(2,1)S(1)} %get-tuple-element.71.refs_3_), channel_id=1, source_target_pairs={{0,1},{1,0},{2,3},{3,2},{4,5},{5,4},{6,7},{7,6},{8,9},{9,8},{10,11... | collective-permute-start | bytes 2949128 | tf_op jit(solution)/shard_map/ppermute | solution.py:234
  67.7 24.2 %collective-permute-start.9 = (bf16[80,6144]{1,0:T(8,128)(2,1)S(1)}, bf16[80,6144]{1,0:T(8,128)(2,1)S(1)}, u32[]{:S(2)}, u32[]{:S(2)}) collective-permute-start(bf16[80,6144]{1,0:T(8,128)(2,1)S(1)} %get-tuple-element.71.refs_3_), channel_id=1, source_target_pairs={{0,4},{1,5},{4,8},{5,9},{8,12},{9,13},{12,14},{13,15},{14,10},{15,... | collective-permute-start | bytes 2949128 | tf_op jit(solution)/shard_map/ppermute | solution.py:234
  69.3 22.6 %collective-permute-start.13 = (bf16[80,6144]{1,0:T(8,128)(2,1)S(1)}, bf16[80,6144]{1,0:T(8,128)(2,1)S(1)}, u32[]{:S(2)}, u32[]{:S(2)}) collective-permute-start(bf16[80,6144]{1,0:T(8,128)(2,1)S(1)} %get-tuple-element.72.refs_4_), channel_id=1, source_target_pairs={{0,1},{1,0},{2,3},{3,2},{4,5},{5,4},{6,7},{7,6},{8,9},{9,8},{10,11... | collective-permute-start | bytes 2949128 | tf_op jit(solution)/shard_map/ppermute | solution.py:234
  69.5 23.9 %collective-permute-start.10 = (bf16[80,6144]{1,0:T(8,128)(2,1)S(1)}, bf16[80,6144]{1,0:T(8,128)(2,1)S(1)}, u32[]{:S(2)}, u32[]{:S(2)}) collective-permute-start(bf16[80,6144]{1,0:T(8,128)(2,1)S(1)} %get-tuple-element.72.refs_4_), channel_id=1, source_target_pairs={{0,2},{1,3},{4,0},{5,1},{8,4},{9,5},{12,8},{13,9},{14,12},{15,13},... | collective-permute-start | bytes 2949128 | tf_op jit(solution)/shard_map/ppermute | solution.py:234
  93.5 15.9 %collective-permute-start.16 = (bf16[80,6144]{1,0:T(8,128)(2,1)S(1)}, bf16[80,6144]{1,0:T(8,128)(2,1)S(1)}, u32[]{:S(2)}, u32[]{:S(2)}) collective-permute-start(bf16[80,6144]{1,0:T(8,128)(2,1)S(1)} %get-tuple-element.74.refs_5_), channel_id=1, source_target_pairs={{0,1},{1,0},{2,3},{3,2},{4,5},{5,4},{6,7},{7,6},{8,9},{9,8},{10,11... | collective-permute-start | bytes 2949128 | tf_op jit(solution)/shard_map/ppermute | solution.py:234
  93.6 15.8 %collective-permute-start.17 = (bf16[80,6144]{1,0:T(8,128)(2,1)S(1)}, bf16[80,6144]{1,0:T(8,128)(2,1)S(1)}, u32[]{:S(2)}, u32[]{:S(2)}) collective-permute-start(bf16[80,6144]{1,0:T(8,128)(2,1)S(1)} %get-tuple-element.75.refs_6_), channel_id=1, source_target_pairs={{0,1},{1,0},{2,3},{3,2},{4,5},{5,4},{6,7},{7,6},{8,9},{9,8},{10,11... | collective-permute-start | bytes 2949128 | tf_op jit(solution)/shard_map/ppermute | solution.py:234
  94.1 15.3 %collective-permute-start.14 = (bf16[48,6144]{1,0:T(8,128)(2,1)S(1)}, bf16[48,6144]{1,0:T(8,128)(2,1)S(1)}, u32[]{:S(2)}, u32[]{:S(2)}) collective-permute-start(bf16[48,6144]{1,0:T(8,128)(2,1)S(1)} %get-tuple-element.76), channel_id=1, source_target_pairs={{0,4},{1,5},{4,8},{5,9},{8,12},{9,13},{12,14},{13,15},{14,10},{15,... | collective-permute-start | bytes 1769480 | tf_op jit(solution)/shard_map/ppermute | solution.py:234
  95.7 10.8 %collective-permute-start.15 = (bf16[32,6144]{1,0:T(8,128)(2,1)S(1)}, bf16[32,6144]{1,0:T(8,128)(2,1)S(1)}, u32[]{:S(2)}, u32[]{:S(2)}) collective-permute-start(bf16[32,6144]{1,0:T(8,128)(2,1)S(1)} %get-tuple-element.77), channel_id=1, source_target_pairs={{0,2},{1,3},{4,0},{5,1},{8,4},{9,5},{12,8},{13,9},{14,12},{15,13},... | collective-permute-start | bytes 1179656 | tf_op jit(solution)/shard_map/ppermute | solution.py:234
  109.4 2.6 %collective-permute-start.18 = (bf16[32,6144]{1,0:T(8,128)(2,1)S(1)}, bf16[32,6144]{1,0:T(8,128)(2,1)S(1)}, u32[]{:S(2)}, u32[]{:S(2)}) collective-permute-start(bf16[32,6144]{1,0:T(8,128)(2,1)S(1)} %get-tuple-element.79.refs_7_), channel_id=1, source_target_pairs={{0,1},{1,0},{2,3},{3,2},{4,5},{5,4},{6,7},{7,6},{8,9},{9,8},{10,11... | collective-permute-start | bytes 1179656 | tf_op jit(solution)/shard_map/ppermute | solution.py:234
  109.5 11.1 %collective-permute-start.21 = (bf16[48,6144]{1,0:T(8,128)(2,1)S(1)}, bf16[48,6144]{1,0:T(8,128)(2,1)S(1)}, u32[]{:S(2)}, u32[]{:S(2)}) collective-permute-start(bf16[48,6144]{1,0:T(8,128)(2,1)S(1)} %get-tuple-element.90.refs_7_), channel_id=1, source_target_pairs={{0,1},{1,0},{2,3},{3,2},{4,5},{5,4},{6,7},{7,6},{8,9},{9,8},{10,11... | collective-permute-start | bytes 1769480 | tf_op jit(solution)/shard_map/ppermute | solution.py:234
  110.0 20.4 %collective-permute-start.20 = (bf16[1536,256]{1,0:T(8,128)(2,1)S(1)}, bf16[1536,256]{1,0:T(8,128)(2,1)S(1)}, u32[]{:S(2)}, u32[]{:S(2)}) collective-permute-start(bf16[1536,256]{1,0:T(8,128)(2,1)S(1)} %get-tuple-element.88), channel_id=1, source_target_pairs={{0,2},{1,3},{4,0},{5,1},{8,4},{9,5},{12,8},{13,9},{14,12},{15,13},... | collective-permute-start | bytes 2359304 | tf_op jit(solution)/shard_map/ppermute | solution.py:234
  110.4 19.9 %collective-permute-start.19 = (bf16[1536,256]{1,0:T(8,128)(2,1)S(1)}, bf16[1536,256]{1,0:T(8,128)(2,1)S(1)}, u32[]{:S(2)}, u32[]{:S(2)}) collective-permute-start(bf16[1536,256]{1,0:T(8,128)(2,1)S(1)} %get-tuple-element.88), channel_id=1, source_target_pairs={{0,4},{1,5},{4,8},{5,9},{8,12},{9,13},{12,14},{13,15},{14,10},{15,... | collective-permute-start | bytes 2359304 | tf_op jit(solution)/shard_map/ppermute | solution.py:234
  120.6 8.8 %copy-start.15 = (bf16[240,256]{1,0:T(8,128)(2,1)}, bf16[240,256]{1,0:T(8,128)(2,1)S(1)}, u32[]{:S(2)}) copy-start(bf16[240,256]{1,0:T(8,128)(2,1)S(1)} %get-tuple-element.109.new_ref) | copy-start | bytes 368644
  129.5 0.9 copy-start.13
  130.3 0.7 copy-start.23
  130.3 60.1 %copy-start.17 = (s32[1,240]{1,0:T(1,128)S(1)}, s32[1,240]{1,0:T(1,128)}, u32[]{:S(2)}) copy-start(s32[1,240]{1,0:T(1,128)} %row_ref.1) | copy-start | bytes 2884
  130.3 60.1 %copy-start.18 = (s32[1,6]{1,0:T(1,128)S(1)}, s32[1,6]{1,0:T(1,128)}, u32[]{:S(2)}) copy-start(s32[1,6]{1,0:T(1,128)} %param.15) | copy-start | bytes 76
  131.2 55.3 %copy-start.3 = (bf16[1536,256]{1,0:T(8,128)(2,1)}, bf16[1536,256]{1,0:T(8,128)(2,1)S(1)}, u32[]{:S(2)}) copy-start(bf16[1536,256]{1,0:T(8,128)(2,1)S(1)} %get-tuple-element.97.refs_1_) | copy-start | bytes 2359300
  131.2 19.0 %collective-permute-start.24 = (bf16[1536,256]{1,0:T(8,128)(2,1)S(1)}, bf16[1536,256]{1,0:T(8,128)(2,1)S(1)}, u32[]{:S(2)}, u32[]{:S(2)}) collective-permute-start(bf16[1536,256]{1,0:T(8,128)(2,1)S(1)} %get-tuple-element.99), channel_id=1, source_target_pairs={{0,16},{16,0},{1,17},{17,1},{2,18},{18,2},{3,19},{19,3},{4,20},{20... | collective-permute-start | bytes 2359304 | tf_op jit(solution)/shard_map/ppermute | solution.py:238
  132.7 22.3 %collective-permute-start.22 = (bf16[1536,256]{1,0:T(8,128)(2,1)S(1)}, bf16[1536,256]{1,0:T(8,128)(2,1)S(1)}, u32[]{:S(2)}, u32[]{:S(2)}) collective-permute-start(bf16[1536,256]{1,0:T(8,128)(2,1)S(1)} %get-tuple-element.97.refs_1_), channel_id=1, source_target_pairs={{0,4},{1,5},{4,8},{5,9},{8,12},{9,13},{12,14},{13,15},{14,10},{15,... | collective-permute-start | bytes 2359304 | tf_op jit(solution)/shard_map/ppermute | solution.py:234
  134.3 22.9 %collective-permute-start.23 = (bf16[1536,256]{1,0:T(8,128)(2,1)S(1)}, bf16[1536,256]{1,0:T(8,128)(2,1)S(1)}, u32[]{:S(2)}, u32[]{:S(2)}) collective-permute-start(bf16[1536,256]{1,0:T(8,128)(2,1)S(1)} %get-tuple-element.98.refs_3_), channel_id=1, source_target_pairs={{0,2},{1,3},{4,0},{5,1},{8,4},{9,5},{12,8},{13,9},{14,12},{15,13},... | collective-permute-start | bytes 2359304 | tf_op jit(solution)/shard_map/ppermute | solution.py:234
  157.3 0.9 copy-start.7
  158.1 30.8 %copy-start.9 = (bf16[1536,256]{1,0:T(8,128)(2,1)}, bf16[1536,256]{1,0:T(8,128)(2,1)S(1)}, u32[]{:S(2)}) copy-start(bf16[1536,256]{1,0:T(8,128)(2,1)S(1)} %get-tuple-element.100.refs_4_) | copy-start | bytes 2359300
  158.2 25.4 %collective-permute-start.27 = (bf16[1536,256]{1,0:T(8,128)(2,1)S(1)}, bf16[1536,256]{1,0:T(8,128)(2,1)S(1)}, u32[]{:S(2)}, u32[]{:S(2)}) collective-permute-start(bf16[1536,256]{1,0:T(8,128)(2,1)S(1)} %get-tuple-element.102), channel_id=1, source_target_pairs={{0,16},{16,0},{1,17},{17,1},{2,18},{18,2},{3,19},{19,3},{4,20},{20... | collective-permute-start | bytes 2359304 | tf_op jit(solution)/shard_map/ppermute | solution.py:238
  158.7 24.9 %collective-permute-start.25 = (bf16[1536,256]{1,0:T(8,128)(2,1)S(1)}, bf16[1536,256]{1,0:T(8,128)(2,1)S(1)}, u32[]{:S(2)}, u32[]{:S(2)}) collective-permute-start(bf16[1536,256]{1,0:T(8,128)(2,1)S(1)} %get-tuple-element.100.refs_4_), channel_id=1, source_target_pairs={{0,4},{1,5},{4,8},{5,9},{8,12},{9,13},{12,14},{13,15},{14,10},{15,... | collective-permute-start | bytes 2359304 | tf_op jit(solution)/shard_map/ppermute | solution.py:234
  160.2 25.2 %collective-permute-start.26 = (bf16[1536,256]{1,0:T(8,128)(2,1)S(1)}, bf16[1536,256]{1,0:T(8,128)(2,1)S(1)}, u32[]{:S(2)}, u32[]{:S(2)}) collective-permute-start(bf16[1536,256]{1,0:T(8,128)(2,1)S(1)} %get-tuple-element.101.refs_6_), channel_id=1, source_target_pairs={{0,2},{1,3},{4,0},{5,1},{8,4},{9,5},{12,8},{13,9},{14,12},{15,13},... | collective-permute-start | bytes 2359304 | tf_op jit(solution)/shard_map/ppermute | solution.py:234
  160.7 0.9 copy-start.11
  161.6 21.9 %collective-permute-start.28 = (bf16[240,768]{1,0:T(8,128)(2,1)}, bf16[240,768]{1,0:T(8,128)(2,1)S(1)}, u32[]{:S(2)}, u32[]{:S(2)}) collective-permute-start(bf16[240,768]{1,0:T(8,128)(2,1)} %copy-done.23), channel_id=1, source_target_pairs={{0,16},{16,0},{1,17},{17,1},{2,18},{18,2},{3,19},{19,3},{4,20},{20... | collective-permute-start | bytes 1105928 | tf_op jit(solution)/shard_map/ppermute | solution.py:238
  186.4 0.9 copy-start.5
  187.4 0.8 copy-start.19
  188.2 0.8 copy-start.21
  189.0 23.4 %collective-permute-start.31 = (bf16[1536,256]{1,0:T(8,128)(2,1)}, bf16[1536,256]{1,0:T(8,128)(2,1)S(1)}, u32[]{:S(2)}, u32[]{:S(2)}) collective-permute-start(bf16[1536,256]{1,0:T(8,128)(2,1)} %get-tuple-element.106), channel_id=1, source_target_pairs={{0,16},{16,0},{1,17},{17,1},{2,18},{18,2},{3,19},{19,3},{4,20},{20... | collective-permute-start | bytes 2359304 | tf_op jit(solution)/shard_map/ppermute | solution.py:238
  190.4 1.1 copy-start.14
  191.5 0.9 copy-start.16
  192.5 7.4 %copy-start.22 = (bf16[768,256]{1,0:T(8,128)(2,1)S(1)}, bf16[768,256]{1,0:T(8,128)(2,1)}, u32[]{:S(2)}) copy-start(bf16[768,256]{1,0:T(8,128)(2,1)} %copy-done.21) | copy-start | bytes 1179652
  192.5 8.7 %copy-start.20 = (bf16[768,256]{1,0:T(8,128)(2,1)S(1)}, bf16[768,256]{1,0:T(8,128)(2,1)}, u32[]{:S(2)}) copy-start(bf16[768,256]{1,0:T(8,128)(2,1)} %copy-done.19) | copy-start | bytes 1179652
  192.5 9.5 %copy-start.2 = (bf16[6,128,1,768]{3,1,2,0:T(8,128)(2,1)S(1)}, bf16[6,128,1,768]{3,1,2,0:T(8,128)(2,1)}, u32[]{:S(2)}) copy-start(bf16[6,128,1,768]{3,1,2,0:T(8,128)(2,1)} %param.14) | copy-start | bytes 3538948
  192.5 9.5 %copy-start.4 = (bf16[1536,256]{1,0:T(8,128)(2,1)S(1)}, bf16[1536,256]{1,0:T(8,128)(2,1)}, u32[]{:S(2)}) copy-start(bf16[1536,256]{1,0:T(8,128)(2,1)} %copy-done.3) | copy-start | bytes 2359300
  192.5 9.5 %copy-start.6 = (bf16[1536,256]{1,0:T(8,128)(2,1)S(1)}, bf16[1536,256]{1,0:T(8,128)(2,1)}, u32[]{:S(2)}) copy-start(bf16[1536,256]{1,0:T(8,128)(2,1)} %copy-done.5) | copy-start | bytes 2359300
  192.5 9.5 %copy-start.8 = (bf16[1536,256]{1,0:T(8,128)(2,1)S(1)}, bf16[1536,256]{1,0:T(8,128)(2,1)}, u32[]{:S(2)}) copy-start(bf16[1536,256]{1,0:T(8,128)(2,1)} %copy-done.7) | copy-start | bytes 2359300
  192.5 9.5 %copy-start.10 = (bf16[1536,256]{1,0:T(8,128)(2,1)S(1)}, bf16[1536,256]{1,0:T(8,128)(2,1)}, u32[]{:S(2)}) copy-start(bf16[1536,256]{1,0:T(8,128)(2,1)} %copy-done.9) | copy-start | bytes 2359300
  192.5 9.5 %copy-start.12 = (bf16[1536,256]{1,0:T(8,128)(2,1)S(1)}, bf16[1536,256]{1,0:T(8,128)(2,1)}, u32[]{:S(2)}) copy-start(bf16[1536,256]{1,0:T(8,128)(2,1)} %copy-done.11) | copy-start | bytes 2359300
  199.8 2.2 collective-permute-start.32
  199.9 11.5 %collective-permute-start.29 = (bf16[768,256]{1,0:T(8,128)(2,1)S(1)}, bf16[768,256]{1,0:T(8,128)(2,1)S(1)}, u32[]{:S(2)}, u32[]{:S(2)}) collective-permute-start(bf16[768,256]{1,0:T(8,128)(2,1)S(1)} %copy-done.22), channel_id=1, source_target_pairs={{0,4},{1,5},{4,8},{5,9},{8,12},{9,13},{12,14},{13,15},{14,10},{15,... | collective-permute-start | bytes 1179656 | tf_op jit(solution)/shard_map/ppermute | solution.py:234
  201.1 11.2 %collective-permute-start.30 = (bf16[768,256]{1,0:T(8,128)(2,1)S(1)}, bf16[768,256]{1,0:T(8,128)(2,1)S(1)}, u32[]{:S(2)}, u32[]{:S(2)}) collective-permute-start(bf16[768,256]{1,0:T(8,128)(2,1)S(1)} %copy-done.20), channel_id=1, source_target_pairs={{0,2},{1,3},{4,0},{5,1},{8,4},{9,5},{12,8},{13,9},{14,12},{15,13},... | collective-permute-start | bytes 1179656 | tf_op jit(solution)/shard_map/ppermute | solution.py:234
  212.3 11.6 %collective-permute-start.34 = (bf16[5,3,240,256]{3,2,1,0:T(8,128)(2,1)S(1)}, bf16[5,3,240,256]{3,2,1,0:T(8,128)(2,1)S(1)}, u32[]{:S(2)}, u32[]{:S(2)}) collective-permute-start(bf16[5,3,240,256]{3,2,1,0:T(8,128)(2,1)S(1)} %get-tuple-element.118), channel_id=1, source_target_pairs={{0,1},{1,0},{2,3},{3,2},{4,5},{5,4},{6,7},{7,6},{8,9},{9,8},{10,11... | collective-permute-start | bytes 5529608 | tf_op jit(solution)/shard_map/ppermute | solution.py:234
  212.3 11.6 %collective-permute-start.33 = (bf16[768,256]{1,0:T(8,128)(2,1)S(1)}, bf16[768,256]{1,0:T(8,128)(2,1)S(1)}, u32[]{:S(2)}, u32[]{:S(2)}) collective-permute-start(bf16[768,256]{1,0:T(8,128)(2,1)S(1)} %get-tuple-element.117), channel_id=1, source_target_pairs={{0,16},{16,0},{1,17},{17,1},{2,18},{18,2},{3,19},{19,3},{4,20},{20... | collective-permute-start | bytes 1179656 | tf_op jit(solution)/shard_map/ppermute | solution.py:238
  223.9 5.3 %collective-permute-start.35 = (bf16[2,3,240,256]{3,2,1,0:T(8,128)(2,1)S(1)}, bf16[2,3,240,256]{3,2,1,0:T(8,128)(2,1)S(1)}, u32[]{:S(2)}, u32[]{:S(2)}) collective-permute-start(bf16[2,3,240,256]{3,2,1,0:T(8,128)(2,1)S(1)} %get-tuple-element.124), channel_id=1, source_target_pairs={{0,1},{1,0},{2,3},{3,2},{4,5},{5,4},{6,7},{7,6},{8,9},{9,8},{10,11... | collective-permute-start | bytes 2211848 | tf_op jit(solution)/shard_map/ppermute | solution.py:234
  227.3 1.9 collective-permute-start.36
Sparse Core Ops, SparseCore 0:
  131.2 48.2 all-gather.2

commit v3 on v2

--- a/solution.py
+++ b/solution.py
@@ -170,17 +170,15 @@
     for pack, out_ref in zip(packs, refs[len(refs) - len(packs) :]):
         at = 0
         for n, first, size in pack:
-            out_ref[at : at + size] = refs[n][first : first + size]
+            out_ref[at : at + size] = refs[n][first : first + size, 0 : out_ref.shape[1]]
             at += size
 
 
 def together(*blocks, packs=()):
-    read = [n for pack in packs for n, first, size in pack]
-    packed = [
-        (sum(size for n, first, size in pack),) + blocks[pack[0][0]].shape[1:] for pack in packs
-    ]
+    read = [n for _, pack in packs for n, first, size in pack]
+    packed = [(sum(size for n, first, size in pack), columns) for columns, pack in packs]
     return pl.pallas_call(
-        partial(hold_kernel, packs),
+        partial(hold_kernel, [pack for _, pack in packs]),
         in_specs=[
             pl.BlockSpec(memory_space=pltpu.VMEM if n in read else pl.ANY) for n in range(len(blocks))
         ],
@@ -189,7 +187,7 @@
         out_shape=[pltpu.VMEM(block.shape, block.dtype) for block in blocks]
         + [pltpu.VMEM(shape, jnp.bfloat16) for shape in packed],
         input_output_aliases={n: n for n in range(len(blocks))},
-        compiler_params=pltpu.CompilerParams(vmem_limit_bytes=2**20),
+        compiler_params=pltpu.CompilerParams(vmem_limit_bytes=6 * 2**20),
         name="together",
     )(*in_vmem(blocks))
 
@@ -198,14 +196,13 @@
     sem = refs[-1]
     group = facts[GROUP]
     copies = []
-    for n, (source, out, row, first, flip, shape) in enumerate(plan):
+    for n, (source, out, row, column, flip, shape) in enumerate(plan):
         side = 1 - group if flip else group
         width = shape[-1]
-        start = first if flip is None else pl.multiple_of(side * width, width)
+        start = column[0] if flip is None else pl.multiple_of(side * width, width)
         view = refs[source].at[pl.ds(row[0], shape[0]), pl.ds(start, width)]
-        copies.append(
-            pltpu.make_async_copy(view, refs[out].at[pl.ds(row[1], shape[0])], sem.at[n])
-        )
+        target = refs[out].at[pl.ds(row[1], shape[0]), pl.ds(column[1], width)]
+        copies.append(pltpu.make_async_copy(view, target, sem.at[n]))
     for copy in copies:
         copy.start()
     for copy in copies:
@@ -250,23 +247,20 @@
     return jnp.concatenate(parts, axis=0).astype(jnp.bfloat16)
 
 
-def kv_kernel(facts, span_ref, req_ref, *refs):
+def kv_kernel(facts, span_ref, req_ref, own_ref, sib_ref, *refs):
     slots = CHIPS * CORES
-    w_refs = refs[:slots]
-    pay_ref, new_ref, cache_ref, span_acc, req_acc = refs[slots:]
+    pay_ref, new_ref, cache_ref, span_acc, req_acc = refs
     step = pl.program_id(0)
-    chunk = span_ref.shape[2]
-    per_half = w_refs[0].shape[1] // chunk
+    chunk = span_ref.shape[2] // pl.num_programs(0)
+    per_half = own_ref.shape[1] // chunk
+    here = pl.ds(pl.multiple_of(step * chunk, chunk), chunk)
     columns = pl.ds(pl.multiple_of(step % per_half * chunk, chunk), chunk)
-    w = jnp.concatenate(
-        [
-            ref[pl.ds(pl.multiple_of(ref.shape[0] - 32 + step // per_half * 16, 16), 16), columns]
-            for ref in w_refs
-        ],
-        axis=0,
-    )
-    span_now = lax.dot_general(span_ref[0], w, NT, preferred_element_type=jnp.float32)
-    req_now = lax.dot_general(req_ref[0], w, NT, preferred_element_type=jnp.float32)
+    size = own_ref.shape[0] // 2
+    found = pl.ds(pl.multiple_of(step // per_half * size, size), size)
+    w = jnp.concatenate([own_ref[found, columns], sib_ref[found, columns]], axis=0)
+    x = jnp.concatenate([span_ref[0, :, here], req_ref[0, :, here]], axis=0)
+    both = lax.dot_general(x, w, NT, preferred_element_type=jnp.float32)
+    span_now, req_now = both[: span_ref.shape[1]], both[span_ref.shape[1] :]
 
     @pl.when(step == 0)
     def _():
@@ -295,20 +289,17 @@
             cache_ref[facts[TABLE + p]] = span_kv[p * PAGE : (p + 1) * PAGE]
 
 
-def project_kv(facts, span_states, recomp_states, w_blocks, last_block):
+def project_kv(facts, span_states, recomp_states, blocks):
     tokens, width = span_states.shape[1:]
     rows = recomp_states.shape[1]
-    chunk = width // 4
-    blocks = w_blocks[: CHIPS - 1] + last_block[:1] + w_blocks[CHIPS - 1 :] + last_block[1:]
+    steps = 4
     return pl.pallas_call(
         kv_kernel,
         grid_spec=pltpu.PrefetchScalarGridSpec(
             num_scalar_prefetch=1,
-            grid=(width // chunk,),
+            grid=(steps,),
             in_specs=[
-                pl.BlockSpec((1, tokens, chunk), lambda k, *_: (0, 0, k)),
-                pl.BlockSpec((1, rows, chunk), lambda k, *_: (0, 0, k)),
-                *([pl.BlockSpec(memory_space=pltpu.VMEM)] * len(blocks)),
+                *([pl.BlockSpec(memory_space=pltpu.VMEM)] * (2 + CORES)),
             ],
             out_specs=[
                 pl.BlockSpec((tokens + PAGE, 2 * HD), lambda k, *_: (0, 0)),
@@ -325,29 +316,23 @@
             jax.ShapeDtypeStruct((rows, 2 * HD), jnp.bfloat16),
             jax.ShapeDtypeStruct((tokens // PAGE, PAGE, 2 * HD), jnp.bfloat16),
         ],
-        cost_estimate=pl.CostEstimate(
-            flops=2 * (tokens + rows) * width * 2 * HD,
-            bytes_accessed=2 * (tokens + rows + 2 * HD) * width,
-            transcendentals=0,
-        ),
+        cost_estimate=pl.CostEstimate(flops=1000, bytes_accessed=1000, transcendentals=0),
         compiler_params=pltpu.CompilerParams(vmem_limit_bytes=16 * 2**20),
         name="project_kv",
-    )(facts, *in_hbm([span_states, recomp_states]), *blocks)
-
-
-def query_kernel(facts, mine_ref, *refs):
-    slots = CHIPS * CORES
-    w_refs = refs[:slots]
-    other_refs = refs[slots:-4]
-    mine_out, other_out, mine_acc, other_acc = refs[-4:]
+    )(facts, span_states, recomp_states, *blocks)
+
+
+def query_kernel(facts, mine_ref, own_ref, sib_ref, other_ref, *refs):
+    mine_out, other_out, mine_acc, other_acc = refs
     step = pl.program_id(0)
-    chunk = mine_ref.shape[2]
-    part = mine_out.shape[1] // slots
+    half = other_ref.shape[1]
+    chunk = half // pl.num_programs(0)
     columns = pl.ds(pl.multiple_of(step * chunk, chunk), chunk)
-    w = jnp.concatenate([ref[0:part, columns] for ref in w_refs], axis=0)
-    mine_now = lax.dot_general(mine_ref[0], w, NT, preferred_element_type=jnp.float32)
-    other = jnp.concatenate([ref[:, columns] for ref in other_refs], axis=0)
-    other_now = lax.dot_general(other, w, NT, preferred_element_type=jnp.float32)
+    here = pl.ds(pl.multiple_of(facts[GROUP] * half + step * chunk, chunk), chunk)
+    w = jnp.concatenate([own_ref[:, columns], sib_ref[:, columns]], axis=0)
+    x = jnp.concatenate([mine_ref[0, :, here], other_ref[:, columns]], axis=0)
+    both = lax.dot_general(x, w, NT, preferred_element_type=jnp.float32)
+    mine_now, other_now = both[: mine_ref.shape[1]], both[mine_ref.shape[1] :]
 
     @pl.when(step == 0)
     def _():
@@ -365,20 +350,17 @@
         other_out[...] = other_acc[...].astype(other_out.dtype)
 
 
-def project_query(facts, recomp_states, other_rows, w_blocks, last_block, columns):
+def project_query(facts, recomp_states, other_rows, blocks, columns):
     rows = recomp_states.shape[1]
-    depth = other_rows[0].shape[1]
-    chunk = depth // 6
-    steps = depth // chunk
-    blocks = w_blocks[: CHIPS - 1] + last_block[:1] + w_blocks[CHIPS - 1 :] + last_block[1:]
+    depth = other_rows.shape[1]
+    steps = 3
     return pl.pallas_call(
         query_kernel,
         grid_spec=pltpu.PrefetchScalarGridSpec(
             num_scalar_prefetch=1,
             grid=(steps,),
             in_specs=[
-                pl.BlockSpec((1, rows, chunk), lambda k, facts: (0, 0, facts[GROUP] * steps + k)),
-                *([pl.BlockSpec(memory_space=pltpu.VMEM)] * (len(blocks) + len(other_rows))),
+                *([pl.BlockSpec(memory_space=pltpu.VMEM)] * (CORES + 2)),
             ],
             out_specs=[
                 pl.BlockSpec((rows, columns), lambda k, *_: (0, 0)),
@@ -393,25 +375,30 @@
             jax.ShapeDtypeStruct((rows, columns), jnp.float32),
             jax.ShapeDtypeStruct((rows, columns), jnp.bfloat16),
         ],
-        cost_estimate=pl.CostEstimate(
-            flops=4 * rows * depth * columns,
-            bytes_accessed=2 * (2 * rows + columns) * depth,
-            transcendentals=0,
-        ),
+        cost_estimate=pl.CostEstimate(flops=1000, bytes_accessed=1000, transcendentals=0),
         compiler_params=pltpu.CompilerParams(vmem_limit_bytes=16 * 2**20),
         name="project_query",
-    )(facts, *in_hbm([recomp_states]), *blocks, *other_rows)
+    )(facts, recomp_states, *blocks, other_rows)
 
 
 def attend_kernel(map_ref, facts, mine_ref, other_ref, new_ref, row_ref, *refs):
-    span_refs = refs[:CPR]
-    out_ref, keys, values, bias = refs[CPR:]
+    out_ref, keys, values, lengths, bias = refs[CORES:]
     rows = new_ref.shape[0]
     cached = CPR * SPAN
     padded = keys.shape[0]
+    sent = refs[0].shape[0] // CHIPS
     for s in range(CPR):
-        keys[s * SPAN : (s + 1) * SPAN] = span_refs[s][0, 0:SPAN, 0:HD]
-        values[s * SPAN : (s + 1) * SPAN] = span_refs[s][0, 0:SPAN, HD : 2 * HD]
+        slot = jnp.int32(0)
+        for p in range(CHIPS * CORES):
+            slot = jnp.where(facts[ORDER + p] == map_ref[s], p, slot)
+        first = pl.multiple_of(slot % CHIPS * sent, 16)
+        for c in range(CORES):
+
+            @pl.when(slot // CHIPS == c)
+            def _(s=s, first=first, ref=refs[c]):
+                keys[s * SPAN : (s + 1) * SPAN] = ref[pl.ds(first, SPAN), 0:HD]
+                values[s * SPAN : (s + 1) * SPAN] = ref[pl.ds(first, SPAN), HD : 2 * HD]
+                lengths[s] = ref[pl.ds(first + SPAN, PAGE), :]
     keys[cached : cached + rows] = new_ref[:, 0:HD]
     values[cached : cached + rows] = new_ref[:, HD : 2 * HD]
     keys[cached + rows :] = jnp.zeros((padded - cached - rows, HD), jnp.bfloat16)
@@ -428,7 +415,7 @@
     for s in range(CPR):
         key_pos = lane + s * SPAN
         redone = jnp.max(jnp.where(mine_at == key_pos, 1.0, 0.0), axis=0, keepdims=True)
-        length = span_refs[s][0, SPAN : SPAN + PAGE, :].astype(jnp.float32)[0:1]
+        length = lengths[s].astype(jnp.float32)[0:1]
         offset = lax.broadcasted_iota(jnp.int32, (1, SPAN), 1).astype(jnp.float32)
         usable = jnp.where(offset < length, 1.0 - redone, 0.0)
         allowed = (jnp.broadcast_to(usable, (rows, SPAN)) > 0.5) & (key_pos <= mine_at)
@@ -452,12 +439,11 @@
         out_ref[:, h * HD : (h + 1) * HD] = (mixed / total).astype(jnp.bfloat16)
 
 
-def attend(span_map, facts, mine, other, new_kv, positions, payload):
+def attend(span_map, facts, mine, other, new_kv, positions, payloads):
     rows, columns = mine.shape
     cached = CPR * SPAN
     padded = cached + SPAN
     whole = lambda *shape: pl.BlockSpec(shape, lambda i, *_: (0,) * len(shape))
-    slot = lambda s: pl.BlockSpec((1,) + payload.shape[1:], lambda i, map_ref, *_: (map_ref[s], 0, 0))
     return pl.pallas_call(
         attend_kernel,
         grid_spec=pltpu.PrefetchScalarGridSpec(
@@ -468,84 +454,80 @@
                 whole(rows, columns),
                 whole(rows, 2 * HD),
                 whole(1, rows),
-                *[slot(s) for s in range(CPR)],
+                *([pl.BlockSpec(memory_space=pltpu.VMEM)] * CORES),
             ],
             out_specs=whole(rows, columns),
             scratch_shapes=[
                 pltpu.VMEM((padded, HD), jnp.bfloat16),
                 pltpu.VMEM((padded, HD), jnp.bfloat16),
+                pltpu.VMEM((CPR, PAGE, 2 * HD), jnp.bfloat16),
                 pltpu.VMEM((rows, padded), jnp.float32),
             ],
         ),
         out_shape=jax.ShapeDtypeStruct((rows, columns), jnp.bfloat16),
-        cost_estimate=pl.CostEstimate(
-            flops=4 * rows * columns * padded,
-            bytes_accessed=2 * padded * 2 * HD + 8 * rows * columns,
-            transcendentals=rows * (columns // HD) * padded,
-        ),
+        cost_estimate=pl.CostEstimate(flops=1000, bytes_accessed=1000, transcendentals=0),
         compiler_params=pltpu.CompilerParams(vmem_limit_bytes=20 * 2**20),
         name="attend",
-    )(span_map, facts, mine, other, new_kv, positions, *in_hbm([payload] * CPR))
+    )(span_map, facts, mine, other, new_kv, positions, *payloads)
 
 
 def output_kernel(plan, arrived, facts, att_ref, att2_ref, *refs):
     out_ref, sent_ref, w_buf, o_buf, in_sem, out_sem, late_sem = refs[-7:]
-    third = o_buf.shape[3]
-    rows = o_buf.shape[2]
+    rows, columns = o_buf.shape[1:]
+    share = columns // 6
+    group = facts[GROUP]
     loads = []
-    for p, (slot, lots) in enumerate(plan):
+    for p, (slot, parts) in enumerate(plan):
         copies = []
-        for lot, parts in enumerate(lots):
-            for n, (source, row, column, first, size) in enumerate(parts):
-                view = refs[source].at[pl.ds(row, size), pl.ds(column, third)]
-                copies.append(
-                    pltpu.make_async_copy(
-                        view, w_buf.at[p, lot, pl.ds(first, size)], in_sem.at[p, lot, n]
-                    )
-                )
-        for copy in copies:
-            copy.start()
+        for source, row, first, size in parts:
+            ref = refs[source]
+            if ref.shape[1] == columns:
+                spans = [(0, 0, columns)]
+            elif ref.shape[1] == share:
+                spans = [(0, pl.multiple_of((1 - group) * share, share), share)]
+            else:
+                own = pl.multiple_of(group * share, share)
+                spans = [(0, own, share), (share, 2 * share, columns - 2 * share)]
+            for start, target, width in spans:
+                view = ref.at[pl.ds(row, size), pl.ds(start, width)]
+                goal = w_buf.at[p, pl.ds(first, size), pl.ds(target, width)]
+                copy = pltpu.make_async_copy(view, goal, in_sem.at[p, len(copies)])
+                copy.start()
+                copies.append(copy)
         loads.append(copies)
     stores = place(facts, [(refs[source], slots) for source, slots in arrived], out_ref, late_sem)
     attended = jnp.concatenate([att_ref[...], att2_ref[...]], axis=0)
-    for p, (slot, lots) in enumerate(plan):
+    width = columns // 3
+    for p, (slot, parts) in enumerate(plan):
         for copy in loads[p]:
             copy.wait()
-        for lot in range(len(lots)):
+        for start in range(0, columns, width):
             both = jnp.dot(
-                attended, w_buf[p, lot], preferred_element_type=jnp.float32
+                attended, w_buf[p, :, start : start + width], preferred_element_type=jnp.float32
             ).astype(jnp.bfloat16)
-            o_buf[p, lot] = both[:rows]
-            sent_ref[p, lot] = both[rows:]
-            copy = pltpu.make_async_copy(
-                o_buf.at[p, lot],
-                out_ref.at[0, :, pl.ds(place_of(facts, slot, lot, third), third)],
-                out_sem.at[p, lot],
-            )
-            copy.start()
-            stores.append(copy)
+            o_buf[p, :, start : start + width] = both[:rows]
+            sent_ref[p, :, start : start + width] = both[rows:]
+        copy = pltpu.make_async_copy(
+            o_buf.at[p], out_ref.at[0, :, columns_of(facts, slot, columns)], out_sem.at[p]
+        )
+        copy.start()
+        stores.append(copy)
     for copy in stores:
         copy.wait()
 
 
-def place_of(facts, slot, lot, third):
-    group = facts[GROUP]
-    kind = lot if slot % CHIPS == 0 else (group, 2, 1 - group)[lot]
-    return pl.multiple_of(facts[ORDER + slot] * (3 * third) + kind * third, third)
+def columns_of(facts, slot, columns):
+    return pl.ds(pl.multiple_of(facts[ORDER + slot] * columns, columns), columns)
 
 
 def place(facts, arrived, out_ref, sem):
     copies = []
     for ref, slots in arrived:
-        third = ref.shape[3]
         for p, slot in enumerate(slots):
-            for lot in range(3):
-                start = place_of(facts, slot + CHIPS, lot, third)
-                copy = pltpu.make_async_copy(
-                    ref.at[p, lot], out_ref.at[0, :, pl.ds(start, third)], sem.at[len(copies)]
-                )
-                copy.start()
-                copies.append(copy)
+            target = out_ref.at[0, :, columns_of(facts, slot + CHIPS, ref.shape[2])]
+            copy = pltpu.make_async_copy(ref.at[p], target, sem.at[len(copies)])
+            copy.start()
+            copies.append(copy)
     return copies
 
 
@@ -565,7 +547,7 @@
             grid=(),
             in_specs=[pl.BlockSpec(memory_space=pl.ANY)] * (len(blocks) + 1),
             out_specs=pl.BlockSpec(memory_space=pl.ANY),
-            scratch_shapes=[pltpu.SemaphoreType.DMA((3 * sum(map(len, slots)),))],
+            scratch_shapes=[pltpu.SemaphoreType.DMA((sum(map(len, slots)),))],
         ),
         out_shape=pltpu.HBM(before.shape, jnp.bfloat16),
         input_output_aliases={1 + len(blocks): 0},
@@ -584,12 +566,11 @@
         return [block is held for held in sources].index(True)
 
     plan = [
-        (slot, [[(index_of(block), *where) for block, *where in lot] for lot in lots])
-        for slot, lots in work
+        (slot, [(index_of(block), *where) for block, *where in parts]) for slot, parts in work
     ]
     arrived = [(index_of(block), slots) for block, slots in arrived]
-    placed = 3 * sum(len(slots) for _, slots in arrived)
-    third = width // (CHIPS * CORES * 3)
+    placed = sum(len(slots) for _, slots in arrived)
+    columns = width // (CHIPS * CORES)
     filled = [] if before is None else [before]
     return pl.pallas_call(
         partial(output_kernel, plan, arrived),
@@ -600,23 +581,19 @@
             + [pl.BlockSpec(memory_space=pl.ANY)] * (len(sources) + len(filled)),
             out_specs=[pl.BlockSpec(memory_space=pl.ANY), pl.BlockSpec(memory_space=pltpu.VMEM)],
             scratch_shapes=[
-                pltpu.VMEM((len(plan), 3, depth, third), jnp.bfloat16),
-                pltpu.VMEM((len(plan), 3, rows, third), jnp.bfloat16),
-                pltpu.SemaphoreType.DMA((len(plan), 3, 2)),
-                pltpu.SemaphoreType.DMA((len(plan), 3)),
+                pltpu.VMEM((len(plan), depth, columns), jnp.bfloat16),
+                pltpu.VMEM((len(plan), rows, columns), jnp.bfloat16),
+                pltpu.SemaphoreType.DMA((len(plan), 9)),
+                pltpu.SemaphoreType.DMA((len(plan),)),
                 pltpu.SemaphoreType.DMA((max(placed, 1),)),
             ],
         ),
         out_shape=[
             pltpu.HBM((1, rows, width), jnp.bfloat16),
-            pltpu.VMEM((len(plan), 3, rows, third), jnp.bfloat16),
+            pltpu.VMEM((len(plan), rows, columns), jnp.bfloat16),
         ],
         input_output_aliases={1 + CORES + len(sources): 0} if filled else {},
-        cost_estimate=pl.CostEstimate(
-            flops=2 * rows * CORES * depth * 3 * third * len(plan),
-            bytes_accessed=2 * 3 * third * len(plan) * (rows + depth),
-            transcendentals=0,
-        ),
+        cost_estimate=pl.CostEstimate(flops=1000, bytes_accessed=1000, transcendentals=0),
         compiler_params=pltpu.CompilerParams(vmem_limit_bytes=(len(plan) * 3 + 6) * 2**20),
         name="project_output",
     )(facts, *attended, *sources, *in_hbm(filled))
@@ -633,6 +610,7 @@
     recompute_idx,
     block_table,
 ):
+    pair = lambda ahead, back: (move(ahead, AHEAD), move(back, BACK))
     swap = lambda *blocks: tuple(move(block, SIBLING) for block in blocks)
     group = lax.axis_index("groups")
     width, heads, part = w_query.shape
@@ -640,114 +618,114 @@
     half = width // 2
     depth = heads * HD
     columns = w_out.shape[3]
-    third = columns // 3
+    share = columns // 6
     order = jnp.asarray(slot_table())[lax.axis_index("serve")]
     facts = jnp.concatenate([group[None].astype(jnp.int32), span_lengths, order, block_table])
 
     query_rows = w_query.transpose(1, 2, 0).reshape(heads * part, width)
     kv_rows = w_kv.transpose(1, 2, 0).reshape(2 * part, width)
     own_out = w_out.reshape(depth, columns)
-    lot = rows // 3
     cut = heads * part
-    (block,) = take_parts(
+    k0, q0 = take_parts(
         facts,
         [query_rows, kv_rows],
-        [(cut + 4 * part, half)],
+        [(4 * part, half), (cut, half)],
         [
-            (0, 0, (0, 0), 0, False, (cut, half)),
-            (1, 0, (0, cut), 0, None, (2 * part, half)),
-            (1, 0, (0, cut + 2 * part), half, None, (2 * part, half)),
+            (1, 0, (0, 0), (0, 0), None, (2 * part, half)),
+            (1, 0, (0, 2 * part), (half, 0), None, (2 * part, half)),
+            (0, 1, (0, 0), (0, 0), False, (cut, half)),
         ],
     )
-    *theirs, out_block = take_parts(
+    cut = depth // 2
+    theirs, top0, low0 = take_parts(
         facts,
-        [recomp_states[0], own_out, block],
-        [(lot, half)] * 3 + [(2 * depth, third)],
-        [(0, n, (n * lot, 0), 0, True, (lot, half)) for n in range(3)]
+        [recomp_states[0], own_out, k0],
+        [(rows, half)] + [(cut, columns - share)] * 2,
+        [(0, 0, (0, 0), (0, 0), True, (rows, half))]
+        + [(1, 1 + n, (n * cut, 0), (0, 0), False, (cut, share)) for n in range(2)]
         + [
-            (1, 3, (0, 0), 0, False, (depth, third)),
-            (1, 3, (0, depth), 2 * third, None, (depth, third)),
+            (1, 1 + n, (n * cut, 0), (2 * share, share), None, (cut, columns - 2 * share))
+            for n in range(2)
         ],
     )
-    out = (move(block, AHEAD), move(block, BACK), across(theirs[0]), *swap(block))
-    ahead1, back1, rows1, block2 = together(*out)
-    out = (move(ahead1, AHEAD), move(back1, BACK), across(theirs[1]), *swap(ahead1, back1))
-    ahead2, back2, rows2, *swapped1 = together(*out)
-    out = (move(ahead2, AHEAD), move(back2, BACK), across(theirs[2]), *swap(ahead2, back2))
-    ahead3, back3, rows3, *swapped2, to_ahead, to_back = together(
-        *out, packs=([(0, 0, cut)], [(1, cut, 4 * part)])
-    )
-    far_query, far_kv, out_block, *swapped3 = together(
-        move(to_ahead, AHEAD), move(to_back, BACK), out_block, *swap(ahead3, back3)
-    )
-    far_query2, far_kv2 = swap(far_query, far_kv)
-    both = [block, ahead1, back1, ahead2, back2, ahead3, back3, block2, *swapped1, *swapped2, *swapped3]
-
-    shared = lambda n: (n, 0, depth)
-    payload, new_kv, cache = project_kv(
-        facts, span_states, recomp_states, both, [far_kv, far_kv2]
-    )
-    mine, theirs_part = project_query(
-        facts, recomp_states, (rows1, rows2, rows3), both, [far_query, far_query2], depth
-    )
-    a1, b1, payload, theirs_part = lax.optimization_barrier(
-        (move(out_block, AHEAD), move(out_block, BACK), payload, theirs_part)
-    )
-    a1, b1, send1 = together(a1, b1, packs=([shared(0), shared(1)],))
-    payloads = lax.all_gather(payload, "serve", axis=0)
-    a2, b2, x1, send2 = together(
-        move(a1, AHEAD), move(b1, BACK), across(send1), packs=([shared(0), shared(1)],)
-    )
-    cut = depth // 2
-    a3, b3, x2, other, send3, to_ahead, to_back = together(
-        move(a2, AHEAD),
-        move(b2, BACK),
-        across(send2),
-        across(theirs_part),
+    ka1, kb1 = together(*pair(k0, k0))
+    qa1, qb1, ka1 = together(*pair(q0, q0), ka1)
+    ka2, kb2, qa1 = together(*pair(ka1, kb1), qa1)
+    qa2, qb2, ka2 = together(*pair(qa1, qb1), ka2)
+    ka3, kb3, qa2 = together(*pair(ka2, kb2), qa2)
+    qa3, qb3, ka3, top0 = together(*pair(qa2, qb2), ka3, top0)
+    keys = (k0, ka1, kb1, ka2, kb2, ka3, kb3, move(kb3, BACK))
+    queries = (q0, qa1, qb1, qa2, qb2, qa3, qb3, move(qa3, AHEAD))
+    key_stack = (half, [(n, h * 2 * part, 2 * part) for h in range(2) for n in range(CHIPS)])
+    query_stack = (half, [(CHIPS + n, 0, heads * part) for n in range(CHIPS)])
+    *_, other_rows, low0, keys, queries = together(
+        *keys, *queries, across(theirs), low0, packs=(key_stack, query_stack)
+    )
+    keys2, queries = lax.optimization_barrier((*swap(keys), queries))
+    queries = (queries, *swap(queries))
+
+    span0, new_kv, cache = project_kv(facts, span_states, recomp_states, (keys, keys2))
+    ta1, tb1, span0 = together(*pair(top0, top0), span0)
+    mine, theirs_part = project_query(facts, recomp_states, other_rows, queries, depth)
+    sides = lambda *found: (share, [(n, 0, cut) for n in found])
+    la1, lb1, sa1, sb1, theirs_part, ta1, tb1, send1 = together(
+        *pair(low0, low0), *pair(span0, span0), theirs_part, ta1, tb1, packs=(sides(5, 0, 6, 1),)
+    )
+    ta2, tb2, sa2, sb2, other = together(*pair(ta1, tb1), *pair(sa1, sb1), across(theirs_part))
+    la2, lb2, sa3, sb3, x1, ta2, tb2, send2 = together(
+        *pair(la1, lb1), *pair(sa2, sb2), across(send1), ta2, tb2, packs=(sides(5, 0, 6, 1),)
+    )
+    spans = (span0, sa1, sb1, sa2, sb2, sa3, sb3, move(sa3, AHEAD))
+    stack = (2 * HD, [(2 + n, 0, span0.shape[0]) for n in range(CHIPS)])
+    quarter = lambda n, first: (columns - share, [(n, first, cut // 2)])
+    ta3, tb3, *_, spans, top_ahead, top_back = together(
+        *pair(ta2, tb2), *spans, packs=(stack, quarter(0, 0), quarter(1, cut // 2))
+    )
+    attended = attend(
+        span_map[0], facts, mine, other, new_kv, recompute_idx, (spans, *swap(spans))
+    )
+    la3, lb3, x2, *attended = lax.optimization_barrier(
+        (*pair(la2, lb2), across(send2), attended, *swap(attended))
+    )
+    la3, lb3, ta3, tb3, send3, low_ahead, low_back = together(
+        la3,
+        lb3,
+        ta3,
+        tb3,
         packs=(
-            [shared(0), shared(1)],
-            [(0, 0, cut), (0, depth, cut)],
-            [(1, cut, cut), (1, depth + cut, cut)],
+            sides(2, 0, 3, 1),
+            quarter(0, 0),
+            quarter(1, cut // 2),
         ),
     )
-    attended = attend(span_map[0], facts, mine, other, new_kv, recompute_idx, payloads)
-    attended = (attended, *swap(attended))
-
-    def near(slot, block, side, first):
-        return slot, [
-            [(block, 0, 0, 0, depth)],
-            [(block, depth, 0, 0, depth)],
-            [(side, first * depth, 0, 0, depth)],
-        ]
+
+    def near(slot, top, low, side, first):
+        return slot, [(top, 0, 0, cut), (low, 0, cut, cut), (side, first * depth, 0, depth)]
 
     early = [
-        (0, [[(own_out, 0, n * third, 0, depth)] for n in range(3)]),
-        near(1, a1, x1, 0),
-        near(2, b1, x1, 1),
-        near(3, a2, x2, 0),
-        near(4, b2, x2, 1),
+        (0, [(own_out, 0, 0, depth)]),
+        near(1, ta1, la1, x1, 0),
+        near(2, tb1, lb1, x1, 1),
+        near(3, ta2, la2, x2, 0),
+        near(4, tb2, lb2, x2, 1),
     ]
     width_out = CHIPS * CORES * columns
     result, sent1 = project_output(facts, attended, None, early, [], width_out)
-    a4, b4, x3, sent1 = lax.optimization_barrier(
-        (move(to_ahead, AHEAD), move(to_back, BACK), across(send3), sent1)
-    )
-    a4, b4, x3, send4 = together(a4, b4, x3, packs=([(0, 0, cut), (1, 0, cut)],))
-    late = [near(5, a3, x3, 0), near(6, b3, x3, 1)]
+    t4a, t4b, l4a, l4b, x3, sent1 = lax.optimization_barrier(
+        (*pair(top_ahead, top_back), *pair(low_ahead, low_back), across(send3), sent1)
+    )
+    t4a, t4b, l4a, l4b, send4 = together(
+        t4a, t4b, l4a, l4b, packs=((share, [(n, 0, cut // 2) for n in range(4)]),)
+    )
+    late = [near(5, ta3, la3, x3, 0), near(6, tb3, lb3, x3, 1)]
     result, sent2 = project_output(facts, attended, result, late, [], width_out)
     x4, arrived1, sent2 = lax.optimization_barrier((across(send4), *swap(sent1), sent2))
-    last = [
-        (
-            7,
-            [
-                [(a4, 0, 0, 0, cut), (b4, 0, 0, cut, cut)],
-                [(a4, cut, 0, 0, cut), (b4, cut, 0, cut, cut)],
-                [(x4, 0, 0, 0, depth)],
-            ],
-        )
-    ]
     arrived = [(arrived1, (0, 1, 2, 3, 4))]
-    result, sent3 = project_output(facts, attended, result, last, arrived, width_out)
+    quarters = [(block, 0, n * cut // 2, cut // 2) for n, block in enumerate((t4a, t4b, l4a, l4b))]
+    far = (7, [*quarters, (x4, 0, 0, depth)])
+    result, sent3 = project_output(
+        facts, attended, result, [far], arrived, width_out
+    )
     arrived = [(swap(sent2)[0], (5, 6)), (swap(sent3)[0], (7,))]
     return (cache, place_output(facts, arrived, result))
 

time: 238 us -> 211 us (0.89)
  starting transfers between devices: 29.3 us -> 46.2 us
  between operations: 15 us -> 1.67 us
  waiting for transfers between devices: 136 us -> 123 us
  Pallas kernels: 47.8 us -> 38 us
  local copies, waits for them, and re-layouts: 8.64 us -> 0.74 us
    ppermute x8 -> x6, waiting for transfers between devices: 78.6 us -> 11.8 us  [across(): return lax.ppermute(block, 'groups', ACROSS)]
    ppermute x29 -> x44, waiting for transfers between devices: 57.5 us -> 111 us  [move(): return lax.ppermute(block, 'serve', pairs)]
    ppermute x29 -> x44, starting transfers between devices: 19.9 us -> 39.4 us  [move(): return lax.ppermute(block, 'serve', pairs)]
    unnamed x48 -> x18, local copies, waits for them, and re-layouts: 7.94 us -> 0.04 us
    pallas_call x3, Pallas kernels: 16 us -> 12.7 us  [project_output(): pl.pallas_call(partial(output_kernel, plan, arrived), grid_spec=pltpu.Pre...]
    pallas_call x1, Pallas kernels: 8.59 us -> 5.65 us  [project_kv(): pl.pallas_call(kv_kernel, grid_spec=pltpu.PrefetchScalarGridSpec(num_scal...]
    ppermute x8 -> x6, starting transfers between devices: 9.42 us -> 6.78 us  [across(): return lax.ppermute(block, 'groups', ACROSS)]
    pallas_call x1, Pallas kernels: 8.83 us -> 6.22 us  [project_query(): pl.pallas_call(query_kernel, grid_spec=pltpu.PrefetchScalarGridSpec(num_s...]
  transfers between devices with their start and end apart: 38 -> 50, of which waited for: 20 -> 32; matrix products, arithmetic and copies ran while one was open for 0% -> 0% of each run, Pallas kernels for 19% -> 16%
where the time goes in v3:
time: 211 us; the launch traced here: 210 us
  waiting for transfers between devices  123 us (58%)
  starting transfers between devices  46.2 us (22%)
  Pallas kernels  38 us (18%)
    ppermute x44, waiting for transfers between devices, move(): return lax.ppermute(block, 'serve', pairs)  111 us
    ppermute x44, starting transfers between devices, move(): return lax.ppermute(block, 'serve', pairs)  39.4 us
    pallas_call x3, Pallas kernels, project_output(): pl.pallas_call(partial(output_kernel, plan, arrived), grid_spec=pltpu.Pre...  12.7 us
    ppermute x6, waiting for transfers between devices, across(): return lax.ppermute(block, 'groups', ACROSS)  11.8 us
    ppermute x6, starting transfers between devices, across(): return lax.ppermute(block, 'groups', ACROSS)  6.78 us
    pallas_call x1, Pallas kernels, project_query(): pl.pallas_call(query_kernel, grid_spec=pltpu.PrefetchScalarGridSpec(num_s...  6.22 us
    pallas_call x1, Pallas kernels, attend(): pl.pallas_call(attend_kernel, grid_spec=pltpu.PrefetchScalarGridSpec(num_...  6.2 us
    pallas_call x1, Pallas kernels, project_kv(): pl.pallas_call(kv_kernel, grid_spec=pltpu.PrefetchScalarGridSpec(num_scal...  5.65 us
  transfers between devices with their start and end apart: 50, of which 32 were waited for; matrix products, arithmetic and copies ran while one was open for 0% of the time, Pallas kernels for 16%

profile of v3, /device:TPU:0, one launch (start us, length us, event | category | flops | bytes accessed | tf_op | source)
XLA Modules:
  0.0 210.5 jit_solution(15642059415175547626)
XLA Ops:
  2.0 0.7 pad_add_fusion.facts
  2.7 1.8 take_parts.2
  4.6 3.1 %collective-permute-start = (bf16[48,6144]{1,0:T(8,128)(2,1)S(1)}, bf16[48,6144]{1,0:T(8,128)(2,1)S(1)}, u32[]{:S(2)}, u32[]{:S(2)}) collective-permute-start(bf16[48,6144]{1,0:T(8,128)(2,1)S(1)} %get-tuple-element.98.refs_8_), channel_id=1, source_target_pairs={{0,4},{1,5},{4,8},{5,9},{8,12},{9,13},{12,14},{13,15},{14,10},{15,... | collective-permute-start | bytes 1769480 | tf_op jit(solution)/shard_map/ppermute | solution.py:231
  7.6 2.0 collective-permute-start.2
  9.7 2.9 %take_parts.3 = (bf16[240,6144]{1,0:T(8,128)(2,1)S(1)}, bf16[384,640]{1,0:T(8,128)(2,1)S(1)}, bf16[384,640]{1,0:T(8,128)(2,1)S(1)}) custom-call(s32[34]{0:T(128)S(1)} %pad_add_fusion.facts, bf16[240,12288]{1,0:T(8,128)(2,1)} %bitcast.12, bf16[768,768]{1,0:T(8,128)(2,1)} %bitcast.17, bf16[32,6144]{1,0:T(8,128)(2,1)} %copy-done.1), custom_call_target="tpu_custom_call" | custom-call | tf_op jit(solution)/shard_map/take_parts/pallas_call | solution.py:215
  12.6 2.0 collective-permute-start.14
  14.6 14.7 %collective-permute-done.2.refs_0_ = bf16[32,6144]{1,0:T(8,128)(2,1)S(1)} collective-permute-done((bf16[32,6144]{1,0:T(8,128)(2,1)S(1)}, bf16[32,6144]{1,0:T(8,128)(2,1)S(1)}, u32[]{:S(2)}, u32[]{:S(2)}) %collective-permute-start.2) | collective-permute-done | bytes 393248 | tf_op jit(solution)/shard_map/ppermute | solution.py:231
  29.3 1.5 collective-permute-done.3.refs_1_
  31.2 1.7 collective-permute-start.4
  33.2 9.7 %collective-permute-done.5.refs_1_ = bf16[32,6144]{1,0:T(8,128)(2,1)S(1)} collective-permute-done((bf16[32,6144]{1,0:T(8,128)(2,1)S(1)}, bf16[32,6144]{1,0:T(8,128)(2,1)S(1)}, u32[]{:S(2)}, u32[]{:S(2)}) %collective-permute-start.5) | collective-permute-done | bytes 393248 | tf_op jit(solution)/shard_map/ppermute | solution.py:231
  42.9 1.6 collective-permute-start.6
  44.9 10.6 %collective-permute-done.7.refs_1_ = bf16[48,6144]{1,0:T(8,128)(2,1)S(1)} collective-permute-done((bf16[48,6144]{1,0:T(8,128)(2,1)S(1)}, bf16[48,6144]{1,0:T(8,128)(2,1)S(1)}, u32[]{:S(2)}, u32[]{:S(2)}) %collective-permute-start.7) | collective-permute-done | bytes 589856 | tf_op jit(solution)/shard_map/ppermute | solution.py:231
  55.6 1.6 collective-permute-start.8
  57.6 6.4 %collective-permute-done.9.refs_1_ = bf16[32,6144]{1,0:T(8,128)(2,1)S(1)} collective-permute-done((bf16[32,6144]{1,0:T(8,128)(2,1)S(1)}, bf16[32,6144]{1,0:T(8,128)(2,1)S(1)}, u32[]{:S(2)}, u32[]{:S(2)}) %collective-permute-start.9) | collective-permute-done | bytes 393248 | tf_op jit(solution)/shard_map/ppermute | solution.py:231
  64.0 0.7 collective-permute-done.8.refs_0_
  64.7 1.6 collective-permute-start.10
  66.3 8.0 %collective-permute-done.11.refs_1_ = bf16[48,6144]{1,0:T(8,128)(2,1)S(1)} collective-permute-done((bf16[48,6144]{1,0:T(8,128)(2,1)S(1)}, bf16[48,6144]{1,0:T(8,128)(2,1)S(1)}, u32[]{:S(2)}, u32[]{:S(2)}) %collective-permute-start.11) | collective-permute-done | bytes 589856 | tf_op jit(solution)/shard_map/ppermute | solution.py:231
  74.2 3.1 %collective-permute-done.10.refs_0_ = bf16[48,6144]{1,0:T(8,128)(2,1)S(1)} collective-permute-done((bf16[48,6144]{1,0:T(8,128)(2,1)S(1)}, bf16[48,6144]{1,0:T(8,128)(2,1)S(1)}, u32[]{:S(2)}, u32[]{:S(2)}) %collective-permute-start.10) | collective-permute-done | bytes 589856 | tf_op jit(solution)/shard_map/ppermute | solution.py:231
  77.3 1.6 collective-permute-start.13
  79.3 7.3 %collective-permute-done.12.refs_7_ = bf16[32,6144]{1,0:T(8,128)(2,1)S(1)} collective-permute-done((bf16[32,6144]{1,0:T(8,128)(2,1)S(1)}, bf16[32,6144]{1,0:T(8,128)(2,1)S(1)}, u32[]{:S(2)}, u32[]{:S(2)}) %collective-permute-start.12) | collective-permute-done | bytes 393248 | tf_op jit(solution)/shard_map/ppermute | solution.py:231
  86.7 1.9 collective-permute-done.13.refs_15_
  89.2 5.6 %collective-permute-done.15.sib_ref = bf16[256,6144]{1,0:T(8,128)(2,1)S(1)} collective-permute-done((bf16[256,6144]{1,0:T(8,128)(2,1)S(1)}, bf16[256,6144]{1,0:T(8,128)(2,1)S(1)}, u32[]{:S(2)}, u32[]{:S(2)}) %collective-permute-start.15) | collective-permute-done | bytes 3145760 | tf_op jit(solution)/shard_map/ppermute | solution.py:231
  95.0 1.6 collective-permute-start.18
  97.0 1.6 collective-permute-start.16
  99.1 5.7 %project_kv.1 = (bf16[272,256]{1,0:T(8,128)(2,1)S(1)}, bf16[240,256]{1,0:T(8,128)(2,1)S(1)}, bf16[16,16,256]{2,1,0:T(8,128)(2,1)}) custom-call(s32[34]{0:T(128)S(1)} %pad_add_fusion.facts, bf16[1,256,12288]{2,1,0:T(8,128)(2,1)S(1)} %bitcast.16, bf16[1,240,12288]{2,1,0:T(8,128)(2,1)S(1)} %bitcast.14, bf16[256,6144]{1,0:T(8,128)(2,1)S(1)} %get-tuple-element.119.own_ref, ...), custom_call_target="tpu_custom_call" | custom-call | flops 1000 | bytes 1000 | tf_op jit(solution)/shard_map/project_kv/pallas_call | solution.py:296
  104.7 4.3 %collective-permute-done.18.refs_0_ = bf16[384,640]{1,0:T(8,128)(2,1)S(1)} collective-permute-done((bf16[384,640]{1,0:T(8,128)(2,1)S(1)}, bf16[384,640]{1,0:T(8,128)(2,1)S(1)}, u32[]{:S(2)}, u32[]{:S(2)}) %collective-permute-start.18) | collective-permute-done | bytes 491552 | tf_op jit(solution)/shard_map/ppermute | solution.py:231
  109.0 1.6 collective-permute-done.19.refs_1_
  110.7 1.6 collective-permute-start.20
  112.7 6.2 %project_query.1 = (f32[240,768]{1,0:T(8,128)S(1)}, bf16[240,768]{1,0:T(8,128)(2,1)S(1)}) custom-call(s32[34]{0:T(128)S(1)} %pad_add_fusion.facts, bf16[1,240,12288]{2,1,0:T(8,128)(2,1)S(1)} %bitcast.14, bf16[384,6144]{1,0:T(8,128)(2,1)S(1)} %get-tuple-element.127.own_ref, bf16[384,6144]{1,0:T(8,128)(2,1)S(1)} %collective-permute-done.22.sib_ref, ...), custom_call_target="tpu_custom_call" | custom-call | flops 1000 | bytes 1000 | tf_op jit(solution)/shard_map/project_query/pallas_call | solution.py:357
  119.6 1.6 collective-permute-done.17.refs_1_
  121.2 0.8 collective-permute-done.20.refs_2_
  122.0 1.3 collective-permute-done.21.refs_3_
  123.4 1.6 collective-permute-start.29
  124.9 1.6 collective-permute-start.25
  126.5 1.5 collective-permute-start.27
  129.0 11.0 %collective-permute-done.27.refs_2_ = bf16[272,256]{1,0:T(8,128)(2,1)S(1)} collective-permute-done((bf16[272,256]{1,0:T(8,128)(2,1)S(1)}, bf16[272,256]{1,0:T(8,128)(2,1)S(1)}, u32[]{:S(2)}, u32[]{:S(2)}) %collective-permute-start.27) | collective-permute-done | bytes 139296 | tf_op jit(solution)/shard_map/ppermute | solution.py:231
  140.0 1.6 collective-permute-start.23
  141.6 1.0 collective-permute-done.28.refs_3_
  143.6 1.5 collective-permute-start.30
  145.6 5.7 %collective-permute-done.32.refs_4_ = bf16[1536,128]{1,0:T(8,128)(2,1)S(1)} collective-permute-done((bf16[1536,128]{1,0:T(8,128)(2,1)S(1)}, bf16[1536,128]{1,0:T(8,128)(2,1)S(1)}, u32[]{:S(2)}, u32[]{:S(2)}) %collective-permute-start.32) | collective-permute-done | bytes 393248 | tf_op jit(solution)/shard_map/ppermute | solution.py:235
  151.3 1.4 collective-permute-done.23.refs_0_
  152.7 2.0 collective-permute-done.24.refs_1_
  154.6 1.5 collective-permute-done.31.refs_3_
  156.2 0.9 collective-permute-start.33
  157.1 1.2 collective-permute-start.34
  158.3 0.8 collective-permute-start.35
  159.1 9.8 %collective-permute-done.35.refs_9_ = bf16[272,256]{1,0:T(8,128)(2,1)S(1)} collective-permute-done((bf16[272,256]{1,0:T(8,128)(2,1)S(1)}, bf16[272,256]{1,0:T(8,128)(2,1)S(1)}, u32[]{:S(2)}, u32[]{:S(2)}) %collective-permute-start.35) | collective-permute-done | bytes 139296 | tf_op jit(solution)/shard_map/ppermute | solution.py:231
  169.1 1.1 collective-permute-start.38
  170.3 0.9 collective-permute-start.39
  171.9 6.2 %attend.1.att_ref = bf16[240,768]{1,0:T(8,128)(2,1)S(1)} custom-call(s32[6]{0:T(128)S(1)} %bitcast.19, s32[34]{0:T(128)S(1)} %pad_add_fusion.facts, f32[240,768]{1,0:T(8,128)S(1)} %get-tuple-element.153.mine_ref, bf16[240,768]{1,0:T(8,128)(2,1)S(1)} %get-tuple-element.154.other_ref, bf16[240,256]{1,0:T(8,128)(2,1)S(1)} %get-tuple-element.155.new_ref, ...), custom_call_target="tpu_custom_call" | custom-call | flops 1000 | bytes 1000 | tf_op jit(solution)/shard_map/attend/pallas_call | solution.py:447
  178.3 3.8 %collective-permute-done.40.refs_8_ = bf16[1536,128]{1,0:T(8,128)(2,1)S(1)} collective-permute-done((bf16[1536,128]{1,0:T(8,128)(2,1)S(1)}, bf16[1536,128]{1,0:T(8,128)(2,1)S(1)}, u32[]{:S(2)}, u32[]{:S(2)}) %collective-permute-start.40) | collective-permute-done | bytes 393248 | tf_op jit(solution)/shard_map/ppermute | solution.py:235
  182.8 0.8 collective-permute-done.39.refs_1_
  184.3 0.9 collective-permute-start.36
  185.2 1.1 collective-permute-start.37
  186.3 0.9 collective-permute-start.43
  187.2 1.1 collective-permute-start.44
  188.3 6.9 %project_output.3 = (bf16[1,240,12288]{2,1,0:T(8,128)(2,1)}, bf16[5,240,768]{2,1,0:T(8,128)(2,1)S(1)}) custom-call(s32[34]{0:T(128)S(1)} %pad_add_fusion.facts, bf16[240,768]{1,0:T(8,128)(2,1)S(1)} %attend.1.att_ref, bf16[240,768]{1,0:T(8,128)(2,1)S(1)} %collective-permute-done.42.att2_ref, bf16[768,768]{1,0:T(8,128)(2,1)S(1)} %bitcast.18, ...), custom_call_target="tpu_custom_call" | custom-call | flops 1000 | bytes 1000 | tf_op jit(solution)/shard_map/project_output/pallas_call | solution.py:575
  195.2 1.2 collective-permute-done.43.refs_2_
  197.2 1.6 collective-permute-start.46
  198.7 3.5 %project_output.4 = (bf16[1,240,12288]{2,1,0:T(8,128)(2,1)}, bf16[2,240,768]{2,1,0:T(8,128)(2,1)S(1)}) custom-call(s32[34]{0:T(128)S(1)} %pad_add_fusion.facts, bf16[240,768]{1,0:T(8,128)(2,1)S(1)} %attend.1.att_ref, bf16[240,768]{1,0:T(8,128)(2,1)S(1)} %collective-permute-done.42.att2_ref, ...), custom_call_target="tpu_custom_call", output_to_operand_aliasing={{0}: (8, {})} | custom-call | flops 1000 | bytes 1000 | tf_op jit(solution)/shard_map/project_output/pallas_call | solution.py:575
  202.3 2.3 %collective-permute-done.46.refs_4_ = bf16[768,128]{1,0:T(8,128)(2,1)S(1)} collective-permute-done((bf16[768,128]{1,0:T(8,128)(2,1)S(1)}, bf16[768,128]{1,0:T(8,128)(2,1)S(1)}, u32[]{:S(2)}, u32[]{:S(2)}) %collective-permute-start.46) | collective-permute-done | bytes 196640 | tf_op jit(solution)/shard_map/ppermute | solution.py:235
  204.6 2.3 %project_output.5 = (bf16[1,240,12288]{2,1,0:T(8,128)(2,1)}, bf16[1,240,768]{2,1,0:T(8,128)(2,1)S(1)}) custom-call(s32[34]{0:T(128)S(1)} %pad_add_fusion.facts, bf16[240,768]{1,0:T(8,128)(2,1)S(1)} %attend.1.att_ref, bf16[240,768]{1,0:T(8,128)(2,1)S(1)} %collective-permute-done.42.att2_ref, ...), custom_call_target="tpu_custom_call", output_to_operand_aliasing={{0}: (9, {})} | custom-call | flops 1000 | bytes 1000 | tf_op jit(solution)/shard_map/project_output/pallas_call | solution.py:575
  207.4 1.3 collective-permute-done.49.refs_1_
  208.7 1.6 place_output.1
  (81 shorter events, 11.8 us)
Async XLA Ops:
  4.6 5.1 %copy-start.1 = (bf16[32,6144]{1,0:T(8,128)(2,1)}, bf16[32,6144]{1,0:T(8,128)(2,1)S(1)}, u32[]{:S(2)}) copy-start(bf16[32,6144]{1,0:T(8,128)(2,1)S(1)} %get-tuple-element.97.refs_2_.refs_0_) | copy-start | bytes 1179652
  4.6 26.6 %collective-permute-start = (bf16[48,6144]{1,0:T(8,128)(2,1)S(1)}, bf16[48,6144]{1,0:T(8,128)(2,1)S(1)}, u32[]{:S(2)}, u32[]{:S(2)}) collective-permute-start(bf16[48,6144]{1,0:T(8,128)(2,1)S(1)} %get-tuple-element.98.refs_8_), channel_id=1, source_target_pairs={{0,4},{1,5},{4,8},{5,9},{8,12},{9,13},{12,14},{13,15},{14,10},{15,... | collective-permute-start | bytes 1769480 | tf_op jit(solution)/shard_map/ppermute | solution.py:231
  7.6 23.5 %collective-permute-start.1 = (bf16[48,6144]{1,0:T(8,128)(2,1)S(1)}, bf16[48,6144]{1,0:T(8,128)(2,1)S(1)}, u32[]{:S(2)}, u32[]{:S(2)}) collective-permute-start(bf16[48,6144]{1,0:T(8,128)(2,1)S(1)} %get-tuple-element.98.refs_8_), channel_id=1, source_target_pairs={{0,2},{1,3},{4,0},{5,1},{8,4},{9,5},{12,8},{13,9},{14,12},{15,13},... | collective-permute-start | bytes 1769480 | tf_op jit(solution)/shard_map/ppermute | solution.py:231
  7.6 21.7 %collective-permute-start.2 = (bf16[32,6144]{1,0:T(8,128)(2,1)S(1)}, bf16[32,6144]{1,0:T(8,128)(2,1)S(1)}, u32[]{:S(2)}, u32[]{:S(2)}) collective-permute-start(bf16[32,6144]{1,0:T(8,128)(2,1)S(1)} %get-tuple-element.97.refs_2_.refs_0_), channel_id=1, source_target_pairs={{0,4},{1,5},{4,8},{5,9},{8,12},{9,13},{12,14},{13,15},{14,10},{15,... | collective-permute-start | bytes 1179656 | tf_op jit(solution)/shard_map/ppermute | solution.py:231
  9.7 21.2 %collective-permute-start.3 = (bf16[32,6144]{1,0:T(8,128)(2,1)S(1)}, bf16[32,6144]{1,0:T(8,128)(2,1)S(1)}, u32[]{:S(2)}, u32[]{:S(2)}) collective-permute-start(bf16[32,6144]{1,0:T(8,128)(2,1)S(1)} %get-tuple-element.97.refs_2_.refs_0_), channel_id=1, source_target_pairs={{0,2},{1,3},{4,0},{5,1},{8,4},{9,5},{12,8},{13,9},{14,12},{15,13},... | collective-permute-start | bytes 1179656 | tf_op jit(solution)/shard_map/ppermute | solution.py:231
  9.7 89.4 %slice-start.2 = ((s8[6291456]{0:T(1024)(128)(4,1)}), s8[4194304]{0:T(1024)(128)(4,1)S(1)}, s32[]{:S(2)}) async-start(s8[6291456]{0:T(1024)(128)(4,1)} %bitcast.15), calls=%async_computation.2 | async-start | bytes 8388608
  12.6 74.1 %collective-permute-start.14 = (bf16[240,6144]{1,0:T(8,128)(2,1)S(1)}, bf16[240,6144]{1,0:T(8,128)(2,1)S(1)}, u32[]{:S(2)}, u32[]{:S(2)}) collective-permute-start(bf16[240,6144]{1,0:T(8,128)(2,1)S(1)} %get-tuple-element.117), channel_id=1, source_target_pairs={{0,16},{16,0},{1,17},{17,1},{2,18},{18,2},{3,19},{19,3},{4,20},{20... | collective-permute-start | bytes 8847368 | tf_op jit(solution)/shard_map/ppermute | solution.py:235
  30.9 12.1 %collective-permute-start.5 = (bf16[32,6144]{1,0:T(8,128)(2,1)S(1)}, bf16[32,6144]{1,0:T(8,128)(2,1)S(1)}, u32[]{:S(2)}, u32[]{:S(2)}) collective-permute-start(bf16[32,6144]{1,0:T(8,128)(2,1)S(1)} %get-tuple-element.101.refs_2_), channel_id=1, source_target_pairs={{0,2},{1,3},{4,0},{5,1},{8,4},{9,5},{12,8},{13,9},{14,12},{15,13},... | collective-permute-start | bytes 1179656 | tf_op jit(solution)/shard_map/ppermute | solution.py:231
  31.2 11.8 %collective-permute-start.4 = (bf16[32,6144]{1,0:T(8,128)(2,1)S(1)}, bf16[32,6144]{1,0:T(8,128)(2,1)S(1)}, u32[]{:S(2)}, u32[]{:S(2)}) collective-permute-start(bf16[32,6144]{1,0:T(8,128)(2,1)S(1)} %get-tuple-element.100.refs_1_), channel_id=1, source_target_pairs={{0,4},{1,5},{4,8},{5,9},{8,12},{9,13},{12,14},{13,15},{14,10},{15,... | collective-permute-start | bytes 1179656 | tf_op jit(solution)/shard_map/ppermute | solution.py:231
  32.9 22.7 %collective-permute-start.7 = (bf16[48,6144]{1,0:T(8,128)(2,1)S(1)}, bf16[48,6144]{1,0:T(8,128)(2,1)S(1)}, u32[]{:S(2)}, u32[]{:S(2)}) collective-permute-start(bf16[48,6144]{1,0:T(8,128)(2,1)S(1)} %get-tuple-element.104.refs_10_), channel_id=1, source_target_pairs={{0,2},{1,3},{4,0},{5,1},{8,4},{9,5},{12,8},{13,9},{14,12},{15,13},... | collective-permute-start | bytes 1769480 | tf_op jit(solution)/shard_map/ppermute | solution.py:231
  42.9 45.7 %copy-start.2 = (bf16[32,6144]{1,0:T(8,128)(2,1)S(1)}, bf16[32,6144]{1,0:T(8,128)(2,1)}, u32[]{:S(2)}) copy-start(bf16[32,6144]{1,0:T(8,128)(2,1)} %copy-done.1) | copy-start | bytes 1179652
  42.9 12.6 %collective-permute-start.6 = (bf16[48,6144]{1,0:T(8,128)(2,1)S(1)}, bf16[48,6144]{1,0:T(8,128)(2,1)S(1)}, u32[]{:S(2)}, u32[]{:S(2)}) collective-permute-start(bf16[48,6144]{1,0:T(8,128)(2,1)S(1)} %get-tuple-element.103.refs_9_), channel_id=1, source_target_pairs={{0,4},{1,5},{4,8},{5,9},{8,12},{9,13},{12,14},{13,15},{14,10},{15,... | collective-permute-start | bytes 1769480 | tf_op jit(solution)/shard_map/ppermute | solution.py:231
  44.5 19.5 %collective-permute-start.9 = (bf16[32,6144]{1,0:T(8,128)(2,1)S(1)}, bf16[32,6144]{1,0:T(8,128)(2,1)S(1)}, u32[]{:S(2)}, u32[]{:S(2)}) collective-permute-start(bf16[32,6144]{1,0:T(8,128)(2,1)S(1)} %get-tuple-element.107.refs_4_), channel_id=1, source_target_pairs={{0,2},{1,3},{4,0},{5,1},{8,4},{9,5},{12,8},{13,9},{14,12},{15,13},... | collective-permute-start | bytes 1179656 | tf_op jit(solution)/shard_map/ppermute | solution.py:231
  55.6 9.1 %collective-permute-start.8 = (bf16[32,6144]{1,0:T(8,128)(2,1)S(1)}, bf16[32,6144]{1,0:T(8,128)(2,1)S(1)}, u32[]{:S(2)}, u32[]{:S(2)}) collective-permute-start(bf16[32,6144]{1,0:T(8,128)(2,1)S(1)} %get-tuple-element.106.refs_3_), channel_id=1, source_target_pairs={{0,4},{1,5},{4,8},{5,9},{8,12},{9,13},{12,14},{13,15},{14,10},{15,... | collective-permute-start | bytes 1179656 | tf_op jit(solution)/shard_map/ppermute | solution.py:231
  57.1 17.1 %collective-permute-start.11 = (bf16[48,6144]{1,0:T(8,128)(2,1)S(1)}, bf16[48,6144]{1,0:T(8,128)(2,1)S(1)}, u32[]{:S(2)}, u32[]{:S(2)}) collective-permute-start(bf16[48,6144]{1,0:T(8,128)(2,1)S(1)} %get-tuple-element.110.refs_12_), channel_id=1, source_target_pairs={{0,2},{1,3},{4,0},{5,1},{8,4},{9,5},{12,8},{13,9},{14,12},{15,13},... | collective-permute-start | bytes 1769480 | tf_op jit(solution)/shard_map/ppermute | solution.py:231
  64.7 34.4 %slice-start.3 = ((s8[6291456]{0:T(1024)(128)(4,1)}), s8[2097152]{0:T(1024)(128)(4,1)S(1)}, s32[]{:S(2)}) async-start(s8[6291456]{0:T(1024)(128)(4,1)} %bitcast.15), calls=%async_computation.3 | async-start | bytes 4194304
  64.7 12.6 %collective-permute-start.10 = (bf16[48,6144]{1,0:T(8,128)(2,1)S(1)}, bf16[48,6144]{1,0:T(8,128)(2,1)S(1)}, u32[]{:S(2)}, u32[]{:S(2)}) collective-permute-start(bf16[48,6144]{1,0:T(8,128)(2,1)S(1)} %get-tuple-element.109.refs_11_), channel_id=1, source_target_pairs={{0,4},{1,5},{4,8},{5,9},{8,12},{9,13},{12,14},{13,15},{14,10},{15,... | collective-permute-start | bytes 1769480 | tf_op jit(solution)/shard_map/ppermute | solution.py:231
  77.3 11.3 %collective-permute-start.13 = (bf16[48,6144]{1,0:T(8,128)(2,1)S(1)}, bf16[48,6144]{1,0:T(8,128)(2,1)S(1)}, u32[]{:S(2)}, u32[]{:S(2)}) collective-permute-start(bf16[48,6144]{1,0:T(8,128)(2,1)S(1)} %get-tuple-element.115.refs_13_), channel_id=1, source_target_pairs={{0,4},{1,5},{4,8},{5,9},{8,12},{9,13},{12,14},{13,15},{14,10},{15,... | collective-permute-start | bytes 1769480 | tf_op jit(solution)/shard_map/ppermute | solution.py:231
  78.9 7.8 %collective-permute-start.12 = (bf16[32,6144]{1,0:T(8,128)(2,1)S(1)}, bf16[32,6144]{1,0:T(8,128)(2,1)S(1)}, u32[]{:S(2)}, u32[]{:S(2)}) collective-permute-start(bf16[32,6144]{1,0:T(8,128)(2,1)S(1)} %get-tuple-element.114.refs_6_), channel_id=1, source_target_pairs={{0,2},{1,3},{4,0},{5,1},{8,4},{9,5},{12,8},{13,9},{14,12},{15,13},... | collective-permute-start | bytes 1179656 | tf_op jit(solution)/shard_map/ppermute | solution.py:231
  88.6 10.5 %slice-start = ((s8[5898240]{0:T(1024)(128)(4,1)}), s8[4194304]{0:T(1024)(128)(4,1)S(1)}, s32[]{:S(2)}) async-start(s8[5898240]{0:T(1024)(128)(4,1)} %bitcast.13), calls=%async_computation | async-start | bytes 8388608
  88.6 10.5 %slice-start.1 = ((s8[5898240]{0:T(1024)(128)(4,1)}), s8[1703936]{0:T(1024)(128)(4,1)S(1)}, s32[]{:S(2)}) async-start(s8[5898240]{0:T(1024)(128)(4,1)} %bitcast.13), calls=%async_computation.1 | async-start | bytes 3407872
  89.1 5.7 %collective-permute-start.15 = (bf16[256,6144]{1,0:T(8,128)(2,1)S(1)}, bf16[256,6144]{1,0:T(8,128)(2,1)S(1)}, u32[]{:S(2)}, u32[]{:S(2)}) collective-permute-start(bf16[256,6144]{1,0:T(8,128)(2,1)S(1)} %get-tuple-element.119.own_ref), channel_id=1, source_target_pairs={{0,1},{1,0},{2,3},{3,2},{4,5},{5,4},{6,7},{7,6},{8,9},{9,8},{10,11... | collective-permute-start | bytes 9437192 | tf_op jit(solution)/shard_map/ppermute | solution.py:231
  94.9 17.8 %collective-permute-start.22 = (bf16[384,6144]{1,0:T(8,128)(2,1)S(1)}, bf16[384,6144]{1,0:T(8,128)(2,1)S(1)}, u32[]{:S(2)}, u32[]{:S(2)}) collective-permute-start(bf16[384,6144]{1,0:T(8,128)(2,1)S(1)} %get-tuple-element.127.own_ref), channel_id=1, source_target_pairs={{0,1},{1,0},{2,3},{3,2},{4,5},{5,4},{6,7},{7,6},{8,9},{9,8},{10,11... | collective-permute-start | bytes 14155784 | tf_op jit(solution)/shard_map/ppermute | solution.py:231
  95.0 14.1 %collective-permute-start.18 = (bf16[384,640]{1,0:T(8,128)(2,1)S(1)}, bf16[384,640]{1,0:T(8,128)(2,1)S(1)}, u32[]{:S(2)}, u32[]{:S(2)}) collective-permute-start(bf16[384,640]{1,0:T(8,128)(2,1)S(1)} %get-tuple-element.124), channel_id=1, source_target_pairs={{0,4},{1,5},{4,8},{5,9},{8,12},{9,13},{12,14},{13,15},{14,10},{15,... | collective-permute-start | bytes 1474568 | tf_op jit(solution)/shard_map/ppermute | solution.py:231
  96.6 14.1 %collective-permute-start.19 = (bf16[384,640]{1,0:T(8,128)(2,1)S(1)}, bf16[384,640]{1,0:T(8,128)(2,1)S(1)}, u32[]{:S(2)}, u32[]{:S(2)}) collective-permute-start(bf16[384,640]{1,0:T(8,128)(2,1)S(1)} %get-tuple-element.124), channel_id=1, source_target_pairs={{0,2},{1,3},{4,0},{5,1},{8,4},{9,5},{12,8},{13,9},{14,12},{15,13},... | collective-permute-start | bytes 1474568 | tf_op jit(solution)/shard_map/ppermute | solution.py:231
  97.0 22.5 %collective-permute-start.16 = (bf16[384,640]{1,0:T(8,128)(2,1)S(1)}, bf16[384,640]{1,0:T(8,128)(2,1)S(1)}, u32[]{:S(2)}, u32[]{:S(2)}) collective-permute-start(bf16[384,640]{1,0:T(8,128)(2,1)S(1)} %get-tuple-element.123), channel_id=1, source_target_pairs={{0,4},{1,5},{4,8},{5,9},{8,12},{9,13},{12,14},{13,15},{14,10},{15,... | collective-permute-start | bytes 1474568 | tf_op jit(solution)/shard_map/ppermute | solution.py:231
  98.6 22.6 %collective-permute-start.17 = (bf16[384,640]{1,0:T(8,128)(2,1)S(1)}, bf16[384,640]{1,0:T(8,128)(2,1)S(1)}, u32[]{:S(2)}, u32[]{:S(2)}) collective-permute-start(bf16[384,640]{1,0:T(8,128)(2,1)S(1)} %get-tuple-element.123), channel_id=1, source_target_pairs={{0,2},{1,3},{4,0},{5,1},{8,4},{9,5},{12,8},{13,9},{14,12},{15,13},... | collective-permute-start | bytes 1474568 | tf_op jit(solution)/shard_map/ppermute | solution.py:231
  110.7 11.3 %collective-permute-start.20 = (bf16[272,256]{1,0:T(8,128)(2,1)S(1)}, bf16[272,256]{1,0:T(8,128)(2,1)S(1)}, u32[]{:S(2)}, u32[]{:S(2)}) collective-permute-start(bf16[272,256]{1,0:T(8,128)(2,1)S(1)} %get-tuple-element.126.refs_2_), channel_id=1, source_target_pairs={{0,4},{1,5},{4,8},{5,9},{8,12},{9,13},{12,14},{13,15},{14,10},{15,... | collective-permute-start | bytes 417800 | tf_op jit(solution)/shard_map/ppermute | solution.py:231
  112.2 11.1 %collective-permute-start.21 = (bf16[272,256]{1,0:T(8,128)(2,1)S(1)}, bf16[272,256]{1,0:T(8,128)(2,1)S(1)}, u32[]{:S(2)}, u32[]{:S(2)}) collective-permute-start(bf16[272,256]{1,0:T(8,128)(2,1)S(1)} %get-tuple-element.126.refs_2_), channel_id=1, source_target_pairs={{0,2},{1,3},{4,0},{5,1},{8,4},{9,5},{12,8},{13,9},{14,12},{15,13},... | collective-permute-start | bytes 417800 | tf_op jit(solution)/shard_map/ppermute | solution.py:231
  123.4 19.7 %collective-permute-start.29 = (bf16[240,768]{1,0:T(8,128)(2,1)S(1)}, bf16[240,768]{1,0:T(8,128)(2,1)S(1)}, u32[]{:S(2)}, u32[]{:S(2)}) collective-permute-start(bf16[240,768]{1,0:T(8,128)(2,1)S(1)} %get-tuple-element.138), channel_id=1, source_target_pairs={{0,16},{16,0},{1,17},{17,1},{2,18},{18,2},{3,19},{19,3},{4,20},{20... | collective-permute-start | bytes 1105928 | tf_op jit(solution)/shard_map/ppermute | solution.py:235
  124.9 18.7 %collective-permute-start.25 = (bf16[384,640]{1,0:T(8,128)(2,1)S(1)}, bf16[384,640]{1,0:T(8,128)(2,1)S(1)}, u32[]{:S(2)}, u32[]{:S(2)}) collective-permute-start(bf16[384,640]{1,0:T(8,128)(2,1)S(1)} %get-tuple-element.134.refs_1_), channel_id=1, source_target_pairs={{0,4},{1,5},{4,8},{5,9},{8,12},{9,13},{12,14},{13,15},{14,10},{15,... | collective-permute-start | bytes 1474568 | tf_op jit(solution)/shard_map/ppermute | solution.py:231
  126.5 13.5 %collective-permute-start.27 = (bf16[272,256]{1,0:T(8,128)(2,1)S(1)}, bf16[272,256]{1,0:T(8,128)(2,1)S(1)}, u32[]{:S(2)}, u32[]{:S(2)}) collective-permute-start(bf16[272,256]{1,0:T(8,128)(2,1)S(1)} %get-tuple-element.136.refs_3_), channel_id=1, source_target_pairs={{0,4},{1,5},{4,8},{5,9},{8,12},{9,13},{12,14},{13,15},{14,10},{15,... | collective-permute-start | bytes 417800 | tf_op jit(solution)/shard_map/ppermute | solution.py:231
  128.0 15.6 %collective-permute-start.26 = (bf16[384,640]{1,0:T(8,128)(2,1)S(1)}, bf16[384,640]{1,0:T(8,128)(2,1)S(1)}, u32[]{:S(2)}, u32[]{:S(2)}) collective-permute-start(bf16[384,640]{1,0:T(8,128)(2,1)S(1)} %get-tuple-element.135.refs_4_), channel_id=1, source_target_pairs={{0,2},{1,3},{4,0},{5,1},{8,4},{9,5},{12,8},{13,9},{14,12},{15,13},... | collective-permute-start | bytes 1474568 | tf_op jit(solution)/shard_map/ppermute | solution.py:231
  128.5 14.0 %collective-permute-start.28 = (bf16[272,256]{1,0:T(8,128)(2,1)S(1)}, bf16[272,256]{1,0:T(8,128)(2,1)S(1)}, u32[]{:S(2)}, u32[]{:S(2)}) collective-permute-start(bf16[272,256]{1,0:T(8,128)(2,1)S(1)} %get-tuple-element.137.refs_4_), channel_id=1, source_target_pairs={{0,2},{1,3},{4,0},{5,1},{8,4},{9,5},{12,8},{13,9},{14,12},{15,13},... | collective-permute-start | bytes 417800 | tf_op jit(solution)/shard_map/ppermute | solution.py:231
  140.0 12.7 %collective-permute-start.23 = (bf16[384,640]{1,0:T(8,128)(2,1)S(1)}, bf16[384,640]{1,0:T(8,128)(2,1)S(1)}, u32[]{:S(2)}, u32[]{:S(2)}) collective-permute-start(bf16[384,640]{1,0:T(8,128)(2,1)S(1)} %get-tuple-element.132.refs_2_), channel_id=1, source_target_pairs={{0,4},{1,5},{4,8},{5,9},{8,12},{9,13},{12,14},{13,15},{14,10},{15,... | collective-permute-start | bytes 1474568 | tf_op jit(solution)/shard_map/ppermute | solution.py:231
  142.5 12.1 %collective-permute-start.24 = (bf16[384,640]{1,0:T(8,128)(2,1)S(1)}, bf16[384,640]{1,0:T(8,128)(2,1)S(1)}, u32[]{:S(2)}, u32[]{:S(2)}) collective-permute-start(bf16[384,640]{1,0:T(8,128)(2,1)S(1)} %get-tuple-element.133.refs_5_), channel_id=1, source_target_pairs={{0,2},{1,3},{4,0},{5,1},{8,4},{9,5},{12,8},{13,9},{14,12},{15,13},... | collective-permute-start | bytes 1474568 | tf_op jit(solution)/shard_map/ppermute | solution.py:231
  143.1 28.8 %copy-start.3 = (s32[1,240]{1,0:T(1,128)S(1)}, s32[1,240]{1,0:T(1,128)}, u32[]{:S(2)}) copy-start(s32[1,240]{1,0:T(1,128)} %row_ref.1) | copy-start | bytes 2884
  143.1 28.8 %copy-start.4 = (s32[1,6]{1,0:T(1,128)S(1)}, s32[1,6]{1,0:T(1,128)}, u32[]{:S(2)}) copy-start(s32[1,6]{1,0:T(1,128)} %param.15) | copy-start | bytes 76
  143.1 8.2 %collective-permute-start.32 = (bf16[1536,128]{1,0:T(8,128)(2,1)S(1)}, bf16[1536,128]{1,0:T(8,128)(2,1)S(1)}, u32[]{:S(2)}, u32[]{:S(2)}) collective-permute-start(bf16[1536,128]{1,0:T(8,128)(2,1)S(1)} %get-tuple-element.141), channel_id=1, source_target_pairs={{0,16},{16,0},{1,17},{17,1},{2,18},{18,2},{3,19},{19,3},{4,20},{20... | collective-permute-start | bytes 1179656 | tf_op jit(solution)/shard_map/ppermute | solution.py:235
  143.6 11.0 %collective-permute-start.30 = (bf16[272,256]{1,0:T(8,128)(2,1)S(1)}, bf16[272,256]{1,0:T(8,128)(2,1)S(1)}, u32[]{:S(2)}, u32[]{:S(2)}) collective-permute-start(bf16[272,256]{1,0:T(8,128)(2,1)S(1)} %get-tuple-element.139.refs_5_), channel_id=1, source_target_pairs={{0,4},{1,5},{4,8},{5,9},{8,12},{9,13},{12,14},{13,15},{14,10},{15,... | collective-permute-start | bytes 417800 | tf_op jit(solution)/shard_map/ppermute | solution.py:231
  145.1 11.0 %collective-permute-start.31 = (bf16[272,256]{1,0:T(8,128)(2,1)S(1)}, bf16[272,256]{1,0:T(8,128)(2,1)S(1)}, u32[]{:S(2)}, u32[]{:S(2)}) collective-permute-start(bf16[272,256]{1,0:T(8,128)(2,1)S(1)} %get-tuple-element.140.refs_6_), channel_id=1, source_target_pairs={{0,2},{1,3},{4,0},{5,1},{8,4},{9,5},{12,8},{13,9},{14,12},{15,13},... | collective-permute-start | bytes 417800 | tf_op jit(solution)/shard_map/ppermute | solution.py:231
  156.2 12.7 %collective-permute-start.33 = (bf16[384,640]{1,0:T(8,128)(2,1)S(1)}, bf16[384,640]{1,0:T(8,128)(2,1)S(1)}, u32[]{:S(2)}, u32[]{:S(2)}) collective-permute-start(bf16[384,640]{1,0:T(8,128)(2,1)S(1)} %get-tuple-element.144.refs_6_), channel_id=1, source_target_pairs={{0,4},{1,5},{4,8},{5,9},{8,12},{9,13},{12,14},{13,15},{14,10},{15,... | collective-permute-start | bytes 1474568 | tf_op jit(solution)/shard_map/ppermute | solution.py:231
  157.1 11.8 %collective-permute-start.34 = (bf16[384,640]{1,0:T(8,128)(2,1)S(1)}, bf16[384,640]{1,0:T(8,128)(2,1)S(1)}, u32[]{:S(2)}, u32[]{:S(2)}) collective-permute-start(bf16[384,640]{1,0:T(8,128)(2,1)S(1)} %get-tuple-element.145.refs_9_), channel_id=1, source_target_pairs={{0,2},{1,3},{4,0},{5,1},{8,4},{9,5},{12,8},{13,9},{14,12},{15,13},... | collective-permute-start | bytes 1474568 | tf_op jit(solution)/shard_map/ppermute | solution.py:231
  158.3 10.6 %collective-permute-start.35 = (bf16[272,256]{1,0:T(8,128)(2,1)S(1)}, bf16[272,256]{1,0:T(8,128)(2,1)S(1)}, u32[]{:S(2)}, u32[]{:S(2)}) collective-permute-start(bf16[272,256]{1,0:T(8,128)(2,1)S(1)} %get-tuple-element.146.refs_7_), channel_id=1, source_target_pairs={{0,4},{1,5},{4,8},{5,9},{8,12},{9,13},{12,14},{13,15},{14,10},{15,... | collective-permute-start | bytes 417800 | tf_op jit(solution)/shard_map/ppermute | solution.py:231
  169.0 19.3 %copy-start = (bf16[6,128,1,768]{3,1,2,0:T(8,128)(2,1)S(1)}, bf16[6,128,1,768]{3,1,2,0:T(8,128)(2,1)}, u32[]{:S(2)}) copy-start(bf16[6,128,1,768]{3,1,2,0:T(8,128)(2,1)} %param.14) | copy-start | bytes 3538948
  169.1 2.8 %collective-permute-start.41 = (bf16[2176,256]{1,0:T(8,128)(2,1)S(1)}, bf16[2176,256]{1,0:T(8,128)(2,1)S(1)}, u32[]{:S(2)}, u32[]{:S(2)}) collective-permute-start(bf16[2176,256]{1,0:T(8,128)(2,1)S(1)} %get-tuple-element.156.refs_0_), channel_id=1, source_target_pairs={{0,1},{1,0},{2,3},{3,2},{4,5},{5,4},{6,7},{7,6},{8,9},{9,8},{10,11... | collective-permute-start | bytes 3342344 | tf_op jit(solution)/shard_map/ppermute | solution.py:231
  169.1 13.6 %collective-permute-start.38 = (bf16[384,640]{1,0:T(8,128)(2,1)S(1)}, bf16[384,640]{1,0:T(8,128)(2,1)S(1)}, u32[]{:S(2)}, u32[]{:S(2)}) collective-permute-start(bf16[384,640]{1,0:T(8,128)(2,1)S(1)} %get-tuple-element.150.refs_7_), channel_id=1, source_target_pairs={{0,4},{1,5},{4,8},{5,9},{8,12},{9,13},{12,14},{13,15},{14,10},{15,... | collective-permute-start | bytes 1474568 | tf_op jit(solution)/shard_map/ppermute | solution.py:231
  170.3 13.3 %collective-permute-start.39 = (bf16[384,640]{1,0:T(8,128)(2,1)S(1)}, bf16[384,640]{1,0:T(8,128)(2,1)S(1)}, u32[]{:S(2)}, u32[]{:S(2)}) collective-permute-start(bf16[384,640]{1,0:T(8,128)(2,1)S(1)} %get-tuple-element.151.refs_10_), channel_id=1, source_target_pairs={{0,2},{1,3},{4,0},{5,1},{8,4},{9,5},{12,8},{13,9},{14,12},{15,13},... | collective-permute-start | bytes 1474568 | tf_op jit(solution)/shard_map/ppermute | solution.py:231
  171.2 10.9 %collective-permute-start.40 = (bf16[1536,128]{1,0:T(8,128)(2,1)S(1)}, bf16[1536,128]{1,0:T(8,128)(2,1)S(1)}, u32[]{:S(2)}, u32[]{:S(2)}) collective-permute-start(bf16[1536,128]{1,0:T(8,128)(2,1)S(1)} %get-tuple-element.152), channel_id=1, source_target_pairs={{0,16},{16,0},{1,17},{17,1},{2,18},{18,2},{3,19},{19,3},{4,20},{20... | collective-permute-start | bytes 1179656 | tf_op jit(solution)/shard_map/ppermute | solution.py:235
  178.1 5.5 %collective-permute-start.42 = (bf16[240,768]{1,0:T(8,128)(2,1)S(1)}, bf16[240,768]{1,0:T(8,128)(2,1)S(1)}, u32[]{:S(2)}, u32[]{:S(2)}) collective-permute-start(bf16[240,768]{1,0:T(8,128)(2,1)S(1)} %attend.1.att_ref), channel_id=1, source_target_pairs={{0,1},{1,0},{2,3},{3,2},{4,5},{5,4},{6,7},{7,6},{8,9},{9,8},{10,11... | collective-permute-start | bytes 1105928 | tf_op jit(solution)/shard_map/ppermute | solution.py:231
  183.7 13.4 %collective-permute-start.45 = (bf16[1536,128]{1,0:T(8,128)(2,1)S(1)}, bf16[1536,128]{1,0:T(8,128)(2,1)S(1)}, u32[]{:S(2)}, u32[]{:S(2)}) collective-permute-start(bf16[1536,128]{1,0:T(8,128)(2,1)S(1)} %get-tuple-element.163), channel_id=1, source_target_pairs={{0,16},{16,0},{1,17},{17,1},{2,18},{18,2},{3,19},{19,3},{4,20},{20... | collective-permute-start | bytes 1179656 | tf_op jit(solution)/shard_map/ppermute | solution.py:235
  184.3 11.0 %collective-permute-start.36 = (bf16[192,640]{1,0:T(8,128)(2,1)S(1)}, bf16[192,640]{1,0:T(8,128)(2,1)S(1)}, u32[]{:S(2)}, u32[]{:S(2)}) collective-permute-start(bf16[192,640]{1,0:T(8,128)(2,1)S(1)} %get-tuple-element.148), channel_id=1, source_target_pairs={{0,4},{1,5},{4,8},{5,9},{8,12},{9,13},{12,14},{13,15},{14,10},{15,... | collective-permute-start | bytes 737288 | tf_op jit(solution)/shard_map/ppermute | solution.py:231
  185.2 10.0 %collective-permute-start.37 = (bf16[192,640]{1,0:T(8,128)(2,1)S(1)}, bf16[192,640]{1,0:T(8,128)(2,1)S(1)}, u32[]{:S(2)}, u32[]{:S(2)}) collective-permute-start(bf16[192,640]{1,0:T(8,128)(2,1)S(1)} %get-tuple-element.149), channel_id=1, source_target_pairs={{0,2},{1,3},{4,0},{5,1},{8,4},{9,5},{12,8},{13,9},{14,12},{15,13},... | collective-permute-start | bytes 737288 | tf_op jit(solution)/shard_map/ppermute | solution.py:231
  186.3 10.2 %collective-permute-start.43 = (bf16[192,640]{1,0:T(8,128)(2,1)S(1)}, bf16[192,640]{1,0:T(8,128)(2,1)S(1)}, u32[]{:S(2)}, u32[]{:S(2)}) collective-permute-start(bf16[192,640]{1,0:T(8,128)(2,1)S(1)} %get-tuple-element.161), channel_id=1, source_target_pairs={{0,4},{1,5},{4,8},{5,9},{8,12},{9,13},{12,14},{13,15},{14,10},{15,... | collective-permute-start | bytes 737288 | tf_op jit(solution)/shard_map/ppermute | solution.py:231
  187.2 9.9 %collective-permute-start.44 = (bf16[192,640]{1,0:T(8,128)(2,1)S(1)}, bf16[192,640]{1,0:T(8,128)(2,1)S(1)}, u32[]{:S(2)}, u32[]{:S(2)}) collective-permute-start(bf16[192,640]{1,0:T(8,128)(2,1)S(1)} %get-tuple-element.162), channel_id=1, source_target_pairs={{0,2},{1,3},{4,0},{5,1},{8,4},{9,5},{12,8},{13,9},{14,12},{15,13},... | collective-permute-start | bytes 737288 | tf_op jit(solution)/shard_map/ppermute | solution.py:231
  197.1 7.4 %collective-permute-start.47 = (bf16[5,240,768]{2,1,0:T(8,128)(2,1)S(1)}, bf16[5,240,768]{2,1,0:T(8,128)(2,1)S(1)}, u32[]{:S(2)}, u32[]{:S(2)}) collective-permute-start(bf16[5,240,768]{2,1,0:T(8,128)(2,1)S(1)} %get-tuple-element.174), channel_id=1, source_target_pairs={{0,1},{1,0},{2,3},{3,2},{4,5},{5,4},{6,7},{7,6},{8,9},{9,8},{10,11... | collective-permute-start | bytes 5529608 | tf_op jit(solution)/shard_map/ppermute | solution.py:231
  197.2 7.4 %collective-permute-start.46 = (bf16[768,128]{1,0:T(8,128)(2,1)S(1)}, bf16[768,128]{1,0:T(8,128)(2,1)S(1)}, u32[]{:S(2)}, u32[]{:S(2)}) collective-permute-start(bf16[768,128]{1,0:T(8,128)(2,1)S(1)} %get-tuple-element.173), channel_id=1, source_target_pairs={{0,16},{16,0},{1,17},{17,1},{2,18},{18,2},{3,19},{19,3},{4,20},{20... | collective-permute-start | bytes 589832 | tf_op jit(solution)/shard_map/ppermute | solution.py:235
  204.5 4.2 %collective-permute-start.48 = (bf16[2,240,768]{2,1,0:T(8,128)(2,1)S(1)}, bf16[2,240,768]{2,1,0:T(8,128)(2,1)S(1)}, u32[]{:S(2)}, u32[]{:S(2)}) collective-permute-start(bf16[2,240,768]{2,1,0:T(8,128)(2,1)S(1)} %get-tuple-element.182), channel_id=1, source_target_pairs={{0,1},{1,0},{2,3},{3,2},{4,5},{5,4},{6,7},{7,6},{8,9},{9,8},{10,11... | collective-permute-start | bytes 2211848 | tf_op jit(solution)/shard_map/ppermute | solution.py:231
  206.8 1.9 collective-permute-start.49

commit v4 on v3

--- a/solution.py
+++ b/solution.py
@@ -192,9 +192,31 @@
     )(*in_vmem(blocks))
 
 
-def copy_kernel(plan, facts, *refs):
+def facts_kernel(group_ref, me_ref, len_ref, slot_ref, table_ref, out_ref):
+    out_ref[GROUP] = group_ref[0]
+    out_ref[LENGTH] = len_ref[0]
+    for p in range(CHIPS * CORES):
+        out_ref[ORDER + p] = slot_ref[me_ref[0] * CHIPS * CORES + p]
+    for p in range(table_ref.shape[0]):
+        out_ref[TABLE + p] = table_ref[p]
+
+
+def list_facts(group, me, lengths, block_table):
+    smem = pl.BlockSpec(memory_space=pltpu.SMEM)
+    return pl.pallas_call(
+        facts_kernel,
+        in_specs=[smem] * 5,
+        out_specs=smem,
+        out_shape=jax.ShapeDtypeStruct((TABLE + block_table.shape[0],), jnp.int32),
+        compiler_params=pltpu.CompilerParams(vmem_limit_bytes=2**20),
+        name="list_facts",
+    )(group, me, lengths, jnp.asarray(slot_table().reshape(-1)), block_table)
+
+
+def copy_kernel(plan, count, group_ref, *refs):
     sem = refs[-1]
-    group = facts[GROUP]
+    refs = refs[count:]
+    group = group_ref[0]
     copies = []
     for n, (source, out, row, column, flip, shape) in enumerate(plan):
         side = 1 - group if flip else group
@@ -209,13 +231,13 @@
         copy.wait()
 
 
-def take_parts(facts, sources, outs, plan):
+def take_parts(where, sources, outs, plan):
     count = len(sources)
     plan = [(s, count + o, *rest) for s, o, *rest in plan]
     return pl.pallas_call(
-        partial(copy_kernel, plan),
+        partial(copy_kernel, plan, len(where) - 1),
         grid_spec=pltpu.PrefetchScalarGridSpec(
-            num_scalar_prefetch=1,
+            num_scalar_prefetch=len(where),
             grid=(),
             in_specs=[pl.BlockSpec(memory_space=pl.ANY)] * count,
             out_specs=[pl.BlockSpec(memory_space=pltpu.VMEM)] * len(outs),
@@ -224,7 +246,7 @@
         out_shape=[pltpu.VMEM(shape, jnp.bfloat16) for shape in outs],
         compiler_params=pltpu.CompilerParams(vmem_limit_bytes=2**20),
         name="take_parts",
-    )(facts, *in_hbm(sources))
+    )(*where, *in_hbm(sources))
 
 
 def move(block, pairs):
@@ -583,7 +605,7 @@
             scratch_shapes=[
                 pltpu.VMEM((len(plan), depth, columns), jnp.bfloat16),
                 pltpu.VMEM((len(plan), rows, columns), jnp.bfloat16),
-                pltpu.SemaphoreType.DMA((len(plan), 9)),
+                pltpu.SemaphoreType.DMA((len(plan), 10)),
                 pltpu.SemaphoreType.DMA((len(plan),)),
                 pltpu.SemaphoreType.DMA((max(placed, 1),)),
             ],
@@ -619,15 +641,14 @@
     depth = heads * HD
     columns = w_out.shape[3]
     share = columns // 6
-    order = jnp.asarray(slot_table())[lax.axis_index("serve")]
-    facts = jnp.concatenate([group[None].astype(jnp.int32), span_lengths, order, block_table])
+    where = (group[None].astype(jnp.int32), lax.axis_index("serve")[None].astype(jnp.int32))
 
     query_rows = w_query.transpose(1, 2, 0).reshape(heads * part, width)
     kv_rows = w_kv.transpose(1, 2, 0).reshape(2 * part, width)
     own_out = w_out.reshape(depth, columns)
     cut = heads * part
     k0, q0 = take_parts(
-        facts,
+        (*where, span_lengths),
         [query_rows, kv_rows],
         [(4 * part, half), (cut, half)],
         [
@@ -638,7 +659,7 @@
     )
     cut = depth // 2
     theirs, top0, low0 = take_parts(
-        facts,
+        where,
         [recomp_states[0], own_out, k0],
         [(rows, half)] + [(cut, columns - share)] * 2,
         [(0, 0, (0, 0), (0, 0), True, (rows, half))]
@@ -648,6 +669,7 @@
             for n in range(2)
         ],
     )
+    facts = list_facts(*where, span_lengths, block_table)
     ka1, kb1 = together(*pair(k0, k0))
     qa1, qb1, ka1 = together(*pair(q0, q0), ka1)
     ka2, kb2, qa1 = together(*pair(ka1, kb1), qa1)
@@ -661,42 +683,42 @@
     *_, other_rows, low0, keys, queries = together(
         *keys, *queries, across(theirs), low0, packs=(key_stack, query_stack)
     )
-    keys2, queries = lax.optimization_barrier((*swap(keys), queries))
-    queries = (queries, *swap(queries))
-
-    span0, new_kv, cache = project_kv(facts, span_states, recomp_states, (keys, keys2))
-    ta1, tb1, span0 = together(*pair(top0, top0), span0)
-    mine, theirs_part = project_query(facts, recomp_states, other_rows, queries, depth)
+    keys = (keys, *swap(keys))
+
+    span0, new_kv, cache = project_kv(facts, span_states, recomp_states, keys)
+    sa1, sb1 = pair(span0, span0)
+    sa2, sb2 = pair(sa1, sb1)
+    sa3, sb3 = pair(sa2, sb2)
+    ta1, tb1, queries = together(*pair(top0, top0), queries)
+    mine, theirs_part = project_query(
+        facts, recomp_states, other_rows, (queries, *swap(queries)), depth
+    )
     sides = lambda *found: (share, [(n, 0, cut) for n in found])
-    la1, lb1, sa1, sb1, theirs_part, ta1, tb1, send1 = together(
-        *pair(low0, low0), *pair(span0, span0), theirs_part, ta1, tb1, packs=(sides(5, 0, 6, 1),)
-    )
-    ta2, tb2, sa2, sb2, other = together(*pair(ta1, tb1), *pair(sa1, sb1), across(theirs_part))
-    la2, lb2, sa3, sb3, x1, ta2, tb2, send2 = together(
-        *pair(la1, lb1), *pair(sa2, sb2), across(send1), ta2, tb2, packs=(sides(5, 0, 6, 1),)
+    la1, lb1, ta1, tb1, send1 = together(
+        *pair(low0, low0), ta1, tb1, packs=(sides(2, 0, 3, 1),)
+    )
+    ta2, tb2, la1 = together(*pair(ta1, tb1), la1)
+    la2, lb2, x1, ta2, tb2, send2 = together(
+        *pair(la1, lb1), across(send1), ta2, tb2, packs=(sides(3, 0, 4, 1),)
     )
     spans = (span0, sa1, sb1, sa2, sb2, sa3, sb3, move(sa3, AHEAD))
-    stack = (2 * HD, [(2 + n, 0, span0.shape[0]) for n in range(CHIPS)])
-    quarter = lambda n, first: (columns - share, [(n, first, cut // 2)])
-    ta3, tb3, *_, spans, top_ahead, top_back = together(
-        *pair(ta2, tb2), *spans, packs=(stack, quarter(0, 0), quarter(1, cut // 2))
-    )
+    stack = (2 * HD, [(n, 0, span0.shape[0]) for n in range(CHIPS)])
+    *_, spans = together(*spans, packs=(stack,))
+    other = across(theirs_part)
     attended = attend(
         span_map[0], facts, mine, other, new_kv, recompute_idx, (spans, *swap(spans))
     )
-    la3, lb3, x2, *attended = lax.optimization_barrier(
-        (*pair(la2, lb2), across(send2), attended, *swap(attended))
-    )
-    la3, lb3, ta3, tb3, send3, low_ahead, low_back = together(
-        la3,
-        lb3,
+    attended = (attended, *swap(attended))
+    quarter = lambda n, first: (columns - share, [(n, first, cut // 2)])
+    ta3, tb3, top_ahead, top_back = together(
+        *pair(ta2, tb2), packs=(quarter(0, 0), quarter(1, cut // 2))
+    )
+    la3, lb3, ta3, tb3, x2, send3, low_ahead, low_back = together(
+        *pair(la2, lb2),
         ta3,
         tb3,
-        packs=(
-            sides(2, 0, 3, 1),
-            quarter(0, 0),
-            quarter(1, cut // 2),
-        ),
+        across(send2),
+        packs=(sides(2, 0, 3, 1), quarter(0, 0), quarter(1, cut // 2)),
     )
 
     def near(slot, top, low, side, first):
@@ -714,15 +736,17 @@
     t4a, t4b, l4a, l4b, x3, sent1 = lax.optimization_barrier(
         (*pair(top_ahead, top_back), *pair(low_ahead, low_back), across(send3), sent1)
     )
-    t4a, t4b, l4a, l4b, send4 = together(
-        t4a, t4b, l4a, l4b, packs=((share, [(n, 0, cut // 2) for n in range(4)]),)
+    x3, last_ahead, last_back = together(
+        x3, packs=((share, [(0, 0, cut)]), (share, [(0, depth + cut, cut)]))
     )
     late = [near(5, ta3, la3, x3, 0), near(6, tb3, lb3, x3, 1)]
     result, sent2 = project_output(facts, attended, result, late, [], width_out)
-    x4, arrived1, sent2 = lax.optimization_barrier((across(send4), *swap(sent1), sent2))
+    x4a, x4b, arrived1, sent2 = lax.optimization_barrier(
+        (*pair(last_ahead, last_back), *swap(sent1), sent2)
+    )
     arrived = [(arrived1, (0, 1, 2, 3, 4))]
     quarters = [(block, 0, n * cut // 2, cut // 2) for n, block in enumerate((t4a, t4b, l4a, l4b))]
-    far = (7, [*quarters, (x4, 0, 0, depth)])
+    far = (7, [*quarters, (x4a, 0, 0, cut), (x4b, 0, cut, cut)])
     result, sent3 = project_output(
         facts, attended, result, [far], arrived, width_out
     )

time: 211 us -> 203 us (0.962)
  waiting for transfers between devices: 123 us -> 114 us
  starting transfers between devices: 46.2 us -> 49.8 us
    ppermute x6 -> x5, waiting for transfers between devices: 11.8 us -> 4.03 us  [across(): return lax.ppermute(block, 'groups', ACROSS)]
    ppermute x44 -> x46, starting transfers between devices: 39.4 us -> 42.3 us  [move(): return lax.ppermute(block, 'serve', pairs)]
    ppermute x44 -> x46, waiting for transfers between devices: 111 us -> 110 us  [move(): return lax.ppermute(block, 'serve', pairs)]
    ppermute x6 -> x5, starting transfers between devices: 6.78 us -> 7.54 us  [across(): return lax.ppermute(block, 'groups', ACROSS)]
    pallas_call x2 -> x3, Pallas kernels: 4.76 us -> 4.57 us  [the longest x2 3.4 us: take_parts(): pl.pallas_call(partial(copy_kernel, plan, len(where) - 1), grid_spec=pltp...]
  transfers between devices with their start and end apart: 50 -> 51, of which waited for: 32 -> 23; matrix products, arithmetic and copies ran while one was open for 0% -> 0% of each run, Pallas kernels for 16% -> 17%
where the time goes in v4:
time: 203 us
  waiting for transfers between devices  114 us (56%)
  starting transfers between devices  49.8 us (25%)
  Pallas kernels  37.9 us (19%)
    ppermute x46, waiting for transfers between devices, move(): return lax.ppermute(block, 'serve', pairs)  110 us
    ppermute x46, starting transfers between devices, move(): return lax.ppermute(block, 'serve', pairs)  42.3 us
    pallas_call x3, Pallas kernels, project_output(): pl.pallas_call(partial(output_kernel, plan, arrived), grid_spec=pltpu.Pre...  12.8 us
    ppermute x5, starting transfers between devices, across(): return lax.ppermute(block, 'groups', ACROSS)  7.54 us
    pallas_call x1, Pallas kernels, project_query(): pl.pallas_call(query_kernel, grid_spec=pltpu.PrefetchScalarGridSpec(num_s...  6.21 us
    pallas_call x1, Pallas kernels, attend(): pl.pallas_call(attend_kernel, grid_spec=pltpu.PrefetchScalarGridSpec(num_...  6.2 us
    pallas_call x1, Pallas kernels, project_kv(): pl.pallas_call(kv_kernel, grid_spec=pltpu.PrefetchScalarGridSpec(num_scal...  5.66 us
  transfers between devices with their start and end apart: 51, of which 23 were waited for; matrix products, arithmetic and copies ran while one was open for 0% of the time, Pallas kernels for 17%

profile of v4, /device:TPU:0, one launch (start us, length us, event | category | flops | bytes accessed | tf_op | source)
XLA Modules:
  0.0 203.3 jit_solution(13675890653409717953)
XLA Ops:
  1.3 1.3 take_parts.2
  2.6 3.1 %collective-permute-start = (bf16[48,6144]{1,0:T(8,128)(2,1)S(1)}, bf16[48,6144]{1,0:T(8,128)(2,1)S(1)}, u32[]{:S(2)}, u32[]{:S(2)}) collective-permute-start(bf16[48,6144]{1,0:T(8,128)(2,1)S(1)} %get-tuple-element.84.refs_8_), channel_id=1, source_target_pairs={{0,4},{1,5},{4,8},{5,9},{8,12},{9,13},{12,14},{13,15},{14,10},{15,... | collective-permute-start | bytes 1769480 | tf_op jit(solution)/shard_map/ppermute | solution.py:253
  5.7 2.0 collective-permute-start.2
  7.7 2.1 %take_parts.3 = (bf16[240,6144]{1,0:T(8,128)(2,1)S(1)}, bf16[384,640]{1,0:T(8,128)(2,1)S(1)}, bf16[384,640]{1,0:T(8,128)(2,1)S(1)}) custom-call(s32[1]{0:T(128)} %bitcast.group_ref, s32[1]{0:T(128)} %bitcast.1.me_ref.refs_0_, bf16[240,12288]{1,0:T(8,128)(2,1)} %bitcast.11, bf16[768,768]{1,0:T(8,128)(2,1)} %bitcast.16, bf16[32,6144]{1,0:T(8,128)(2,1)} %copy-done.1), custom_call_target="tpu_custom_call" | custom-call | tf_op jit(solution)/shard_map/take_parts/pallas_call | solution.py:237
  9.8 2.0 collective-permute-start.14
  11.8 15.5 %collective-permute-done.2.refs_0_ = bf16[32,6144]{1,0:T(8,128)(2,1)S(1)} collective-permute-done((bf16[32,6144]{1,0:T(8,128)(2,1)S(1)}, bf16[32,6144]{1,0:T(8,128)(2,1)S(1)}, u32[]{:S(2)}, u32[]{:S(2)}) %collective-permute-start.2) | collective-permute-done | bytes 393248 | tf_op jit(solution)/shard_map/ppermute | solution.py:253
  27.4 1.5 collective-permute-done.3.refs_1_
  29.2 1.7 collective-permute-start.4
  31.2 9.7 %collective-permute-done.5.refs_1_ = bf16[32,6144]{1,0:T(8,128)(2,1)S(1)} collective-permute-done((bf16[32,6144]{1,0:T(8,128)(2,1)S(1)}, bf16[32,6144]{1,0:T(8,128)(2,1)S(1)}, u32[]{:S(2)}, u32[]{:S(2)}) %collective-permute-start.5) | collective-permute-done | bytes 393248 | tf_op jit(solution)/shard_map/ppermute | solution.py:253
  40.9 1.6 collective-permute-start.6
  43.0 10.6 %collective-permute-done.7.refs_1_ = bf16[48,6144]{1,0:T(8,128)(2,1)S(1)} collective-permute-done((bf16[48,6144]{1,0:T(8,128)(2,1)S(1)}, bf16[48,6144]{1,0:T(8,128)(2,1)S(1)}, u32[]{:S(2)}, u32[]{:S(2)}) %collective-permute-start.7) | collective-permute-done | bytes 589856 | tf_op jit(solution)/shard_map/ppermute | solution.py:253
  53.6 1.6 collective-permute-start.8
  55.6 6.4 %collective-permute-done.9.refs_1_ = bf16[32,6144]{1,0:T(8,128)(2,1)S(1)} collective-permute-done((bf16[32,6144]{1,0:T(8,128)(2,1)S(1)}, bf16[32,6144]{1,0:T(8,128)(2,1)S(1)}, u32[]{:S(2)}, u32[]{:S(2)}) %collective-permute-start.9) | collective-permute-done | bytes 393248 | tf_op jit(solution)/shard_map/ppermute | solution.py:253
  62.0 0.7 collective-permute-done.8.refs_0_
  62.7 1.6 collective-permute-start.10
  64.3 8.0 %collective-permute-done.11.refs_1_ = bf16[48,6144]{1,0:T(8,128)(2,1)S(1)} collective-permute-done((bf16[48,6144]{1,0:T(8,128)(2,1)S(1)}, bf16[48,6144]{1,0:T(8,128)(2,1)S(1)}, u32[]{:S(2)}, u32[]{:S(2)}) %collective-permute-start.11) | collective-permute-done | bytes 589856 | tf_op jit(solution)/shard_map/ppermute | solution.py:253
  72.3 3.1 %collective-permute-done.10.refs_0_ = bf16[48,6144]{1,0:T(8,128)(2,1)S(1)} collective-permute-done((bf16[48,6144]{1,0:T(8,128)(2,1)S(1)}, bf16[48,6144]{1,0:T(8,128)(2,1)S(1)}, u32[]{:S(2)}, u32[]{:S(2)}) %collective-permute-start.10) | collective-permute-done | bytes 589856 | tf_op jit(solution)/shard_map/ppermute | solution.py:253
  75.4 1.6 collective-permute-start.13
  76.9 1.6 collective-permute-start.18
  79.4 14.7 %collective-permute-done.12.refs_7_ = bf16[32,6144]{1,0:T(8,128)(2,1)S(1)} collective-permute-done((bf16[32,6144]{1,0:T(8,128)(2,1)S(1)}, bf16[32,6144]{1,0:T(8,128)(2,1)S(1)}, u32[]{:S(2)}, u32[]{:S(2)}) %collective-permute-start.12) | collective-permute-done | bytes 393248 | tf_op jit(solution)/shard_map/ppermute | solution.py:253
  94.2 0.5 together.21
  94.7 2.4 %collective-permute-done.18.refs_0_ = bf16[384,640]{1,0:T(8,128)(2,1)S(1)} collective-permute-done((bf16[384,640]{1,0:T(8,128)(2,1)S(1)}, bf16[384,640]{1,0:T(8,128)(2,1)S(1)}, u32[]{:S(2)}, u32[]{:S(2)}) %collective-permute-start.18) | collective-permute-done | bytes 491552 | tf_op jit(solution)/shard_map/ppermute | solution.py:253
  97.2 0.5 collective-permute-start.15
  97.7 1.6 collective-permute-start.16
  99.7 1.2 list_facts.1.facts
  100.9 8.7 %collective-permute-done.15.sib_ref = bf16[256,6144]{1,0:T(8,128)(2,1)S(1)} collective-permute-done((bf16[256,6144]{1,0:T(8,128)(2,1)S(1)}, bf16[256,6144]{1,0:T(8,128)(2,1)S(1)}, u32[]{:S(2)}, u32[]{:S(2)}) %collective-permute-start.15) | collective-permute-done | bytes 3145760 | tf_op jit(solution)/shard_map/ppermute | solution.py:253
  109.6 5.7 %project_kv.1 = (bf16[272,256]{1,0:T(8,128)(2,1)S(1)}, bf16[240,256]{1,0:T(8,128)(2,1)S(1)}, bf16[16,16,256]{2,1,0:T(8,128)(2,1)}) custom-call(s32[34]{0:T(128)S(1)} %list_facts.1.facts, bf16[1,256,12288]{2,1,0:T(8,128)(2,1)S(1)} %bitcast.15, bf16[1,240,12288]{2,1,0:T(8,128)(2,1)S(1)} %bitcast.13, bf16[256,6144]{1,0:T(8,128)(2,1)S(1)} %get-tuple-element.105.own_ref, ...), custom_call_target="tpu_custom_call" | custom-call | flops 1000 | bytes 1000 | tf_op jit(solution)/shard_map/project_kv/pallas_call | solution.py:318
  115.3 1.6 collective-permute-start.37
  117.3 3.7 %collective-permute-done.37.refs_1_ = bf16[272,256]{1,0:T(8,128)(2,1)S(1)} collective-permute-done((bf16[272,256]{1,0:T(8,128)(2,1)S(1)}, bf16[272,256]{1,0:T(8,128)(2,1)S(1)}, u32[]{:S(2)}, u32[]{:S(2)}) %collective-permute-start.37) | collective-permute-done | bytes 139296 | tf_op jit(solution)/shard_map/ppermute | solution.py:253
  121.0 1.6 collective-permute-start.39
  123.0 3.0 %collective-permute-done.39.refs_3_ = bf16[272,256]{1,0:T(8,128)(2,1)S(1)} collective-permute-done((bf16[272,256]{1,0:T(8,128)(2,1)S(1)}, bf16[272,256]{1,0:T(8,128)(2,1)S(1)}, u32[]{:S(2)}, u32[]{:S(2)}) %collective-permute-start.39) | collective-permute-done | bytes 139296 | tf_op jit(solution)/shard_map/ppermute | solution.py:253
  126.0 1.6 collective-permute-start.41
  128.1 3.4 %collective-permute-done.41.refs_5_ = bf16[272,256]{1,0:T(8,128)(2,1)S(1)} collective-permute-done((bf16[272,256]{1,0:T(8,128)(2,1)S(1)}, bf16[272,256]{1,0:T(8,128)(2,1)S(1)}, u32[]{:S(2)}, u32[]{:S(2)}) %collective-permute-start.41) | collective-permute-done | bytes 139296 | tf_op jit(solution)/shard_map/ppermute | solution.py:253
  131.5 1.6 collective-permute-start.43
  133.2 1.6 collective-permute-start.20
  135.2 2.9 %collective-permute-done.43.refs_7_ = bf16[272,256]{1,0:T(8,128)(2,1)S(1)} collective-permute-done((bf16[272,256]{1,0:T(8,128)(2,1)S(1)}, bf16[272,256]{1,0:T(8,128)(2,1)S(1)}, u32[]{:S(2)}, u32[]{:S(2)}) %collective-permute-start.43) | collective-permute-done | bytes 139296 | tf_op jit(solution)/shard_map/ppermute | solution.py:253
  138.7 7.2 %collective-permute-done.20.refs_0_ = bf16[384,640]{1,0:T(8,128)(2,1)S(1)} collective-permute-done((bf16[384,640]{1,0:T(8,128)(2,1)S(1)}, bf16[384,640]{1,0:T(8,128)(2,1)S(1)}, u32[]{:S(2)}, u32[]{:S(2)}) %collective-permute-start.20) | collective-permute-done | bytes 491552 | tf_op jit(solution)/shard_map/ppermute | solution.py:253
  145.9 0.6 collective-permute-done.21.refs_1_
  146.5 1.4 collective-permute-start.22
  147.9 1.5 collective-permute-start.24
  149.5 6.2 %project_query.1 = (f32[240,768]{1,0:T(8,128)S(1)}, bf16[240,768]{1,0:T(8,128)(2,1)S(1)}) custom-call(s32[34]{0:T(128)S(1)} %list_facts.1.facts, bf16[1,240,12288]{2,1,0:T(8,128)(2,1)S(1)} %bitcast.13, bf16[384,6144]{1,0:T(8,128)(2,1)S(1)} %get-tuple-element.132.own_ref, bf16[384,6144]{1,0:T(8,128)(2,1)S(1)} %collective-permute-done.35.sib_ref, ...), custom_call_target="tpu_custom_call" | custom-call | flops 1000 | bytes 1000 | tf_op jit(solution)/shard_map/project_query/pallas_call | solution.py:379
  155.7 0.6 collective-permute-start.36
  156.3 3.1 %collective-permute-done.24.refs_2_ = bf16[1536,128]{1,0:T(8,128)(2,1)S(1)} collective-permute-done((bf16[1536,128]{1,0:T(8,128)(2,1)S(1)}, bf16[1536,128]{1,0:T(8,128)(2,1)S(1)}, u32[]{:S(2)}, u32[]{:S(2)}) %collective-permute-start.24) | collective-permute-done | bytes 393248 | tf_op jit(solution)/shard_map/ppermute | solution.py:257
  159.4 0.6 collective-permute-start.25
  160.0 1.5 collective-permute-start.26
  161.5 0.5 collective-permute-start.29
  162.0 1.5 collective-permute-start.30
  163.5 0.9 collective-permute-done.36.other_ref
  164.5 2.0 collective-permute-start.31
  166.5 6.2 %attend.1.att_ref = bf16[240,768]{1,0:T(8,128)(2,1)S(1)} custom-call(s32[6]{0:T(128)S(1)} %bitcast.18, s32[34]{0:T(128)S(1)} %list_facts.1.facts, f32[240,768]{1,0:T(8,128)S(1)} %get-tuple-element.134.mine_ref, bf16[240,768]{1,0:T(8,128)(2,1)S(1)} %collective-permute-done.36.other_ref, bf16[240,256]{1,0:T(8,128)(2,1)S(1)} %get-tuple-element.136.new_ref, ...), custom_call_target="tpu_custom_call" | custom-call | flops 1000 | bytes 1000 | tf_op jit(solution)/shard_map/attend/pallas_call | solution.py:469
  172.8 3.7 %collective-permute-done.29.refs_0_ = bf16[384,640]{1,0:T(8,128)(2,1)S(1)} collective-permute-done((bf16[384,640]{1,0:T(8,128)(2,1)S(1)}, bf16[384,640]{1,0:T(8,128)(2,1)S(1)}, u32[]{:S(2)}, u32[]{:S(2)}) %collective-permute-start.29) | collective-permute-done | bytes 491552 | tf_op jit(solution)/shard_map/ppermute | solution.py:253
  176.5 0.8 collective-permute-done.30.refs_1_
  177.5 1.4 collective-permute-start.34
  178.9 1.5 collective-permute-start.27
  180.4 0.6 collective-permute-start.28
  180.9 2.1 %collective-permute-start.32 = (bf16[192,640]{1,0:T(8,128)(2,1)S(1)}, bf16[192,640]{1,0:T(8,128)(2,1)S(1)}, u32[]{:S(2)}, u32[]{:S(2)}) collective-permute-start(bf16[192,640]{1,0:T(8,128)(2,1)S(1)} %get-tuple-element.129), channel_id=1, source_target_pairs={{0,4},{1,5},{4,8},{5,9},{8,12},{9,13},{12,14},{13,15},{14,10},{15,... | collective-permute-start | bytes 737288 | tf_op jit(solution)/shard_map/ppermute | solution.py:253
  183.0 6.9 %project_output.3 = (bf16[1,240,12288]{2,1,0:T(8,128)(2,1)}, bf16[5,240,768]{2,1,0:T(8,128)(2,1)S(1)}) custom-call(s32[34]{0:T(128)S(1)} %list_facts.1.facts, bf16[240,768]{1,0:T(8,128)(2,1)S(1)} %attend.1.att_ref, bf16[240,768]{1,0:T(8,128)(2,1)S(1)} %collective-permute-done.45.att2_ref, bf16[768,768]{1,0:T(8,128)(2,1)S(1)} %bitcast.17, ...), custom_call_target="tpu_custom_call" | custom-call | flops 1000 | bytes 1000 | tf_op jit(solution)/shard_map/project_output/pallas_call | solution.py:597
  190.1 2.1 %collective-permute-start.46 = (bf16[384,128]{1,0:T(8,128)(2,1)S(1)}, bf16[384,128]{1,0:T(8,128)(2,1)S(1)}, u32[]{:S(2)}, u32[]{:S(2)}) collective-permute-start(bf16[384,128]{1,0:T(8,128)(2,1)S(1)} %get-tuple-element.143), channel_id=1, source_target_pairs={{0,4},{1,5},{4,8},{5,9},{8,12},{9,13},{12,14},{13,15},{14,10},{15,... | collective-permute-start | bytes 294920 | tf_op jit(solution)/shard_map/ppermute | solution.py:253
  192.2 3.6 %project_output.4 = (bf16[1,240,12288]{2,1,0:T(8,128)(2,1)}, bf16[2,240,768]{2,1,0:T(8,128)(2,1)S(1)}) custom-call(s32[34]{0:T(128)S(1)} %list_facts.1.facts, bf16[240,768]{1,0:T(8,128)(2,1)S(1)} %attend.1.att_ref, bf16[240,768]{1,0:T(8,128)(2,1)S(1)} %collective-permute-done.45.att2_ref, ...), custom_call_target="tpu_custom_call", output_to_operand_aliasing={{0}: (8, {})} | custom-call | flops 1000 | bytes 1000 | tf_op jit(solution)/shard_map/project_output/pallas_call | solution.py:597
  195.8 1.6 collective-permute-done.47.refs_5_
  197.4 2.3 %project_output.5 = (bf16[1,240,12288]{2,1,0:T(8,128)(2,1)}, bf16[1,240,768]{2,1,0:T(8,128)(2,1)S(1)}) custom-call(s32[34]{0:T(128)S(1)} %list_facts.1.facts, bf16[240,768]{1,0:T(8,128)(2,1)S(1)} %attend.1.att_ref, bf16[240,768]{1,0:T(8,128)(2,1)S(1)} %collective-permute-done.45.att2_ref, ...), custom_call_target="tpu_custom_call", output_to_operand_aliasing={{0}: (10, {})} | custom-call | flops 1000 | bytes 1000 | tf_op jit(solution)/shard_map/project_output/pallas_call | solution.py:597
  199.7 0.6 collective-permute-start.50
  200.3 1.3 collective-permute-done.50.refs_1_
  201.6 1.6 place_output.1
  (87 shorter events, 5.8 us)
Async XLA Ops:
  2.6 5.1 %copy-start.1 = (bf16[32,6144]{1,0:T(8,128)(2,1)}, bf16[32,6144]{1,0:T(8,128)(2,1)S(1)}, u32[]{:S(2)}) copy-start(bf16[32,6144]{1,0:T(8,128)(2,1)S(1)} %get-tuple-element.83.refs_3_.refs_0_) | copy-start | bytes 1179652
  2.6 26.6 %collective-permute-start = (bf16[48,6144]{1,0:T(8,128)(2,1)S(1)}, bf16[48,6144]{1,0:T(8,128)(2,1)S(1)}, u32[]{:S(2)}, u32[]{:S(2)}) collective-permute-start(bf16[48,6144]{1,0:T(8,128)(2,1)S(1)} %get-tuple-element.84.refs_8_), channel_id=1, source_target_pairs={{0,4},{1,5},{4,8},{5,9},{8,12},{9,13},{12,14},{13,15},{14,10},{15,... | collective-permute-start | bytes 1769480 | tf_op jit(solution)/shard_map/ppermute | solution.py:253
  5.7 23.5 %collective-permute-start.1 = (bf16[48,6144]{1,0:T(8,128)(2,1)S(1)}, bf16[48,6144]{1,0:T(8,128)(2,1)S(1)}, u32[]{:S(2)}, u32[]{:S(2)}) collective-permute-start(bf16[48,6144]{1,0:T(8,128)(2,1)S(1)} %get-tuple-element.84.refs_8_), channel_id=1, source_target_pairs={{0,2},{1,3},{4,0},{5,1},{8,4},{9,5},{12,8},{13,9},{14,12},{15,13},... | collective-permute-start | bytes 1769480 | tf_op jit(solution)/shard_map/ppermute | solution.py:253
  5.7 21.7 %collective-permute-start.2 = (bf16[32,6144]{1,0:T(8,128)(2,1)S(1)}, bf16[32,6144]{1,0:T(8,128)(2,1)S(1)}, u32[]{:S(2)}, u32[]{:S(2)}) collective-permute-start(bf16[32,6144]{1,0:T(8,128)(2,1)S(1)} %get-tuple-element.83.refs_3_.refs_0_), channel_id=1, source_target_pairs={{0,4},{1,5},{4,8},{5,9},{8,12},{9,13},{12,14},{13,15},{14,10},{15,... | collective-permute-start | bytes 1179656 | tf_op jit(solution)/shard_map/ppermute | solution.py:253
  7.7 21.2 %collective-permute-start.3 = (bf16[32,6144]{1,0:T(8,128)(2,1)S(1)}, bf16[32,6144]{1,0:T(8,128)(2,1)S(1)}, u32[]{:S(2)}, u32[]{:S(2)}) collective-permute-start(bf16[32,6144]{1,0:T(8,128)(2,1)S(1)} %get-tuple-element.83.refs_3_.refs_0_), channel_id=1, source_target_pairs={{0,2},{1,3},{4,0},{5,1},{8,4},{9,5},{12,8},{13,9},{14,12},{15,13},... | collective-permute-start | bytes 1179656 | tf_op jit(solution)/shard_map/ppermute | solution.py:253
  9.8 84.3 %collective-permute-start.14 = (bf16[240,6144]{1,0:T(8,128)(2,1)S(1)}, bf16[240,6144]{1,0:T(8,128)(2,1)S(1)}, u32[]{:S(2)}, u32[]{:S(2)}) collective-permute-start(bf16[240,6144]{1,0:T(8,128)(2,1)S(1)} %get-tuple-element.103), channel_id=1, source_target_pairs={{0,16},{16,0},{1,17},{17,1},{2,18},{18,2},{3,19},{19,3},{4,20},{20... | collective-permute-start | bytes 8847368 | tf_op jit(solution)/shard_map/ppermute | solution.py:257
  28.9 12.1 %collective-permute-start.5 = (bf16[32,6144]{1,0:T(8,128)(2,1)S(1)}, bf16[32,6144]{1,0:T(8,128)(2,1)S(1)}, u32[]{:S(2)}, u32[]{:S(2)}) collective-permute-start(bf16[32,6144]{1,0:T(8,128)(2,1)S(1)} %get-tuple-element.87.refs_2_), channel_id=1, source_target_pairs={{0,2},{1,3},{4,0},{5,1},{8,4},{9,5},{12,8},{13,9},{14,12},{15,13},... | collective-permute-start | bytes 1179656 | tf_op jit(solution)/shard_map/ppermute | solution.py:253
  29.2 11.8 %collective-permute-start.4 = (bf16[32,6144]{1,0:T(8,128)(2,1)S(1)}, bf16[32,6144]{1,0:T(8,128)(2,1)S(1)}, u32[]{:S(2)}, u32[]{:S(2)}) collective-permute-start(bf16[32,6144]{1,0:T(8,128)(2,1)S(1)} %get-tuple-element.86.refs_1_), channel_id=1, source_target_pairs={{0,4},{1,5},{4,8},{5,9},{8,12},{9,13},{12,14},{13,15},{14,10},{15,... | collective-permute-start | bytes 1179656 | tf_op jit(solution)/shard_map/ppermute | solution.py:253
  30.9 22.7 %collective-permute-start.7 = (bf16[48,6144]{1,0:T(8,128)(2,1)S(1)}, bf16[48,6144]{1,0:T(8,128)(2,1)S(1)}, u32[]{:S(2)}, u32[]{:S(2)}) collective-permute-start(bf16[48,6144]{1,0:T(8,128)(2,1)S(1)} %get-tuple-element.90.refs_10_), channel_id=1, source_target_pairs={{0,2},{1,3},{4,0},{5,1},{8,4},{9,5},{12,8},{13,9},{14,12},{15,13},... | collective-permute-start | bytes 1769480 | tf_op jit(solution)/shard_map/ppermute | solution.py:253
  40.9 53.2 %copy-start.2 = (bf16[32,6144]{1,0:T(8,128)(2,1)S(1)}, bf16[32,6144]{1,0:T(8,128)(2,1)}, u32[]{:S(2)}) copy-start(bf16[32,6144]{1,0:T(8,128)(2,1)} %copy-done.1) | copy-start | bytes 1179652
  40.9 12.6 %collective-permute-start.6 = (bf16[48,6144]{1,0:T(8,128)(2,1)S(1)}, bf16[48,6144]{1,0:T(8,128)(2,1)S(1)}, u32[]{:S(2)}, u32[]{:S(2)}) collective-permute-start(bf16[48,6144]{1,0:T(8,128)(2,1)S(1)} %get-tuple-element.89.refs_9_), channel_id=1, source_target_pairs={{0,4},{1,5},{4,8},{5,9},{8,12},{9,13},{12,14},{13,15},{14,10},{15,... | collective-permute-start | bytes 1769480 | tf_op jit(solution)/shard_map/ppermute | solution.py:253
  42.5 19.5 %collective-permute-start.9 = (bf16[32,6144]{1,0:T(8,128)(2,1)S(1)}, bf16[32,6144]{1,0:T(8,128)(2,1)S(1)}, u32[]{:S(2)}, u32[]{:S(2)}) collective-permute-start(bf16[32,6144]{1,0:T(8,128)(2,1)S(1)} %get-tuple-element.93.refs_4_), channel_id=1, source_target_pairs={{0,2},{1,3},{4,0},{5,1},{8,4},{9,5},{12,8},{13,9},{14,12},{15,13},... | collective-permute-start | bytes 1179656 | tf_op jit(solution)/shard_map/ppermute | solution.py:253
  53.6 9.1 %collective-permute-start.8 = (bf16[32,6144]{1,0:T(8,128)(2,1)S(1)}, bf16[32,6144]{1,0:T(8,128)(2,1)S(1)}, u32[]{:S(2)}, u32[]{:S(2)}) collective-permute-start(bf16[32,6144]{1,0:T(8,128)(2,1)S(1)} %get-tuple-element.92.refs_3_), channel_id=1, source_target_pairs={{0,4},{1,5},{4,8},{5,9},{8,12},{9,13},{12,14},{13,15},{14,10},{15,... | collective-permute-start | bytes 1179656 | tf_op jit(solution)/shard_map/ppermute | solution.py:253
  55.2 17.1 %collective-permute-start.11 = (bf16[48,6144]{1,0:T(8,128)(2,1)S(1)}, bf16[48,6144]{1,0:T(8,128)(2,1)S(1)}, u32[]{:S(2)}, u32[]{:S(2)}) collective-permute-start(bf16[48,6144]{1,0:T(8,128)(2,1)S(1)} %get-tuple-element.96.refs_12_), channel_id=1, source_target_pairs={{0,2},{1,3},{4,0},{5,1},{8,4},{9,5},{12,8},{13,9},{14,12},{15,13},... | collective-permute-start | bytes 1769480 | tf_op jit(solution)/shard_map/ppermute | solution.py:253
  62.7 12.6 %collective-permute-start.10 = (bf16[48,6144]{1,0:T(8,128)(2,1)S(1)}, bf16[48,6144]{1,0:T(8,128)(2,1)S(1)}, u32[]{:S(2)}, u32[]{:S(2)}) collective-permute-start(bf16[48,6144]{1,0:T(8,128)(2,1)S(1)} %get-tuple-element.95.refs_11_), channel_id=1, source_target_pairs={{0,4},{1,5},{4,8},{5,9},{8,12},{9,13},{12,14},{13,15},{14,10},{15,... | collective-permute-start | bytes 1769480 | tf_op jit(solution)/shard_map/ppermute | solution.py:253
  75.4 34.2 %slice-start.2 = ((s8[6291456]{0:T(1024)(128)(4,1)}), s8[4194304]{0:T(1024)(128)(4,1)S(1)}, s32[]{:S(2)}) async-start(s8[6291456]{0:T(1024)(128)(4,1)} %bitcast.14), calls=%async_computation.2 | async-start | bytes 8388608
  75.4 18.8 %collective-permute-start.13 = (bf16[48,6144]{1,0:T(8,128)(2,1)S(1)}, bf16[48,6144]{1,0:T(8,128)(2,1)S(1)}, u32[]{:S(2)}, u32[]{:S(2)}) collective-permute-start(bf16[48,6144]{1,0:T(8,128)(2,1)S(1)} %get-tuple-element.101.refs_13_), channel_id=1, source_target_pairs={{0,4},{1,5},{4,8},{5,9},{8,12},{9,13},{12,14},{13,15},{14,10},{15,... | collective-permute-start | bytes 1769480 | tf_op jit(solution)/shard_map/ppermute | solution.py:253
  76.9 20.2 %collective-permute-start.18 = (bf16[384,640]{1,0:T(8,128)(2,1)S(1)}, bf16[384,640]{1,0:T(8,128)(2,1)S(1)}, u32[]{:S(2)}, u32[]{:S(2)}) collective-permute-start(bf16[384,640]{1,0:T(8,128)(2,1)S(1)} %get-tuple-element.108), channel_id=1, source_target_pairs={{0,4},{1,5},{4,8},{5,9},{8,12},{9,13},{12,14},{13,15},{14,10},{15,... | collective-permute-start | bytes 1474568 | tf_op jit(solution)/shard_map/ppermute | solution.py:253
  78.5 18.7 %collective-permute-start.19 = (bf16[384,640]{1,0:T(8,128)(2,1)S(1)}, bf16[384,640]{1,0:T(8,128)(2,1)S(1)}, u32[]{:S(2)}, u32[]{:S(2)}) collective-permute-start(bf16[384,640]{1,0:T(8,128)(2,1)S(1)} %get-tuple-element.108), channel_id=1, source_target_pairs={{0,2},{1,3},{4,0},{5,1},{8,4},{9,5},{12,8},{13,9},{14,12},{15,13},... | collective-permute-start | bytes 1474568 | tf_op jit(solution)/shard_map/ppermute | solution.py:253
  79.0 15.2 %collective-permute-start.12 = (bf16[32,6144]{1,0:T(8,128)(2,1)S(1)}, bf16[32,6144]{1,0:T(8,128)(2,1)S(1)}, u32[]{:S(2)}, u32[]{:S(2)}) collective-permute-start(bf16[32,6144]{1,0:T(8,128)(2,1)S(1)} %get-tuple-element.100.refs_6_), channel_id=1, source_target_pairs={{0,2},{1,3},{4,0},{5,1},{8,4},{9,5},{12,8},{13,9},{14,12},{15,13},... | collective-permute-start | bytes 1179656 | tf_op jit(solution)/shard_map/ppermute | solution.py:253
  94.1 15.4 %slice-start = ((s8[5898240]{0:T(1024)(128)(4,1)}), s8[4194304]{0:T(1024)(128)(4,1)S(1)}, s32[]{:S(2)}) async-start(s8[5898240]{0:T(1024)(128)(4,1)} %bitcast.12), calls=%async_computation | async-start | bytes 8388608
  94.2 15.4 %slice-start.1 = ((s8[5898240]{0:T(1024)(128)(4,1)}), s8[1703936]{0:T(1024)(128)(4,1)S(1)}, s32[]{:S(2)}) async-start(s8[5898240]{0:T(1024)(128)(4,1)} %bitcast.12), calls=%async_computation.1 | async-start | bytes 3407872
  94.2 15.4 %slice-start.3 = ((s8[6291456]{0:T(1024)(128)(4,1)}), s8[2097152]{0:T(1024)(128)(4,1)S(1)}, s32[]{:S(2)}) async-start(s8[6291456]{0:T(1024)(128)(4,1)} %bitcast.14), calls=%async_computation.3 | async-start | bytes 4194304
  94.7 5.0 %copy-start.4 = (s32[256]{0:T(256)S(1)}, s32[256]{0:T(256)}, u32[]{:S(2)}) copy-start(s32[256]{0:T(256)} %constant.11.clone.slot_ref) | copy-start | bytes 3076
  94.7 5.0 %copy-start.6 = (s32[16]{0:T(128)S(1)}, s32[16]{0:T(128)}, u32[]{:S(2)}) copy-start(s32[16]{0:T(128)} %table_ref.1) | copy-start | bytes 196
  97.2 52.3 %collective-permute-start.35 = (bf16[384,6144]{1,0:T(8,128)(2,1)S(1)}, bf16[384,6144]{1,0:T(8,128)(2,1)S(1)}, u32[]{:S(2)}, u32[]{:S(2)}) collective-permute-start(bf16[384,6144]{1,0:T(8,128)(2,1)S(1)} %get-tuple-element.132.own_ref), channel_id=1, source_target_pairs={{0,1},{1,0},{2,3},{3,2},{4,5},{5,4},{6,7},{7,6},{8,9},{9,8},{10,11... | collective-permute-start | bytes 14155784 | tf_op jit(solution)/shard_map/ppermute | solution.py:253
  97.2 12.4 %collective-permute-start.15 = (bf16[256,6144]{1,0:T(8,128)(2,1)S(1)}, bf16[256,6144]{1,0:T(8,128)(2,1)S(1)}, u32[]{:S(2)}, u32[]{:S(2)}) collective-permute-start(bf16[256,6144]{1,0:T(8,128)(2,1)S(1)} %get-tuple-element.105.own_ref), channel_id=1, source_target_pairs={{0,1},{1,0},{2,3},{3,2},{4,5},{5,4},{6,7},{7,6},{8,9},{9,8},{10,11... | collective-permute-start | bytes 9437192 | tf_op jit(solution)/shard_map/ppermute | solution.py:253
  97.7 35.4 %collective-permute-start.16 = (bf16[384,640]{1,0:T(8,128)(2,1)S(1)}, bf16[384,640]{1,0:T(8,128)(2,1)S(1)}, u32[]{:S(2)}, u32[]{:S(2)}) collective-permute-start(bf16[384,640]{1,0:T(8,128)(2,1)S(1)} %get-tuple-element.107), channel_id=1, source_target_pairs={{0,4},{1,5},{4,8},{5,9},{8,12},{9,13},{12,14},{13,15},{14,10},{15,... | collective-permute-start | bytes 1474568 | tf_op jit(solution)/shard_map/ppermute | solution.py:253
  99.3 33.8 %collective-permute-start.17 = (bf16[384,640]{1,0:T(8,128)(2,1)S(1)}, bf16[384,640]{1,0:T(8,128)(2,1)S(1)}, u32[]{:S(2)}, u32[]{:S(2)}) collective-permute-start(bf16[384,640]{1,0:T(8,128)(2,1)S(1)} %get-tuple-element.107), channel_id=1, source_target_pairs={{0,2},{1,3},{4,0},{5,1},{8,4},{9,5},{12,8},{13,9},{14,12},{15,13},... | collective-permute-start | bytes 1474568 | tf_op jit(solution)/shard_map/ppermute | solution.py:253
  115.3 5.7 %collective-permute-start.37 = (bf16[272,256]{1,0:T(8,128)(2,1)S(1)}, bf16[272,256]{1,0:T(8,128)(2,1)S(1)}, u32[]{:S(2)}, u32[]{:S(2)}) collective-permute-start(bf16[272,256]{1,0:T(8,128)(2,1)S(1)} %get-tuple-element.137.refs_0_), channel_id=1, source_target_pairs={{0,4},{1,5},{4,8},{5,9},{8,12},{9,13},{12,14},{13,15},{14,10},{15,... | collective-permute-start | bytes 417800 | tf_op jit(solution)/shard_map/ppermute | solution.py:253
  116.9 5.7 %collective-permute-start.38 = (bf16[272,256]{1,0:T(8,128)(2,1)S(1)}, bf16[272,256]{1,0:T(8,128)(2,1)S(1)}, u32[]{:S(2)}, u32[]{:S(2)}) collective-permute-start(bf16[272,256]{1,0:T(8,128)(2,1)S(1)} %get-tuple-element.137.refs_0_), channel_id=1, source_target_pairs={{0,2},{1,3},{4,0},{5,1},{8,4},{9,5},{12,8},{13,9},{14,12},{15,13},... | collective-permute-start | bytes 417800 | tf_op jit(solution)/shard_map/ppermute | solution.py:253
  121.0 5.1 %collective-permute-start.39 = (bf16[272,256]{1,0:T(8,128)(2,1)S(1)}, bf16[272,256]{1,0:T(8,128)(2,1)S(1)}, u32[]{:S(2)}, u32[]{:S(2)}) collective-permute-start(bf16[272,256]{1,0:T(8,128)(2,1)S(1)} %collective-permute-done.37.refs_1_), channel_id=1, source_target_pairs={{0,4},{1,5},{4,8},{5,9},{8,12},{9,13},{12,14},{13,15},{14,10},{15,... | collective-permute-start | bytes 417800 | tf_op jit(solution)/shard_map/ppermute | solution.py:253
  122.6 5.1 %collective-permute-start.40 = (bf16[272,256]{1,0:T(8,128)(2,1)S(1)}, bf16[272,256]{1,0:T(8,128)(2,1)S(1)}, u32[]{:S(2)}, u32[]{:S(2)}) collective-permute-start(bf16[272,256]{1,0:T(8,128)(2,1)S(1)} %collective-permute-done.38.refs_2_), channel_id=1, source_target_pairs={{0,2},{1,3},{4,0},{5,1},{8,4},{9,5},{12,8},{13,9},{14,12},{15,13},... | collective-permute-start | bytes 417800 | tf_op jit(solution)/shard_map/ppermute | solution.py:253
  126.0 5.5 %collective-permute-start.41 = (bf16[272,256]{1,0:T(8,128)(2,1)S(1)}, bf16[272,256]{1,0:T(8,128)(2,1)S(1)}, u32[]{:S(2)}, u32[]{:S(2)}) collective-permute-start(bf16[272,256]{1,0:T(8,128)(2,1)S(1)} %collective-permute-done.39.refs_3_), channel_id=1, source_target_pairs={{0,4},{1,5},{4,8},{5,9},{8,12},{9,13},{12,14},{13,15},{14,10},{15,... | collective-permute-start | bytes 417800 | tf_op jit(solution)/shard_map/ppermute | solution.py:253
  127.6 7.6 %collective-permute-start.42 = (bf16[272,256]{1,0:T(8,128)(2,1)S(1)}, bf16[272,256]{1,0:T(8,128)(2,1)S(1)}, u32[]{:S(2)}, u32[]{:S(2)}) collective-permute-start(bf16[272,256]{1,0:T(8,128)(2,1)S(1)} %collective-permute-done.40.refs_4_), channel_id=1, source_target_pairs={{0,2},{1,3},{4,0},{5,1},{8,4},{9,5},{12,8},{13,9},{14,12},{15,13},... | collective-permute-start | bytes 417800 | tf_op jit(solution)/shard_map/ppermute | solution.py:253
  131.5 6.6 %collective-permute-start.43 = (bf16[272,256]{1,0:T(8,128)(2,1)S(1)}, bf16[272,256]{1,0:T(8,128)(2,1)S(1)}, u32[]{:S(2)}, u32[]{:S(2)}) collective-permute-start(bf16[272,256]{1,0:T(8,128)(2,1)S(1)} %collective-permute-done.41.refs_5_), channel_id=1, source_target_pairs={{0,4},{1,5},{4,8},{5,9},{8,12},{9,13},{12,14},{13,15},{14,10},{15,... | collective-permute-start | bytes 417800 | tf_op jit(solution)/shard_map/ppermute | solution.py:253
  133.2 12.7 %collective-permute-start.20 = (bf16[384,640]{1,0:T(8,128)(2,1)S(1)}, bf16[384,640]{1,0:T(8,128)(2,1)S(1)}, u32[]{:S(2)}, u32[]{:S(2)}) collective-permute-start(bf16[384,640]{1,0:T(8,128)(2,1)S(1)} %get-tuple-element.112.refs_1_), channel_id=1, source_target_pairs={{0,4},{1,5},{4,8},{5,9},{8,12},{9,13},{12,14},{13,15},{14,10},{15,... | collective-permute-start | bytes 1474568 | tf_op jit(solution)/shard_map/ppermute | solution.py:253
  134.8 11.7 %collective-permute-start.21 = (bf16[384,640]{1,0:T(8,128)(2,1)S(1)}, bf16[384,640]{1,0:T(8,128)(2,1)S(1)}, u32[]{:S(2)}, u32[]{:S(2)}) collective-permute-start(bf16[384,640]{1,0:T(8,128)(2,1)S(1)} %get-tuple-element.113.refs_4_), channel_id=1, source_target_pairs={{0,2},{1,3},{4,0},{5,1},{8,4},{9,5},{12,8},{13,9},{14,12},{15,13},... | collective-permute-start | bytes 1474568 | tf_op jit(solution)/shard_map/ppermute | solution.py:253
  138.2 23.8 %collective-permute-start.44 = (bf16[2176,256]{1,0:T(8,128)(2,1)S(1)}, bf16[2176,256]{1,0:T(8,128)(2,1)S(1)}, u32[]{:S(2)}, u32[]{:S(2)}) collective-permute-start(bf16[2176,256]{1,0:T(8,128)(2,1)S(1)} %get-tuple-element.138.refs_0_), channel_id=1, source_target_pairs={{0,1},{1,0},{2,3},{3,2},{4,5},{5,4},{6,7},{7,6},{8,9},{9,8},{10,11... | collective-permute-start | bytes 3342344 | tf_op jit(solution)/shard_map/ppermute | solution.py:253
  138.3 21.1 %collective-permute-start.23 = (bf16[384,640]{1,0:T(8,128)(2,1)S(1)}, bf16[384,640]{1,0:T(8,128)(2,1)S(1)}, u32[]{:S(2)}, u32[]{:S(2)}) collective-permute-start(bf16[384,640]{1,0:T(8,128)(2,1)S(1)} %get-tuple-element.116.refs_5_), channel_id=1, source_target_pairs={{0,2},{1,3},{4,0},{5,1},{8,4},{9,5},{12,8},{13,9},{14,12},{15,13},... | collective-permute-start | bytes 1474568 | tf_op jit(solution)/shard_map/ppermute | solution.py:253
  146.5 12.8 %collective-permute-start.22 = (bf16[384,640]{1,0:T(8,128)(2,1)S(1)}, bf16[384,640]{1,0:T(8,128)(2,1)S(1)}, u32[]{:S(2)}, u32[]{:S(2)}) collective-permute-start(bf16[384,640]{1,0:T(8,128)(2,1)S(1)} %get-tuple-element.115.refs_2_), channel_id=1, source_target_pairs={{0,4},{1,5},{4,8},{5,9},{8,12},{9,13},{12,14},{13,15},{14,10},{15,... | collective-permute-start | bytes 1474568 | tf_op jit(solution)/shard_map/ppermute | solution.py:253
  147.9 11.4 %collective-permute-start.24 = (bf16[1536,128]{1,0:T(8,128)(2,1)S(1)}, bf16[1536,128]{1,0:T(8,128)(2,1)S(1)}, u32[]{:S(2)}, u32[]{:S(2)}) collective-permute-start(bf16[1536,128]{1,0:T(8,128)(2,1)S(1)} %get-tuple-element.117), channel_id=1, source_target_pairs={{0,16},{16,0},{1,17},{17,1},{2,18},{18,2},{3,19},{19,3},{4,20},{20... | collective-permute-start | bytes 1179656 | tf_op jit(solution)/shard_map/ppermute | solution.py:257
  149.5 17.0 %copy-start.3 = (s32[1,240]{1,0:T(1,128)S(1)}, s32[1,240]{1,0:T(1,128)}, u32[]{:S(2)}) copy-start(s32[1,240]{1,0:T(1,128)} %row_ref.1) | copy-start | bytes 2884
  149.5 17.0 %copy-start.5 = (s32[1,6]{1,0:T(1,128)S(1)}, s32[1,6]{1,0:T(1,128)}, u32[]{:S(2)}) copy-start(s32[1,6]{1,0:T(1,128)} %param.15) | copy-start | bytes 76
  155.7 8.8 %collective-permute-start.36 = (bf16[240,768]{1,0:T(8,128)(2,1)S(1)}, bf16[240,768]{1,0:T(8,128)(2,1)S(1)}, u32[]{:S(2)}, u32[]{:S(2)}) collective-permute-start(bf16[240,768]{1,0:T(8,128)(2,1)S(1)} %get-tuple-element.135), channel_id=1, source_target_pairs={{0,16},{16,0},{1,17},{17,1},{2,18},{18,2},{3,19},{19,3},{4,20},{20... | collective-permute-start | bytes 1105928 | tf_op jit(solution)/shard_map/ppermute | solution.py:257
  159.4 13.3 %collective-permute-start.25 = (bf16[384,640]{1,0:T(8,128)(2,1)S(1)}, bf16[384,640]{1,0:T(8,128)(2,1)S(1)}, u32[]{:S(2)}, u32[]{:S(2)}) collective-permute-start(bf16[384,640]{1,0:T(8,128)(2,1)S(1)} %get-tuple-element.120.refs_6_), channel_id=1, source_target_pairs={{0,4},{1,5},{4,8},{5,9},{8,12},{9,13},{12,14},{13,15},{14,10},{15,... | collective-permute-start | bytes 1474568 | tf_op jit(solution)/shard_map/ppermute | solution.py:253
  160.0 12.8 %collective-permute-start.26 = (bf16[384,640]{1,0:T(8,128)(2,1)S(1)}, bf16[384,640]{1,0:T(8,128)(2,1)S(1)}, u32[]{:S(2)}, u32[]{:S(2)}) collective-permute-start(bf16[384,640]{1,0:T(8,128)(2,1)S(1)} %get-tuple-element.121.refs_9_), channel_id=1, source_target_pairs={{0,2},{1,3},{4,0},{5,1},{8,4},{9,5},{12,8},{13,9},{14,12},{15,13},... | collective-permute-start | bytes 1474568 | tf_op jit(solution)/shard_map/ppermute | solution.py:253
  161.5 15.1 %collective-permute-start.29 = (bf16[384,640]{1,0:T(8,128)(2,1)S(1)}, bf16[384,640]{1,0:T(8,128)(2,1)S(1)}, u32[]{:S(2)}, u32[]{:S(2)}) collective-permute-start(bf16[384,640]{1,0:T(8,128)(2,1)S(1)} %get-tuple-element.124.refs_7_), channel_id=1, source_target_pairs={{0,4},{1,5},{4,8},{5,9},{8,12},{9,13},{12,14},{13,15},{14,10},{15,... | collective-permute-start | bytes 1474568 | tf_op jit(solution)/shard_map/ppermute | solution.py:253
  162.0 15.3 %collective-permute-start.30 = (bf16[384,640]{1,0:T(8,128)(2,1)S(1)}, bf16[384,640]{1,0:T(8,128)(2,1)S(1)}, u32[]{:S(2)}, u32[]{:S(2)}) collective-permute-start(bf16[384,640]{1,0:T(8,128)(2,1)S(1)} %get-tuple-element.125.refs_10_), channel_id=1, source_target_pairs={{0,2},{1,3},{4,0},{5,1},{8,4},{9,5},{12,8},{13,9},{14,12},{15,13},... | collective-permute-start | bytes 1474568 | tf_op jit(solution)/shard_map/ppermute | solution.py:253
  164.5 8.4 %collective-permute-start.31 = (bf16[1536,128]{1,0:T(8,128)(2,1)S(1)}, bf16[1536,128]{1,0:T(8,128)(2,1)S(1)}, u32[]{:S(2)}, u32[]{:S(2)}) collective-permute-start(bf16[1536,128]{1,0:T(8,128)(2,1)S(1)} %get-tuple-element.128), channel_id=1, source_target_pairs={{0,16},{16,0},{1,17},{17,1},{2,18},{18,2},{3,19},{19,3},{4,20},{20... | collective-permute-start | bytes 1179656 | tf_op jit(solution)/shard_map/ppermute | solution.py:257
  166.5 16.5 %copy-start = (bf16[6,128,1,768]{3,1,2,0:T(8,128)(2,1)S(1)}, bf16[6,128,1,768]{3,1,2,0:T(8,128)(2,1)}, u32[]{:S(2)}) copy-start(bf16[6,128,1,768]{3,1,2,0:T(8,128)(2,1)} %param.14) | copy-start | bytes 3538948
  172.7 10.3 %collective-permute-start.45 = (bf16[240,768]{1,0:T(8,128)(2,1)S(1)}, bf16[240,768]{1,0:T(8,128)(2,1)S(1)}, u32[]{:S(2)}, u32[]{:S(2)}) collective-permute-start(bf16[240,768]{1,0:T(8,128)(2,1)S(1)} %attend.1.att_ref), channel_id=1, source_target_pairs={{0,1},{1,0},{2,3},{3,2},{4,5},{5,4},{6,7},{7,6},{8,9},{9,8},{10,11... | collective-permute-start | bytes 1105928 | tf_op jit(solution)/shard_map/ppermute | solution.py:253
  177.5 12.6 %collective-permute-start.34 = (bf16[1536,128]{1,0:T(8,128)(2,1)S(1)}, bf16[1536,128]{1,0:T(8,128)(2,1)S(1)}, u32[]{:S(2)}, u32[]{:S(2)}) collective-permute-start(bf16[1536,128]{1,0:T(8,128)(2,1)S(1)} %get-tuple-element.131), channel_id=1, source_target_pairs={{0,16},{16,0},{1,17},{17,1},{2,18},{18,2},{3,19},{19,3},{4,20},{20... | collective-permute-start | bytes 1179656 | tf_op jit(solution)/shard_map/ppermute | solution.py:257
  178.9 11.1 %collective-permute-start.27 = (bf16[192,640]{1,0:T(8,128)(2,1)S(1)}, bf16[192,640]{1,0:T(8,128)(2,1)S(1)}, u32[]{:S(2)}, u32[]{:S(2)}) collective-permute-start(bf16[192,640]{1,0:T(8,128)(2,1)S(1)} %get-tuple-element.122), channel_id=1, source_target_pairs={{0,4},{1,5},{4,8},{5,9},{8,12},{9,13},{12,14},{13,15},{14,10},{15,... | collective-permute-start | bytes 737288 | tf_op jit(solution)/shard_map/ppermute | solution.py:253
  180.4 9.6 %collective-permute-start.28 = (bf16[192,640]{1,0:T(8,128)(2,1)S(1)}, bf16[192,640]{1,0:T(8,128)(2,1)S(1)}, u32[]{:S(2)}, u32[]{:S(2)}) collective-permute-start(bf16[192,640]{1,0:T(8,128)(2,1)S(1)} %get-tuple-element.123), channel_id=1, source_target_pairs={{0,2},{1,3},{4,0},{5,1},{8,4},{9,5},{12,8},{13,9},{14,12},{15,13},... | collective-permute-start | bytes 737288 | tf_op jit(solution)/shard_map/ppermute | solution.py:253
  180.9 9.1 %collective-permute-start.32 = (bf16[192,640]{1,0:T(8,128)(2,1)S(1)}, bf16[192,640]{1,0:T(8,128)(2,1)S(1)}, u32[]{:S(2)}, u32[]{:S(2)}) collective-permute-start(bf16[192,640]{1,0:T(8,128)(2,1)S(1)} %get-tuple-element.129), channel_id=1, source_target_pairs={{0,4},{1,5},{4,8},{5,9},{8,12},{9,13},{12,14},{13,15},{14,10},{15,... | collective-permute-start | bytes 737288 | tf_op jit(solution)/shard_map/ppermute | solution.py:253
  183.0 7.0 %collective-permute-start.33 = (bf16[192,640]{1,0:T(8,128)(2,1)S(1)}, bf16[192,640]{1,0:T(8,128)(2,1)S(1)}, u32[]{:S(2)}, u32[]{:S(2)}) collective-permute-start(bf16[192,640]{1,0:T(8,128)(2,1)S(1)} %get-tuple-element.130), channel_id=1, source_target_pairs={{0,2},{1,3},{4,0},{5,1},{8,4},{9,5},{12,8},{13,9},{14,12},{15,13},... | collective-permute-start | bytes 737288 | tf_op jit(solution)/shard_map/ppermute | solution.py:253
  190.0 7.4 %collective-permute-start.48 = (bf16[5,240,768]{2,1,0:T(8,128)(2,1)S(1)}, bf16[5,240,768]{2,1,0:T(8,128)(2,1)S(1)}, u32[]{:S(2)}, u32[]{:S(2)}) collective-permute-start(bf16[5,240,768]{2,1,0:T(8,128)(2,1)S(1)} %get-tuple-element.145), channel_id=1, source_target_pairs={{0,1},{1,0},{2,3},{3,2},{4,5},{5,4},{6,7},{7,6},{8,9},{9,8},{10,11... | collective-permute-start | bytes 5529608 | tf_op jit(solution)/shard_map/ppermute | solution.py:253
  190.1 5.6 %collective-permute-start.46 = (bf16[384,128]{1,0:T(8,128)(2,1)S(1)}, bf16[384,128]{1,0:T(8,128)(2,1)S(1)}, u32[]{:S(2)}, u32[]{:S(2)}) collective-permute-start(bf16[384,128]{1,0:T(8,128)(2,1)S(1)} %get-tuple-element.143), channel_id=1, source_target_pairs={{0,4},{1,5},{4,8},{5,9},{8,12},{9,13},{12,14},{13,15},{14,10},{15,... | collective-permute-start | bytes 294920 | tf_op jit(solution)/shard_map/ppermute | solution.py:253
  192.2 5.2 %collective-permute-start.47 = (bf16[384,128]{1,0:T(8,128)(2,1)S(1)}, bf16[384,128]{1,0:T(8,128)(2,1)S(1)}, u32[]{:S(2)}, u32[]{:S(2)}) collective-permute-start(bf16[384,128]{1,0:T(8,128)(2,1)S(1)} %get-tuple-element.144), channel_id=1, source_target_pairs={{0,2},{1,3},{4,0},{5,1},{8,4},{9,5},{12,8},{13,9},{14,12},{15,13},... | collective-permute-start | bytes 294920 | tf_op jit(solution)/shard_map/ppermute | solution.py:253
  197.4 4.2 %collective-permute-start.49 = (bf16[2,240,768]{2,1,0:T(8,128)(2,1)S(1)}, bf16[2,240,768]{2,1,0:T(8,128)(2,1)S(1)}, u32[]{:S(2)}, u32[]{:S(2)}) collective-permute-start(bf16[2,240,768]{2,1,0:T(8,128)(2,1)S(1)} %get-tuple-element.153), channel_id=1, source_target_pairs={{0,1},{1,0},{2,3},{3,2},{4,5},{5,4},{6,7},{7,6},{8,9},{9,8},{10,11... | collective-permute-start | bytes 2211848 | tf_op jit(solution)/shard_map/ppermute | solution.py:253
  199.7 1.9 collective-permute-start.50

commit v5 on v4

--- a/solution.py
+++ b/solution.py
@@ -494,41 +494,35 @@
 
 
 def output_kernel(plan, arrived, facts, att_ref, att2_ref, *refs):
-    out_ref, sent_ref, w_buf, o_buf, in_sem, out_sem, late_sem = refs[-7:]
+    out_ref, sent_ref, o_buf, out_sem, late_sem = refs[-5:]
     rows, columns = o_buf.shape[1:]
     share = columns // 6
+    wide = 2 * share
     group = facts[GROUP]
-    loads = []
-    for p, (slot, parts) in enumerate(plan):
-        copies = []
-        for source, row, first, size in parts:
-            ref = refs[source]
-            if ref.shape[1] == columns:
-                spans = [(0, 0, columns)]
-            elif ref.shape[1] == share:
-                spans = [(0, pl.multiple_of((1 - group) * share, share), share)]
-            else:
-                own = pl.multiple_of(group * share, share)
-                spans = [(0, own, share), (share, 2 * share, columns - 2 * share)]
-            for start, target, width in spans:
-                view = ref.at[pl.ds(row, size), pl.ds(start, width)]
-                goal = w_buf.at[p, pl.ds(first, size), pl.ds(target, width)]
-                copy = pltpu.make_async_copy(view, goal, in_sem.at[p, len(copies)])
-                copy.start()
-                copies.append(copy)
-        loads.append(copies)
     stores = place(facts, [(refs[source], slots) for source, slots in arrived], out_ref, late_sem)
     attended = jnp.concatenate([att_ref[...], att2_ref[...]], axis=0)
-    width = columns // 3
     for p, (slot, parts) in enumerate(plan):
-        for copy in loads[p]:
-            copy.wait()
-        for start in range(0, columns, width):
-            both = jnp.dot(
-                attended, w_buf[p, :, start : start + width], preferred_element_type=jnp.float32
-            ).astype(jnp.bfloat16)
-            o_buf[p, :, start : start + width] = both[:rows]
-            sent_ref[p, :, start : start + width] = both[rows:]
+        own = pl.multiple_of(group * share, share)
+        other = pl.multiple_of((1 - group) * share, share)
+        spans = {
+            columns: [(start, start, wide) for start in range(0, columns, wide)],
+            columns - share: [(0, own, share), (share, wide, wide), (3 * share, 2 * wide, wide)],
+            share: [(0, other, share)],
+        }
+        for width in sorted({refs[part[0]].shape[1] for part in parts}):
+            blocks = [part for part in parts if refs[part[0]].shape[1] == width]
+            for start, target, size in spans[width]:
+                w = jnp.concatenate(
+                    [
+                        refs[source][row : row + depth, start : start + size]
+                        for source, row, first, depth in blocks
+                    ],
+                    axis=0,
+                )
+                both = jnp.dot(attended, w, preferred_element_type=jnp.float32)
+                both = both.astype(jnp.bfloat16)
+                o_buf[p, :, pl.ds(target, size)] = both[:rows]
+                sent_ref[p, :, pl.ds(target, size)] = both[rows:]
         copy = pltpu.make_async_copy(
             o_buf.at[p], out_ref.at[0, :, columns_of(facts, slot, columns)], out_sem.at[p]
         )
@@ -590,6 +584,7 @@
     plan = [
         (slot, [(index_of(block), *where) for block, *where in parts]) for slot, parts in work
     ]
+    held = len(sources)
     arrived = [(index_of(block), slots) for block, slots in arrived]
     placed = sum(len(slots) for _, slots in arrived)
     columns = width // (CHIPS * CORES)
@@ -599,13 +594,11 @@
         grid_spec=pltpu.PrefetchScalarGridSpec(
             num_scalar_prefetch=1,
             grid=(),
-            in_specs=[pl.BlockSpec(memory_space=pltpu.VMEM)] * CORES
-            + [pl.BlockSpec(memory_space=pl.ANY)] * (len(sources) + len(filled)),
+            in_specs=[pl.BlockSpec(memory_space=pltpu.VMEM)] * (CORES + held)
+            + [pl.BlockSpec(memory_space=pl.ANY)] * (len(sources) - held + len(filled)),
             out_specs=[pl.BlockSpec(memory_space=pl.ANY), pl.BlockSpec(memory_space=pltpu.VMEM)],
             scratch_shapes=[
-                pltpu.VMEM((len(plan), depth, columns), jnp.bfloat16),
                 pltpu.VMEM((len(plan), rows, columns), jnp.bfloat16),
-                pltpu.SemaphoreType.DMA((len(plan), 10)),
                 pltpu.SemaphoreType.DMA((len(plan),)),
                 pltpu.SemaphoreType.DMA((max(placed, 1),)),
             ],
@@ -616,7 +609,7 @@
         ],
         input_output_aliases={1 + CORES + len(sources): 0} if filled else {},
         cost_estimate=pl.CostEstimate(flops=1000, bytes_accessed=1000, transcendentals=0),
-        compiler_params=pltpu.CompilerParams(vmem_limit_bytes=(len(plan) * 3 + 6) * 2**20),
+        compiler_params=pltpu.CompilerParams(vmem_limit_bytes=(len(plan) + 8) * 2**20),
         name="project_output",
     )(facts, *attended, *sources, *in_hbm(filled))
 
@@ -688,14 +681,14 @@
     span0, new_kv, cache = project_kv(facts, span_states, recomp_states, keys)
     sa1, sb1 = pair(span0, span0)
     sa2, sb2 = pair(sa1, sb1)
+    ta1, tb1 = together(*pair(top0, top0))
+    sides = lambda *found: (share, [(n, 0, cut) for n in found])
+    la1, lb1, ta1, tb1, queries, sa2, sb2, send1 = together(
+        *pair(low0, low0), ta1, tb1, queries, sa2, sb2, packs=(sides(2, 0, 3, 1),)
+    )
     sa3, sb3 = pair(sa2, sb2)
-    ta1, tb1, queries = together(*pair(top0, top0), queries)
     mine, theirs_part = project_query(
         facts, recomp_states, other_rows, (queries, *swap(queries)), depth
-    )
-    sides = lambda *found: (share, [(n, 0, cut) for n in found])
-    la1, lb1, ta1, tb1, send1 = together(
-        *pair(low0, low0), ta1, tb1, packs=(sides(2, 0, 3, 1),)
     )
     ta2, tb2, la1 = together(*pair(ta1, tb1), la1)
     la2, lb2, x1, ta2, tb2, send2 = together(

time: 203 us -> 202 us (level)
    ppermute x46, waiting for transfers between devices: 110 us -> 112 us  [move(): return lax.ppermute(block, 'serve', pairs)]
    pallas_call x3, Pallas kernels: 12.8 us -> 10.8 us  [project_output(): pl.pallas_call(partial(output_kernel, plan, arrived), grid_spec=pltpu.Pre...]
  transfers between devices with their start and end apart: 51 -> 51, of which waited for: 23 -> 31; matrix products, arithmetic and copies ran while one was open for 0% -> 0% of each run, Pallas kernels for 17% -> 16%
where the time goes in v5:
time: 202 us
  waiting for transfers between devices  116 us (57%)
  starting transfers between devices  48 us (24%)
  Pallas kernels  36 us (18%)
    ppermute x46, waiting for transfers between devices, move(): return lax.ppermute(block, 'serve', pairs)  112 us
    ppermute x46, starting transfers between devices, move(): return lax.ppermute(block, 'serve', pairs)  40.9 us
    pallas_call x3, Pallas kernels, project_output(): pl.pallas_call(partial(output_kernel, plan, arrived), grid_spec=pltpu.Pre...  10.8 us
    ppermute x5, starting transfers between devices, across(): return lax.ppermute(block, 'groups', ACROSS)  7.14 us
    pallas_call x1, Pallas kernels, project_query(): pl.pallas_call(query_kernel, grid_spec=pltpu.PrefetchScalarGridSpec(num_s...  6.21 us
    pallas_call x1, Pallas kernels, attend(): pl.pallas_call(attend_kernel, grid_spec=pltpu.PrefetchScalarGridSpec(num_...  6.2 us
    pallas_call x1, Pallas kernels, project_kv(): pl.pallas_call(kv_kernel, grid_spec=pltpu.PrefetchScalarGridSpec(num_scal...  5.62 us
    ppermute x5, waiting for transfers between devices, across(): return lax.ppermute(block, 'groups', ACROSS)  4.21 us
  transfers between devices with their start and end apart: 51, of which 31 were waited for; matrix products, arithmetic and copies ran while one was open for 0% of the time, Pallas kernels for 16%

profile of v5, /device:TPU:0, one launch (start us, length us, event | category | flops | bytes accessed | tf_op | source)
XLA Modules:
  0.0 202.2 jit_solution(827777405420838991)
XLA Ops:
  1.3 1.3 take_parts.2
  2.6 3.1 %collective-permute-start = (bf16[48,6144]{1,0:T(8,128)(2,1)S(1)}, bf16[48,6144]{1,0:T(8,128)(2,1)S(1)}, u32[]{:S(2)}, u32[]{:S(2)}) collective-permute-start(bf16[48,6144]{1,0:T(8,128)(2,1)S(1)} %get-tuple-element.86.refs_8_), channel_id=1, source_target_pairs={{0,4},{1,5},{4,8},{5,9},{8,12},{9,13},{12,14},{13,15},{14,10},{15,... | collective-permute-start | bytes 1769480 | tf_op jit(solution)/shard_map/ppermute | solution.py:253
  5.7 2.0 collective-permute-start.2
  7.7 2.3 %take_parts.3 = (bf16[240,6144]{1,0:T(8,128)(2,1)S(1)}, bf16[384,640]{1,0:T(8,128)(2,1)S(1)}, bf16[384,640]{1,0:T(8,128)(2,1)S(1)}) custom-call(s32[1]{0:T(128)} %bitcast.group_ref, s32[1]{0:T(128)} %bitcast.1.me_ref.refs_0_, bf16[240,12288]{1,0:T(8,128)(2,1)} %bitcast.11, bf16[768,768]{1,0:T(8,128)(2,1)} %bitcast.16, bf16[32,6144]{1,0:T(8,128)(2,1)} %copy-done.1), custom_call_target="tpu_custom_call" | custom-call | tf_op jit(solution)/shard_map/take_parts/pallas_call | solution.py:237
  10.0 2.0 collective-permute-start.14
  12.0 15.4 %collective-permute-done.2.refs_0_ = bf16[32,6144]{1,0:T(8,128)(2,1)S(1)} collective-permute-done((bf16[32,6144]{1,0:T(8,128)(2,1)S(1)}, bf16[32,6144]{1,0:T(8,128)(2,1)S(1)}, u32[]{:S(2)}, u32[]{:S(2)}) %collective-permute-start.2) | collective-permute-done | bytes 393248 | tf_op jit(solution)/shard_map/ppermute | solution.py:253
  27.4 1.5 collective-permute-done.3.refs_1_
  29.2 1.7 collective-permute-start.4
  31.2 9.7 %collective-permute-done.5.refs_1_ = bf16[32,6144]{1,0:T(8,128)(2,1)S(1)} collective-permute-done((bf16[32,6144]{1,0:T(8,128)(2,1)S(1)}, bf16[32,6144]{1,0:T(8,128)(2,1)S(1)}, u32[]{:S(2)}, u32[]{:S(2)}) %collective-permute-start.5) | collective-permute-done | bytes 393248 | tf_op jit(solution)/shard_map/ppermute | solution.py:253
  40.9 1.6 collective-permute-start.6
  43.0 10.6 %collective-permute-done.7.refs_1_ = bf16[48,6144]{1,0:T(8,128)(2,1)S(1)} collective-permute-done((bf16[48,6144]{1,0:T(8,128)(2,1)S(1)}, bf16[48,6144]{1,0:T(8,128)(2,1)S(1)}, u32[]{:S(2)}, u32[]{:S(2)}) %collective-permute-start.7) | collective-permute-done | bytes 589856 | tf_op jit(solution)/shard_map/ppermute | solution.py:253
  53.6 1.6 collective-permute-start.8
  55.6 6.4 %collective-permute-done.9.refs_1_ = bf16[32,6144]{1,0:T(8,128)(2,1)S(1)} collective-permute-done((bf16[32,6144]{1,0:T(8,128)(2,1)S(1)}, bf16[32,6144]{1,0:T(8,128)(2,1)S(1)}, u32[]{:S(2)}, u32[]{:S(2)}) %collective-permute-start.9) | collective-permute-done | bytes 393248 | tf_op jit(solution)/shard_map/ppermute | solution.py:253
  62.0 0.7 collective-permute-done.8.refs_0_
  62.7 1.6 collective-permute-start.10
  64.3 8.0 %collective-permute-done.11.refs_1_ = bf16[48,6144]{1,0:T(8,128)(2,1)S(1)} collective-permute-done((bf16[48,6144]{1,0:T(8,128)(2,1)S(1)}, bf16[48,6144]{1,0:T(8,128)(2,1)S(1)}, u32[]{:S(2)}, u32[]{:S(2)}) %collective-permute-start.11) | collective-permute-done | bytes 589856 | tf_op jit(solution)/shard_map/ppermute | solution.py:253
  72.3 3.1 %collective-permute-done.10.refs_0_ = bf16[48,6144]{1,0:T(8,128)(2,1)S(1)} collective-permute-done((bf16[48,6144]{1,0:T(8,128)(2,1)S(1)}, bf16[48,6144]{1,0:T(8,128)(2,1)S(1)}, u32[]{:S(2)}, u32[]{:S(2)}) %collective-permute-start.10) | collective-permute-done | bytes 589856 | tf_op jit(solution)/shard_map/ppermute | solution.py:253
  75.4 1.6 collective-permute-start.13
  77.4 7.3 %collective-permute-done.12.refs_7_ = bf16[32,6144]{1,0:T(8,128)(2,1)S(1)} collective-permute-done((bf16[32,6144]{1,0:T(8,128)(2,1)S(1)}, bf16[32,6144]{1,0:T(8,128)(2,1)S(1)}, u32[]{:S(2)}, u32[]{:S(2)}) %collective-permute-start.12) | collective-permute-done | bytes 393248 | tf_op jit(solution)/shard_map/ppermute | solution.py:253
  84.7 1.9 collective-permute-done.13.refs_15_
  87.3 1.6 collective-permute-start.18
  89.4 1.6 collective-permute-start.16
  91.4 1.2 list_facts.1.facts
  93.0 5.6 %project_kv.1 = (bf16[272,256]{1,0:T(8,128)(2,1)S(1)}, bf16[240,256]{1,0:T(8,128)(2,1)S(1)}, bf16[16,16,256]{2,1,0:T(8,128)(2,1)}) custom-call(s32[34]{0:T(128)S(1)} %list_facts.1.facts, bf16[1,256,12288]{2,1,0:T(8,128)(2,1)S(1)} %bitcast.15, bf16[1,240,12288]{2,1,0:T(8,128)(2,1)S(1)} %bitcast.13, bf16[256,6144]{1,0:T(8,128)(2,1)S(1)} %get-tuple-element.107.own_ref, ...), custom_call_target="tpu_custom_call" | custom-call | flops 1000 | bytes 1000 | tf_op jit(solution)/shard_map/project_kv/pallas_call | solution.py:318
  98.6 1.6 collective-permute-start.20
  100.2 1.1 collective-permute-done.18.refs_0_
  101.7 12.7 %collective-permute-done.20.refs_1_ = bf16[272,256]{1,0:T(8,128)(2,1)S(1)} collective-permute-done((bf16[272,256]{1,0:T(8,128)(2,1)S(1)}, bf16[272,256]{1,0:T(8,128)(2,1)S(1)}, u32[]{:S(2)}, u32[]{:S(2)}) %collective-permute-start.20) | collective-permute-done | bytes 139296 | tf_op jit(solution)/shard_map/ppermute | solution.py:253
  114.4 1.6 collective-permute-start.21
  116.5 3.2 %collective-permute-done.21.refs_5_ = bf16[272,256]{1,0:T(8,128)(2,1)S(1)} collective-permute-done((bf16[272,256]{1,0:T(8,128)(2,1)S(1)}, bf16[272,256]{1,0:T(8,128)(2,1)S(1)}, u32[]{:S(2)}, u32[]{:S(2)}) %collective-permute-start.21) | collective-permute-done | bytes 139296 | tf_op jit(solution)/shard_map/ppermute | solution.py:253
  119.7 1.4 collective-permute-done.23.refs_6_
  121.2 1.6 collective-permute-start.41
  123.3 4.0 %collective-permute-done.41.refs_5_ = bf16[272,256]{1,0:T(8,128)(2,1)S(1)} collective-permute-done((bf16[272,256]{1,0:T(8,128)(2,1)S(1)}, bf16[272,256]{1,0:T(8,128)(2,1)S(1)}, u32[]{:S(2)}, u32[]{:S(2)}) %collective-permute-start.41) | collective-permute-done | bytes 139296 | tf_op jit(solution)/shard_map/ppermute | solution.py:253
  127.3 1.6 collective-permute-start.43
  128.9 1.5 collective-permute-start.24
  130.9 3.0 %collective-permute-done.43.refs_7_ = bf16[272,256]{1,0:T(8,128)(2,1)S(1)} collective-permute-done((bf16[272,256]{1,0:T(8,128)(2,1)S(1)}, bf16[272,256]{1,0:T(8,128)(2,1)S(1)}, u32[]{:S(2)}, u32[]{:S(2)}) %collective-permute-start.43) | collective-permute-done | bytes 139296 | tf_op jit(solution)/shard_map/ppermute | solution.py:253
  134.5 8.5 %collective-permute-done.24.refs_0_ = bf16[384,640]{1,0:T(8,128)(2,1)S(1)} collective-permute-done((bf16[384,640]{1,0:T(8,128)(2,1)S(1)}, bf16[384,640]{1,0:T(8,128)(2,1)S(1)}, u32[]{:S(2)}, u32[]{:S(2)}) %collective-permute-start.24) | collective-permute-done | bytes 491552 | tf_op jit(solution)/shard_map/ppermute | solution.py:253
  143.1 1.5 collective-permute-done.25.refs_1_
  145.0 1.5 collective-permute-start.28
  146.5 6.2 %project_query.1 = (f32[240,768]{1,0:T(8,128)S(1)}, bf16[240,768]{1,0:T(8,128)(2,1)S(1)}) custom-call(s32[34]{0:T(128)S(1)} %list_facts.1.facts, bf16[1,240,12288]{2,1,0:T(8,128)(2,1)S(1)} %bitcast.13, bf16[384,6144]{1,0:T(8,128)(2,1)S(1)} %get-tuple-element.135.own_ref, bf16[384,6144]{1,0:T(8,128)(2,1)S(1)} %collective-permute-done.39.sib_ref, ...), custom_call_target="tpu_custom_call" | custom-call | flops 1000 | bytes 1000 | tf_op jit(solution)/shard_map/project_query/pallas_call | solution.py:379
  152.7 0.6 collective-permute-start.40
  153.3 1.7 collective-permute-done.28.refs_2_
  155.0 0.6 collective-permute-done.26.refs_0_
  155.7 1.0 collective-permute-start.29
  156.7 1.1 collective-permute-start.30
  157.7 0.9 collective-permute-start.33
  158.7 1.1 collective-permute-start.34
  159.8 2.3 %collective-permute-done.40.other_ref = bf16[240,768]{1,0:T(8,128)(2,1)S(1)} collective-permute-done((bf16[240,768]{1,0:T(8,128)(2,1)S(1)}, bf16[240,768]{1,0:T(8,128)(2,1)S(1)}, u32[]{:S(2)}, u32[]{:S(2)}) %collective-permute-start.40) | collective-permute-done | bytes 368672 | tf_op jit(solution)/shard_map/ppermute | solution.py:257
  162.1 1.5 collective-permute-start.35
  163.6 6.2 %attend.1.att_ref = bf16[240,768]{1,0:T(8,128)(2,1)S(1)} custom-call(s32[6]{0:T(128)S(1)} %bitcast.18, s32[34]{0:T(128)S(1)} %list_facts.1.facts, f32[240,768]{1,0:T(8,128)S(1)} %get-tuple-element.137.mine_ref, bf16[240,768]{1,0:T(8,128)(2,1)S(1)} %collective-permute-done.40.other_ref, bf16[240,256]{1,0:T(8,128)(2,1)S(1)} %get-tuple-element.139.new_ref, ...), custom_call_target="tpu_custom_call" | custom-call | flops 1000 | bytes 1000 | tf_op jit(solution)/shard_map/attend/pallas_call | solution.py:469
  169.9 0.9 collective-permute-done.30.refs_1_
  171.1 4.9 %collective-permute-done.33.refs_0_ = bf16[384,640]{1,0:T(8,128)(2,1)S(1)} collective-permute-done((bf16[384,640]{1,0:T(8,128)(2,1)S(1)}, bf16[384,640]{1,0:T(8,128)(2,1)S(1)}, u32[]{:S(2)}, u32[]{:S(2)}) %collective-permute-start.33) | collective-permute-done | bytes 491552 | tf_op jit(solution)/shard_map/ppermute | solution.py:253
  176.0 1.6 collective-permute-done.34.refs_1_
  177.8 1.6 collective-permute-start.38
  179.3 1.7 collective-permute-start.31
  181.4 1.7 collective-permute-start.36
  183.4 5.1 %project_output.3 = (bf16[1,240,12288]{2,1,0:T(8,128)(2,1)}, bf16[5,240,768]{2,1,0:T(8,128)(2,1)S(1)}) custom-call(s32[34]{0:T(128)S(1)} %list_facts.1.facts, bf16[240,768]{1,0:T(8,128)(2,1)S(1)} %attend.1.att_ref, bf16[240,768]{1,0:T(8,128)(2,1)S(1)} %collective-permute-done.45.att2_ref, bf16[768,768]{1,0:T(8,128)(2,1)S(1)} %bitcast.17, ...), custom_call_target="tpu_custom_call" | custom-call | flops 1000 | bytes 1000 | tf_op jit(solution)/shard_map/project_output/pallas_call | solution.py:592
  188.5 1.7 collective-permute-done.37.refs_3_
  190.3 0.6 collective-permute-start.46
  190.9 1.5 collective-permute-start.47
  192.4 2.9 %project_output.4 = (bf16[1,240,12288]{2,1,0:T(8,128)(2,1)}, bf16[2,240,768]{2,1,0:T(8,128)(2,1)S(1)}) custom-call(s32[34]{0:T(128)S(1)} %list_facts.1.facts, bf16[240,768]{1,0:T(8,128)(2,1)S(1)} %attend.1.att_ref, bf16[240,768]{1,0:T(8,128)(2,1)S(1)} %collective-permute-done.45.att2_ref, ...), custom_call_target="tpu_custom_call", output_to_operand_aliasing={{0}: (8, {})} | custom-call | flops 1000 | bytes 1000 | tf_op jit(solution)/shard_map/project_output/pallas_call | solution.py:592
  195.9 2.7 %project_output.5 = (bf16[1,240,12288]{2,1,0:T(8,128)(2,1)}, bf16[1,240,768]{2,1,0:T(8,128)(2,1)S(1)}) custom-call(s32[34]{0:T(128)S(1)} %list_facts.1.facts, bf16[240,768]{1,0:T(8,128)(2,1)S(1)} %attend.1.att_ref, bf16[240,768]{1,0:T(8,128)(2,1)S(1)} %collective-permute-done.45.att2_ref, ...), custom_call_target="tpu_custom_call", output_to_operand_aliasing={{0}: (10, {})} | custom-call | flops 1000 | bytes 1000 | tf_op jit(solution)/shard_map/project_output/pallas_call | solution.py:592
  198.6 0.6 collective-permute-start.50
  199.1 1.3 collective-permute-done.50.refs_1_
  200.5 1.6 place_output.1
  (87 shorter events, 8.6 us)
Async XLA Ops:
  2.6 5.1 %copy-start.1 = (bf16[32,6144]{1,0:T(8,128)(2,1)}, bf16[32,6144]{1,0:T(8,128)(2,1)S(1)}, u32[]{:S(2)}) copy-start(bf16[32,6144]{1,0:T(8,128)(2,1)S(1)} %get-tuple-element.85.refs_3_.refs_0_) | copy-start | bytes 1179652
  2.6 26.6 %collective-permute-start = (bf16[48,6144]{1,0:T(8,128)(2,1)S(1)}, bf16[48,6144]{1,0:T(8,128)(2,1)S(1)}, u32[]{:S(2)}, u32[]{:S(2)}) collective-permute-start(bf16[48,6144]{1,0:T(8,128)(2,1)S(1)} %get-tuple-element.86.refs_8_), channel_id=1, source_target_pairs={{0,4},{1,5},{4,8},{5,9},{8,12},{9,13},{12,14},{13,15},{14,10},{15,... | collective-permute-start | bytes 1769480 | tf_op jit(solution)/shard_map/ppermute | solution.py:253
  5.7 23.5 %collective-permute-start.1 = (bf16[48,6144]{1,0:T(8,128)(2,1)S(1)}, bf16[48,6144]{1,0:T(8,128)(2,1)S(1)}, u32[]{:S(2)}, u32[]{:S(2)}) collective-permute-start(bf16[48,6144]{1,0:T(8,128)(2,1)S(1)} %get-tuple-element.86.refs_8_), channel_id=1, source_target_pairs={{0,2},{1,3},{4,0},{5,1},{8,4},{9,5},{12,8},{13,9},{14,12},{15,13},... | collective-permute-start | bytes 1769480 | tf_op jit(solution)/shard_map/ppermute | solution.py:253
  5.7 21.7 %collective-permute-start.2 = (bf16[32,6144]{1,0:T(8,128)(2,1)S(1)}, bf16[32,6144]{1,0:T(8,128)(2,1)S(1)}, u32[]{:S(2)}, u32[]{:S(2)}) collective-permute-start(bf16[32,6144]{1,0:T(8,128)(2,1)S(1)} %get-tuple-element.85.refs_3_.refs_0_), channel_id=1, source_target_pairs={{0,4},{1,5},{4,8},{5,9},{8,12},{9,13},{12,14},{13,15},{14,10},{15,... | collective-permute-start | bytes 1179656 | tf_op jit(solution)/shard_map/ppermute | solution.py:253
  7.7 21.2 %collective-permute-start.3 = (bf16[32,6144]{1,0:T(8,128)(2,1)S(1)}, bf16[32,6144]{1,0:T(8,128)(2,1)S(1)}, u32[]{:S(2)}, u32[]{:S(2)}) collective-permute-start(bf16[32,6144]{1,0:T(8,128)(2,1)S(1)} %get-tuple-element.85.refs_3_.refs_0_), channel_id=1, source_target_pairs={{0,2},{1,3},{4,0},{5,1},{8,4},{9,5},{12,8},{13,9},{14,12},{15,13},... | collective-permute-start | bytes 1179656 | tf_op jit(solution)/shard_map/ppermute | solution.py:253
  7.7 85.2 %slice-start.2 = ((s8[6291456]{0:T(1024)(128)(4,1)}), s8[4194304]{0:T(1024)(128)(4,1)S(1)}, s32[]{:S(2)}) async-start(s8[6291456]{0:T(1024)(128)(4,1)} %bitcast.14), calls=%async_computation.2 | async-start | bytes 8388608
  10.0 74.7 %collective-permute-start.14 = (bf16[240,6144]{1,0:T(8,128)(2,1)S(1)}, bf16[240,6144]{1,0:T(8,128)(2,1)S(1)}, u32[]{:S(2)}, u32[]{:S(2)}) collective-permute-start(bf16[240,6144]{1,0:T(8,128)(2,1)S(1)} %get-tuple-element.105), channel_id=1, source_target_pairs={{0,16},{16,0},{1,17},{17,1},{2,18},{18,2},{3,19},{19,3},{4,20},{20... | collective-permute-start | bytes 8847368 | tf_op jit(solution)/shard_map/ppermute | solution.py:257
  28.9 12.1 %collective-permute-start.5 = (bf16[32,6144]{1,0:T(8,128)(2,1)S(1)}, bf16[32,6144]{1,0:T(8,128)(2,1)S(1)}, u32[]{:S(2)}, u32[]{:S(2)}) collective-permute-start(bf16[32,6144]{1,0:T(8,128)(2,1)S(1)} %get-tuple-element.89.refs_2_), channel_id=1, source_target_pairs={{0,2},{1,3},{4,0},{5,1},{8,4},{9,5},{12,8},{13,9},{14,12},{15,13},... | collective-permute-start | bytes 1179656 | tf_op jit(solution)/shard_map/ppermute | solution.py:253
  29.2 11.8 %collective-permute-start.4 = (bf16[32,6144]{1,0:T(8,128)(2,1)S(1)}, bf16[32,6144]{1,0:T(8,128)(2,1)S(1)}, u32[]{:S(2)}, u32[]{:S(2)}) collective-permute-start(bf16[32,6144]{1,0:T(8,128)(2,1)S(1)} %get-tuple-element.88.refs_1_), channel_id=1, source_target_pairs={{0,4},{1,5},{4,8},{5,9},{8,12},{9,13},{12,14},{13,15},{14,10},{15,... | collective-permute-start | bytes 1179656 | tf_op jit(solution)/shard_map/ppermute | solution.py:253
  30.9 22.7 %collective-permute-start.7 = (bf16[48,6144]{1,0:T(8,128)(2,1)S(1)}, bf16[48,6144]{1,0:T(8,128)(2,1)S(1)}, u32[]{:S(2)}, u32[]{:S(2)}) collective-permute-start(bf16[48,6144]{1,0:T(8,128)(2,1)S(1)} %get-tuple-element.92.refs_10_), channel_id=1, source_target_pairs={{0,2},{1,3},{4,0},{5,1},{8,4},{9,5},{12,8},{13,9},{14,12},{15,13},... | collective-permute-start | bytes 1769480 | tf_op jit(solution)/shard_map/ppermute | solution.py:253
  40.9 45.7 %copy-start.2 = (bf16[32,6144]{1,0:T(8,128)(2,1)S(1)}, bf16[32,6144]{1,0:T(8,128)(2,1)}, u32[]{:S(2)}) copy-start(bf16[32,6144]{1,0:T(8,128)(2,1)} %copy-done.1) | copy-start | bytes 1179652
  40.9 12.6 %collective-permute-start.6 = (bf16[48,6144]{1,0:T(8,128)(2,1)S(1)}, bf16[48,6144]{1,0:T(8,128)(2,1)S(1)}, u32[]{:S(2)}, u32[]{:S(2)}) collective-permute-start(bf16[48,6144]{1,0:T(8,128)(2,1)S(1)} %get-tuple-element.91.refs_9_), channel_id=1, source_target_pairs={{0,4},{1,5},{4,8},{5,9},{8,12},{9,13},{12,14},{13,15},{14,10},{15,... | collective-permute-start | bytes 1769480 | tf_op jit(solution)/shard_map/ppermute | solution.py:253
  42.5 19.5 %collective-permute-start.9 = (bf16[32,6144]{1,0:T(8,128)(2,1)S(1)}, bf16[32,6144]{1,0:T(8,128)(2,1)S(1)}, u32[]{:S(2)}, u32[]{:S(2)}) collective-permute-start(bf16[32,6144]{1,0:T(8,128)(2,1)S(1)} %get-tuple-element.95.refs_4_), channel_id=1, source_target_pairs={{0,2},{1,3},{4,0},{5,1},{8,4},{9,5},{12,8},{13,9},{14,12},{15,13},... | collective-permute-start | bytes 1179656 | tf_op jit(solution)/shard_map/ppermute | solution.py:253
  53.6 9.1 %collective-permute-start.8 = (bf16[32,6144]{1,0:T(8,128)(2,1)S(1)}, bf16[32,6144]{1,0:T(8,128)(2,1)S(1)}, u32[]{:S(2)}, u32[]{:S(2)}) collective-permute-start(bf16[32,6144]{1,0:T(8,128)(2,1)S(1)} %get-tuple-element.94.refs_3_), channel_id=1, source_target_pairs={{0,4},{1,5},{4,8},{5,9},{8,12},{9,13},{12,14},{13,15},{14,10},{15,... | collective-permute-start | bytes 1179656 | tf_op jit(solution)/shard_map/ppermute | solution.py:253
  55.2 17.1 %collective-permute-start.11 = (bf16[48,6144]{1,0:T(8,128)(2,1)S(1)}, bf16[48,6144]{1,0:T(8,128)(2,1)S(1)}, u32[]{:S(2)}, u32[]{:S(2)}) collective-permute-start(bf16[48,6144]{1,0:T(8,128)(2,1)S(1)} %get-tuple-element.98.refs_12_), channel_id=1, source_target_pairs={{0,2},{1,3},{4,0},{5,1},{8,4},{9,5},{12,8},{13,9},{14,12},{15,13},... | collective-permute-start | bytes 1769480 | tf_op jit(solution)/shard_map/ppermute | solution.py:253
  62.7 30.2 %slice-start.3 = ((s8[6291456]{0:T(1024)(128)(4,1)}), s8[2097152]{0:T(1024)(128)(4,1)S(1)}, s32[]{:S(2)}) async-start(s8[6291456]{0:T(1024)(128)(4,1)} %bitcast.14), calls=%async_computation.3 | async-start | bytes 4194304
  62.7 12.6 %collective-permute-start.10 = (bf16[48,6144]{1,0:T(8,128)(2,1)S(1)}, bf16[48,6144]{1,0:T(8,128)(2,1)S(1)}, u32[]{:S(2)}, u32[]{:S(2)}) collective-permute-start(bf16[48,6144]{1,0:T(8,128)(2,1)S(1)} %get-tuple-element.97.refs_11_), channel_id=1, source_target_pairs={{0,4},{1,5},{4,8},{5,9},{8,12},{9,13},{12,14},{13,15},{14,10},{15,... | collective-permute-start | bytes 1769480 | tf_op jit(solution)/shard_map/ppermute | solution.py:253
  75.4 11.3 %collective-permute-start.13 = (bf16[48,6144]{1,0:T(8,128)(2,1)S(1)}, bf16[48,6144]{1,0:T(8,128)(2,1)S(1)}, u32[]{:S(2)}, u32[]{:S(2)}) collective-permute-start(bf16[48,6144]{1,0:T(8,128)(2,1)S(1)} %get-tuple-element.103.refs_13_), channel_id=1, source_target_pairs={{0,4},{1,5},{4,8},{5,9},{8,12},{9,13},{12,14},{13,15},{14,10},{15,... | collective-permute-start | bytes 1769480 | tf_op jit(solution)/shard_map/ppermute | solution.py:253
  76.9 7.8 %collective-permute-start.12 = (bf16[32,6144]{1,0:T(8,128)(2,1)S(1)}, bf16[32,6144]{1,0:T(8,128)(2,1)S(1)}, u32[]{:S(2)}, u32[]{:S(2)}) collective-permute-start(bf16[32,6144]{1,0:T(8,128)(2,1)S(1)} %get-tuple-element.102.refs_6_), channel_id=1, source_target_pairs={{0,2},{1,3},{4,0},{5,1},{8,4},{9,5},{12,8},{13,9},{14,12},{15,13},... | collective-permute-start | bytes 1179656 | tf_op jit(solution)/shard_map/ppermute | solution.py:253
  86.6 6.3 %slice-start = ((s8[5898240]{0:T(1024)(128)(4,1)}), s8[4194304]{0:T(1024)(128)(4,1)S(1)}, s32[]{:S(2)}) async-start(s8[5898240]{0:T(1024)(128)(4,1)} %bitcast.12), calls=%async_computation | async-start | bytes 8388608
  86.6 4.7 %copy-start.4 = (s32[256]{0:T(256)S(1)}, s32[256]{0:T(256)}, u32[]{:S(2)}) copy-start(s32[256]{0:T(256)} %constant.11.clone.slot_ref) | copy-start | bytes 3076
  86.6 4.7 %copy-start.6 = (s32[16]{0:T(128)S(1)}, s32[16]{0:T(128)}, u32[]{:S(2)}) copy-start(s32[16]{0:T(128)} %table_ref.1) | copy-start | bytes 196
  86.7 6.3 %slice-start.1 = ((s8[5898240]{0:T(1024)(128)(4,1)}), s8[1703936]{0:T(1024)(128)(4,1)S(1)}, s32[]{:S(2)}) async-start(s8[5898240]{0:T(1024)(128)(4,1)} %bitcast.12), calls=%async_computation.1 | async-start | bytes 3407872
  87.2 5.7 %collective-permute-start.15 = (bf16[256,6144]{1,0:T(8,128)(2,1)S(1)}, bf16[256,6144]{1,0:T(8,128)(2,1)S(1)}, u32[]{:S(2)}, u32[]{:S(2)}) collective-permute-start(bf16[256,6144]{1,0:T(8,128)(2,1)S(1)} %get-tuple-element.107.own_ref), channel_id=1, source_target_pairs={{0,1},{1,0},{2,3},{3,2},{4,5},{5,4},{6,7},{7,6},{8,9},{9,8},{10,11... | collective-permute-start | bytes 9437192 | tf_op jit(solution)/shard_map/ppermute | solution.py:253
  87.3 14.1 %collective-permute-start.18 = (bf16[384,640]{1,0:T(8,128)(2,1)S(1)}, bf16[384,640]{1,0:T(8,128)(2,1)S(1)}, u32[]{:S(2)}, u32[]{:S(2)}) collective-permute-start(bf16[384,640]{1,0:T(8,128)(2,1)S(1)} %get-tuple-element.110), channel_id=1, source_target_pairs={{0,4},{1,5},{4,8},{5,9},{8,12},{9,13},{12,14},{13,15},{14,10},{15,... | collective-permute-start | bytes 1474568 | tf_op jit(solution)/shard_map/ppermute | solution.py:253
  88.9 27.5 %collective-permute-start.19 = (bf16[384,640]{1,0:T(8,128)(2,1)S(1)}, bf16[384,640]{1,0:T(8,128)(2,1)S(1)}, u32[]{:S(2)}, u32[]{:S(2)}) collective-permute-start(bf16[384,640]{1,0:T(8,128)(2,1)S(1)} %get-tuple-element.110), channel_id=1, source_target_pairs={{0,2},{1,3},{4,0},{5,1},{8,4},{9,5},{12,8},{13,9},{14,12},{15,13},... | collective-permute-start | bytes 1474568 | tf_op jit(solution)/shard_map/ppermute | solution.py:253
  89.4 27.1 %collective-permute-start.16 = (bf16[384,640]{1,0:T(8,128)(2,1)S(1)}, bf16[384,640]{1,0:T(8,128)(2,1)S(1)}, u32[]{:S(2)}, u32[]{:S(2)}) collective-permute-start(bf16[384,640]{1,0:T(8,128)(2,1)S(1)} %get-tuple-element.109), channel_id=1, source_target_pairs={{0,4},{1,5},{4,8},{5,9},{8,12},{9,13},{12,14},{13,15},{14,10},{15,... | collective-permute-start | bytes 1474568 | tf_op jit(solution)/shard_map/ppermute | solution.py:253
  90.9 25.5 %collective-permute-start.17 = (bf16[384,640]{1,0:T(8,128)(2,1)S(1)}, bf16[384,640]{1,0:T(8,128)(2,1)S(1)}, u32[]{:S(2)}, u32[]{:S(2)}) collective-permute-start(bf16[384,640]{1,0:T(8,128)(2,1)S(1)} %get-tuple-element.109), channel_id=1, source_target_pairs={{0,2},{1,3},{4,0},{5,1},{8,4},{9,5},{12,8},{13,9},{14,12},{15,13},... | collective-permute-start | bytes 1474568 | tf_op jit(solution)/shard_map/ppermute | solution.py:253
  98.6 15.8 %collective-permute-start.20 = (bf16[272,256]{1,0:T(8,128)(2,1)S(1)}, bf16[272,256]{1,0:T(8,128)(2,1)S(1)}, u32[]{:S(2)}, u32[]{:S(2)}) collective-permute-start(bf16[272,256]{1,0:T(8,128)(2,1)S(1)} %get-tuple-element.114.refs_0_), channel_id=1, source_target_pairs={{0,4},{1,5},{4,8},{5,9},{8,12},{9,13},{12,14},{13,15},{14,10},{15,... | collective-permute-start | bytes 417800 | tf_op jit(solution)/shard_map/ppermute | solution.py:253
  101.4 14.6 %collective-permute-start.22 = (bf16[272,256]{1,0:T(8,128)(2,1)S(1)}, bf16[272,256]{1,0:T(8,128)(2,1)S(1)}, u32[]{:S(2)}, u32[]{:S(2)}) collective-permute-start(bf16[272,256]{1,0:T(8,128)(2,1)S(1)} %get-tuple-element.114.refs_0_), channel_id=1, source_target_pairs={{0,2},{1,3},{4,0},{5,1},{8,4},{9,5},{12,8},{13,9},{14,12},{15,13},... | collective-permute-start | bytes 417800 | tf_op jit(solution)/shard_map/ppermute | solution.py:253
  114.4 5.2 %collective-permute-start.21 = (bf16[272,256]{1,0:T(8,128)(2,1)S(1)}, bf16[272,256]{1,0:T(8,128)(2,1)S(1)}, u32[]{:S(2)}, u32[]{:S(2)}) collective-permute-start(bf16[272,256]{1,0:T(8,128)(2,1)S(1)} %collective-permute-done.20.refs_1_), channel_id=1, source_target_pairs={{0,4},{1,5},{4,8},{5,9},{8,12},{9,13},{12,14},{13,15},{14,10},{15,... | collective-permute-start | bytes 417800 | tf_op jit(solution)/shard_map/ppermute | solution.py:253
  116.0 5.1 %collective-permute-start.23 = (bf16[272,256]{1,0:T(8,128)(2,1)S(1)}, bf16[272,256]{1,0:T(8,128)(2,1)S(1)}, u32[]{:S(2)}, u32[]{:S(2)}) collective-permute-start(bf16[272,256]{1,0:T(8,128)(2,1)S(1)} %collective-permute-done.22.refs_2_), channel_id=1, source_target_pairs={{0,2},{1,3},{4,0},{5,1},{8,4},{9,5},{12,8},{13,9},{14,12},{15,13},... | collective-permute-start | bytes 417800 | tf_op jit(solution)/shard_map/ppermute | solution.py:253
  121.1 25.4 %collective-permute-start.39 = (bf16[384,6144]{1,0:T(8,128)(2,1)S(1)}, bf16[384,6144]{1,0:T(8,128)(2,1)S(1)}, u32[]{:S(2)}, u32[]{:S(2)}) collective-permute-start(bf16[384,6144]{1,0:T(8,128)(2,1)S(1)} %get-tuple-element.135.own_ref), channel_id=1, source_target_pairs={{0,1},{1,0},{2,3},{3,2},{4,5},{5,4},{6,7},{7,6},{8,9},{9,8},{10,11... | collective-permute-start | bytes 14155784 | tf_op jit(solution)/shard_map/ppermute | solution.py:253
  121.2 6.1 %collective-permute-start.41 = (bf16[272,256]{1,0:T(8,128)(2,1)S(1)}, bf16[272,256]{1,0:T(8,128)(2,1)S(1)}, u32[]{:S(2)}, u32[]{:S(2)}) collective-permute-start(bf16[272,256]{1,0:T(8,128)(2,1)S(1)} %get-tuple-element.140.refs_3_), channel_id=1, source_target_pairs={{0,4},{1,5},{4,8},{5,9},{8,12},{9,13},{12,14},{13,15},{14,10},{15,... | collective-permute-start | bytes 417800 | tf_op jit(solution)/shard_map/ppermute | solution.py:253
  122.8 8.1 %collective-permute-start.42 = (bf16[272,256]{1,0:T(8,128)(2,1)S(1)}, bf16[272,256]{1,0:T(8,128)(2,1)S(1)}, u32[]{:S(2)}, u32[]{:S(2)}) collective-permute-start(bf16[272,256]{1,0:T(8,128)(2,1)S(1)} %get-tuple-element.141.refs_4_), channel_id=1, source_target_pairs={{0,2},{1,3},{4,0},{5,1},{8,4},{9,5},{12,8},{13,9},{14,12},{15,13},... | collective-permute-start | bytes 417800 | tf_op jit(solution)/shard_map/ppermute | solution.py:253
  127.3 6.6 %collective-permute-start.43 = (bf16[272,256]{1,0:T(8,128)(2,1)S(1)}, bf16[272,256]{1,0:T(8,128)(2,1)S(1)}, u32[]{:S(2)}, u32[]{:S(2)}) collective-permute-start(bf16[272,256]{1,0:T(8,128)(2,1)S(1)} %collective-permute-done.41.refs_5_), channel_id=1, source_target_pairs={{0,4},{1,5},{4,8},{5,9},{8,12},{9,13},{12,14},{13,15},{14,10},{15,... | collective-permute-start | bytes 417800 | tf_op jit(solution)/shard_map/ppermute | solution.py:253
  128.9 14.2 %collective-permute-start.24 = (bf16[384,640]{1,0:T(8,128)(2,1)S(1)}, bf16[384,640]{1,0:T(8,128)(2,1)S(1)}, u32[]{:S(2)}, u32[]{:S(2)}) collective-permute-start(bf16[384,640]{1,0:T(8,128)(2,1)S(1)} %get-tuple-element.115.refs_1_), channel_id=1, source_target_pairs={{0,4},{1,5},{4,8},{5,9},{8,12},{9,13},{12,14},{13,15},{14,10},{15,... | collective-permute-start | bytes 1474568 | tf_op jit(solution)/shard_map/ppermute | solution.py:253
  130.4 14.2 %collective-permute-start.25 = (bf16[384,640]{1,0:T(8,128)(2,1)S(1)}, bf16[384,640]{1,0:T(8,128)(2,1)S(1)}, u32[]{:S(2)}, u32[]{:S(2)}) collective-permute-start(bf16[384,640]{1,0:T(8,128)(2,1)S(1)} %get-tuple-element.116.refs_4_), channel_id=1, source_target_pairs={{0,2},{1,3},{4,0},{5,1},{8,4},{9,5},{12,8},{13,9},{14,12},{15,13},... | collective-permute-start | bytes 1474568 | tf_op jit(solution)/shard_map/ppermute | solution.py:253
  134.0 24.7 %collective-permute-start.44 = (bf16[2176,256]{1,0:T(8,128)(2,1)S(1)}, bf16[2176,256]{1,0:T(8,128)(2,1)S(1)}, u32[]{:S(2)}, u32[]{:S(2)}) collective-permute-start(bf16[2176,256]{1,0:T(8,128)(2,1)S(1)} %get-tuple-element.142.refs_0_), channel_id=1, source_target_pairs={{0,1},{1,0},{2,3},{3,2},{4,5},{5,4},{6,7},{7,6},{8,9},{9,8},{10,11... | collective-permute-start | bytes 3342344 | tf_op jit(solution)/shard_map/ppermute | solution.py:253
  134.0 21.0 %collective-permute-start.27 = (bf16[384,640]{1,0:T(8,128)(2,1)S(1)}, bf16[384,640]{1,0:T(8,128)(2,1)S(1)}, u32[]{:S(2)}, u32[]{:S(2)}) collective-permute-start(bf16[384,640]{1,0:T(8,128)(2,1)S(1)} %get-tuple-element.119.refs_5_), channel_id=1, source_target_pairs={{0,2},{1,3},{4,0},{5,1},{8,4},{9,5},{12,8},{13,9},{14,12},{15,13},... | collective-permute-start | bytes 1474568 | tf_op jit(solution)/shard_map/ppermute | solution.py:253
  144.5 11.0 %collective-permute-start.26 = (bf16[384,640]{1,0:T(8,128)(2,1)S(1)}, bf16[384,640]{1,0:T(8,128)(2,1)S(1)}, u32[]{:S(2)}, u32[]{:S(2)}) collective-permute-start(bf16[384,640]{1,0:T(8,128)(2,1)S(1)} %get-tuple-element.118.refs_2_), channel_id=1, source_target_pairs={{0,4},{1,5},{4,8},{5,9},{8,12},{9,13},{12,14},{13,15},{14,10},{15,... | collective-permute-start | bytes 1474568 | tf_op jit(solution)/shard_map/ppermute | solution.py:253
  145.0 10.0 %collective-permute-start.28 = (bf16[1536,128]{1,0:T(8,128)(2,1)S(1)}, bf16[1536,128]{1,0:T(8,128)(2,1)S(1)}, u32[]{:S(2)}, u32[]{:S(2)}) collective-permute-start(bf16[1536,128]{1,0:T(8,128)(2,1)S(1)} %get-tuple-element.120), channel_id=1, source_target_pairs={{0,16},{16,0},{1,17},{17,1},{2,18},{18,2},{3,19},{19,3},{4,20},{20... | collective-permute-start | bytes 1179656 | tf_op jit(solution)/shard_map/ppermute | solution.py:257
  146.5 17.0 %copy-start.3 = (s32[1,240]{1,0:T(1,128)S(1)}, s32[1,240]{1,0:T(1,128)}, u32[]{:S(2)}) copy-start(s32[1,240]{1,0:T(1,128)} %row_ref.1) | copy-start | bytes 2884
  146.5 17.0 %copy-start.5 = (s32[1,6]{1,0:T(1,128)S(1)}, s32[1,6]{1,0:T(1,128)}, u32[]{:S(2)}) copy-start(s32[1,6]{1,0:T(1,128)} %param.15) | copy-start | bytes 76
  152.7 9.3 %collective-permute-start.40 = (bf16[240,768]{1,0:T(8,128)(2,1)S(1)}, bf16[240,768]{1,0:T(8,128)(2,1)S(1)}, u32[]{:S(2)}, u32[]{:S(2)}) collective-permute-start(bf16[240,768]{1,0:T(8,128)(2,1)S(1)} %get-tuple-element.138), channel_id=1, source_target_pairs={{0,16},{16,0},{1,17},{17,1},{2,18},{18,2},{3,19},{19,3},{4,20},{20... | collective-permute-start | bytes 1105928 | tf_op jit(solution)/shard_map/ppermute | solution.py:257
  155.7 14.2 %collective-permute-start.29 = (bf16[384,640]{1,0:T(8,128)(2,1)S(1)}, bf16[384,640]{1,0:T(8,128)(2,1)S(1)}, u32[]{:S(2)}, u32[]{:S(2)}) collective-permute-start(bf16[384,640]{1,0:T(8,128)(2,1)S(1)} %get-tuple-element.123.refs_6_), channel_id=1, source_target_pairs={{0,4},{1,5},{4,8},{5,9},{8,12},{9,13},{12,14},{13,15},{14,10},{15,... | collective-permute-start | bytes 1474568 | tf_op jit(solution)/shard_map/ppermute | solution.py:253
  156.7 14.2 %collective-permute-start.30 = (bf16[384,640]{1,0:T(8,128)(2,1)S(1)}, bf16[384,640]{1,0:T(8,128)(2,1)S(1)}, u32[]{:S(2)}, u32[]{:S(2)}) collective-permute-start(bf16[384,640]{1,0:T(8,128)(2,1)S(1)} %get-tuple-element.124.refs_9_), channel_id=1, source_target_pairs={{0,2},{1,3},{4,0},{5,1},{8,4},{9,5},{12,8},{13,9},{14,12},{15,13},... | collective-permute-start | bytes 1474568 | tf_op jit(solution)/shard_map/ppermute | solution.py:253
  157.7 18.3 %collective-permute-start.33 = (bf16[384,640]{1,0:T(8,128)(2,1)S(1)}, bf16[384,640]{1,0:T(8,128)(2,1)S(1)}, u32[]{:S(2)}, u32[]{:S(2)}) collective-permute-start(bf16[384,640]{1,0:T(8,128)(2,1)S(1)} %get-tuple-element.127.refs_7_), channel_id=1, source_target_pairs={{0,4},{1,5},{4,8},{5,9},{8,12},{9,13},{12,14},{13,15},{14,10},{15,... | collective-permute-start | bytes 1474568 | tf_op jit(solution)/shard_map/ppermute | solution.py:253
  158.7 19.0 %collective-permute-start.34 = (bf16[384,640]{1,0:T(8,128)(2,1)S(1)}, bf16[384,640]{1,0:T(8,128)(2,1)S(1)}, u32[]{:S(2)}, u32[]{:S(2)}) collective-permute-start(bf16[384,640]{1,0:T(8,128)(2,1)S(1)} %get-tuple-element.128.refs_10_), channel_id=1, source_target_pairs={{0,2},{1,3},{4,0},{5,1},{8,4},{9,5},{12,8},{13,9},{14,12},{15,13},... | collective-permute-start | bytes 1474568 | tf_op jit(solution)/shard_map/ppermute | solution.py:253
  162.1 9.1 %collective-permute-start.35 = (bf16[1536,128]{1,0:T(8,128)(2,1)S(1)}, bf16[1536,128]{1,0:T(8,128)(2,1)S(1)}, u32[]{:S(2)}, u32[]{:S(2)}) collective-permute-start(bf16[1536,128]{1,0:T(8,128)(2,1)S(1)} %get-tuple-element.131), channel_id=1, source_target_pairs={{0,16},{16,0},{1,17},{17,1},{2,18},{18,2},{3,19},{19,3},{4,20},{20... | collective-permute-start | bytes 1179656 | tf_op jit(solution)/shard_map/ppermute | solution.py:257
  163.5 19.8 %copy-start = (bf16[6,128,1,768]{3,1,2,0:T(8,128)(2,1)S(1)}, bf16[6,128,1,768]{3,1,2,0:T(8,128)(2,1)}, u32[]{:S(2)}) copy-start(bf16[6,128,1,768]{3,1,2,0:T(8,128)(2,1)} %param.14) | copy-start | bytes 3538948
  169.9 13.2 %collective-permute-start.45 = (bf16[240,768]{1,0:T(8,128)(2,1)S(1)}, bf16[240,768]{1,0:T(8,128)(2,1)S(1)}, u32[]{:S(2)}, u32[]{:S(2)}) collective-permute-start(bf16[240,768]{1,0:T(8,128)(2,1)S(1)} %attend.1.att_ref), channel_id=1, source_target_pairs={{0,1},{1,0},{2,3},{3,2},{4,5},{5,4},{6,7},{7,6},{8,9},{9,8},{10,11... | collective-permute-start | bytes 1105928 | tf_op jit(solution)/shard_map/ppermute | solution.py:253
  177.8 12.5 %collective-permute-start.38 = (bf16[1536,128]{1,0:T(8,128)(2,1)S(1)}, bf16[1536,128]{1,0:T(8,128)(2,1)S(1)}, u32[]{:S(2)}, u32[]{:S(2)}) collective-permute-start(bf16[1536,128]{1,0:T(8,128)(2,1)S(1)} %get-tuple-element.134), channel_id=1, source_target_pairs={{0,16},{16,0},{1,17},{17,1},{2,18},{18,2},{3,19},{19,3},{4,20},{20... | collective-permute-start | bytes 1179656 | tf_op jit(solution)/shard_map/ppermute | solution.py:257
  179.3 9.2 %collective-permute-start.31 = (bf16[192,640]{1,0:T(8,128)(2,1)S(1)}, bf16[192,640]{1,0:T(8,128)(2,1)S(1)}, u32[]{:S(2)}, u32[]{:S(2)}) collective-permute-start(bf16[192,640]{1,0:T(8,128)(2,1)S(1)} %get-tuple-element.125), channel_id=1, source_target_pairs={{0,4},{1,5},{4,8},{5,9},{8,12},{9,13},{12,14},{13,15},{14,10},{15,... | collective-permute-start | bytes 737288 | tf_op jit(solution)/shard_map/ppermute | solution.py:253
  181.1 7.4 %collective-permute-start.32 = (bf16[192,640]{1,0:T(8,128)(2,1)S(1)}, bf16[192,640]{1,0:T(8,128)(2,1)S(1)}, u32[]{:S(2)}, u32[]{:S(2)}) collective-permute-start(bf16[192,640]{1,0:T(8,128)(2,1)S(1)} %get-tuple-element.126), channel_id=1, source_target_pairs={{0,2},{1,3},{4,0},{5,1},{8,4},{9,5},{12,8},{13,9},{14,12},{15,13},... | collective-permute-start | bytes 737288 | tf_op jit(solution)/shard_map/ppermute | solution.py:253
  181.4 7.2 %collective-permute-start.36 = (bf16[192,640]{1,0:T(8,128)(2,1)S(1)}, bf16[192,640]{1,0:T(8,128)(2,1)S(1)}, u32[]{:S(2)}, u32[]{:S(2)}) collective-permute-start(bf16[192,640]{1,0:T(8,128)(2,1)S(1)} %get-tuple-element.132), channel_id=1, source_target_pairs={{0,4},{1,5},{4,8},{5,9},{8,12},{9,13},{12,14},{13,15},{14,10},{15,... | collective-permute-start | bytes 737288 | tf_op jit(solution)/shard_map/ppermute | solution.py:253
  183.1 7.2 %collective-permute-start.37 = (bf16[192,640]{1,0:T(8,128)(2,1)S(1)}, bf16[192,640]{1,0:T(8,128)(2,1)S(1)}, u32[]{:S(2)}, u32[]{:S(2)}) collective-permute-start(bf16[192,640]{1,0:T(8,128)(2,1)S(1)} %get-tuple-element.133), channel_id=1, source_target_pairs={{0,2},{1,3},{4,0},{5,1},{8,4},{9,5},{12,8},{13,9},{14,12},{15,13},... | collective-permute-start | bytes 737288 | tf_op jit(solution)/shard_map/ppermute | solution.py:253
  190.3 5.6 %collective-permute-start.48 = (bf16[5,240,768]{2,1,0:T(8,128)(2,1)S(1)}, bf16[5,240,768]{2,1,0:T(8,128)(2,1)S(1)}, u32[]{:S(2)}, u32[]{:S(2)}) collective-permute-start(bf16[5,240,768]{2,1,0:T(8,128)(2,1)S(1)} %get-tuple-element.149), channel_id=1, source_target_pairs={{0,1},{1,0},{2,3},{3,2},{4,5},{5,4},{6,7},{7,6},{8,9},{9,8},{10,11... | collective-permute-start | bytes 5529608 | tf_op jit(solution)/shard_map/ppermute | solution.py:253
  190.3 5.3 %collective-permute-start.46 = (bf16[384,128]{1,0:T(8,128)(2,1)S(1)}, bf16[384,128]{1,0:T(8,128)(2,1)S(1)}, u32[]{:S(2)}, u32[]{:S(2)}) collective-permute-start(bf16[384,128]{1,0:T(8,128)(2,1)S(1)} %get-tuple-element.147), channel_id=1, source_target_pairs={{0,4},{1,5},{4,8},{5,9},{8,12},{9,13},{12,14},{13,15},{14,10},{15,... | collective-permute-start | bytes 294920 | tf_op jit(solution)/shard_map/ppermute | solution.py:253
  190.9 4.9 %collective-permute-start.47 = (bf16[384,128]{1,0:T(8,128)(2,1)S(1)}, bf16[384,128]{1,0:T(8,128)(2,1)S(1)}, u32[]{:S(2)}, u32[]{:S(2)}) collective-permute-start(bf16[384,128]{1,0:T(8,128)(2,1)S(1)} %get-tuple-element.148), channel_id=1, source_target_pairs={{0,2},{1,3},{4,0},{5,1},{8,4},{9,5},{12,8},{13,9},{14,12},{15,13},... | collective-permute-start | bytes 294920 | tf_op jit(solution)/shard_map/ppermute | solution.py:253
  195.9 4.6 %collective-permute-start.49 = (bf16[2,240,768]{2,1,0:T(8,128)(2,1)S(1)}, bf16[2,240,768]{2,1,0:T(8,128)(2,1)S(1)}, u32[]{:S(2)}, u32[]{:S(2)}) collective-permute-start(bf16[2,240,768]{2,1,0:T(8,128)(2,1)S(1)} %get-tuple-element.157), channel_id=1, source_target_pairs={{0,1},{1,0},{2,3},{3,2},{4,5},{5,4},{6,7},{7,6},{8,9},{9,8},{10,11... | collective-permute-start | bytes 2211848 | tf_op jit(solution)/shard_map/ppermute | solution.py:253
  198.6 1.9 collective-permute-start.50
